TPU v7x, 128 devices: a whole 4x4x4 slice. The times are simulated.
128 devices in a mesh: dp: 8 (over y_lo, z), tp: 16 (over x, y_hi, core).
Axes of the slice: x: 4, y: 4 (y_hi: 2, y_lo: 2; y = y_hi * 2 + y_lo), z: 4, core: 2. Of those that a mesh axis runs over, the one named last changes fastest.
Arguments:
- queries: bfloat16 [4096, 128, 576], P(('dp', 'tp')), may hold values from -16 to 16
- new_latent: bfloat16 [4096, 576], P(('dp', 'tp')), may hold values from -6 to 6
- latent_cache: bfloat16 [4096, 384, 576], P(('dp', 'tp')), may hold values from -6 to 6
- lengths: int32 [4096], P(('dp', 'tp')), may hold values from 1 to 384, 524288 in all
- residual: bfloat16 [4096, 7168], P(('dp', 'tp')), may hold values from -1.1953125 to 1.1953125
- value_up: bfloat16 [128, 512, 128], P('tp'), may hold values from -0.25 to 0.25
- out_proj: bfloat16 [16384, 7168], P('tp'), may hold values from -0.046875 to 0.046875
- norm_gain: bfloat16 [7168], replicated, may hold values from 0.5 to 1.5
Outputs:
- hidden: bfloat16 [4096, 7168], P(('dp', 'tp'))
- normed: bfloat16 [4096, 7168], P(('dp', 'tp'))
Inputs may be any that keep to these rules, and one draw needn't show every extreme that they name: `lengths`: slots at or past a request's length hold stale entries that are not read.
All inputs are finite; a program needn't handle non-finite values. No bound on the sum of `lengths` on one device may be relied on, other than what follows from the above.
Results may differ from a plain program's by a relative error of at most 0.02.
Values may be sent and summed in bfloat16 or wider, within the bound.
No kernel may reach another device: no remote copies, remote signals or barrier semaphores. Data moves between devices by JAX's collectives and lax.ppermute only.
A program may use at most 192 MiB of HBM per device.

v0:
```python
import jax
import jax.numpy as jnp
from jax import lax
from jax.sharding import PartitionSpec as P

softmax_scale = 0.1353
masked_score = -1e30
epsilon = 1e-06


def attend_rows(queries, key_rows, lengths, new_key, latent):
    scores = (
        jnp.einsum("bhc,blc->bhl", queries, key_rows, preferred_element_type=jnp.float32)
        * softmax_scale
    )
    positions = lax.broadcasted_iota(jnp.int32, (1, 1, key_rows.shape[1]), 2)
    visible = positions < lengths[:, None, None]
    masked = jnp.where(visible, scores, masked_score)
    new_score = (
        jnp.einsum("bhc,bc->bh", queries, new_key, preferred_element_type=jnp.float32)
        * softmax_scale
    )
    maxima = jnp.maximum(jnp.max(masked, axis=2), new_score)
    probs = jnp.where(visible, jnp.exp(masked - maxima[:, :, None]), 0.0)
    new_prob = jnp.exp(new_score - maxima)
    totals = jnp.sum(probs, axis=2) + new_prob
    summed = jnp.einsum(
        "bhl,bld->bhd",
        probs.astype(jnp.bfloat16),
        key_rows[:, :, :latent],
        preferred_element_type=jnp.float32,
    )
    new_low = lax.optimization_barrier(new_prob.astype(jnp.bfloat16)).astype(jnp.float32)
    summed = summed + new_low[:, :, None] * new_key[:, None, :latent].astype(jnp.float32)
    return (summed / totals[:, :, None]).astype(jnp.bfloat16)


def per_device(queries, new_latent, latent_cache, lengths, residual, value_up, out_proj, norm_gain):
    latent = value_up.shape[1]
    attended = attend_rows(queries, latent_cache, lengths, new_latent, latent)
    by_heads = lax.all_to_all(attended, "tp", split_axis=1, concat_axis=0, tiled=True)
    head_values = jnp.einsum(
        "bhk,hkd->bhd", by_heads, value_up, preferred_element_type=jnp.float32
    ).astype(jnp.bfloat16)
    flattened = head_values.reshape(head_values.shape[0], -1)
    projected = lax.psum_scatter(
        jnp.dot(flattened, out_proj, preferred_element_type=jnp.float32).astype(jnp.bfloat16),
        "tp",
        scatter_dimension=0,
        tiled=True,
    ).astype(jnp.float32)
    hidden = (residual.astype(jnp.float32) + projected).astype(jnp.bfloat16)
    widened = lax.optimization_barrier(hidden).astype(jnp.float32)
    mean_square = jnp.mean(widened * widened, axis=1, keepdims=True)
    normed = (widened * lax.rsqrt(mean_square + epsilon) * norm_gain.astype(jnp.float32)).astype(
        jnp.bfloat16
    )
    return (hidden, normed)


def solution(mesh):
    return jax.shard_map(
        per_device,
        mesh=mesh,
        in_specs=(
            P(("dp", "tp"), None, None),
            P(("dp", "tp"), None),
            P(("dp", "tp"), None, None),
            P(("dp", "tp")),
            P(("dp", "tp"), None),
            P("tp", None, None),
            P("tp", None),
            P(),
        ),
        out_specs=(P(("dp", "tp"), None), P(("dp", "tp"), None)),
        check_vma=False,
    )
```

profile of v0, /device:TPU:72, one launch (start us, length us, event | category | flops | bytes accessed | tf_op | source)
XLA Modules:
  0.0 209.1 jit_solution(14477213226340277814)
XLA Ops:
  7.2 0.0 copy-start
  7.2 0.0 reduce-scatter.2.cloned.1.call-start
  7.2 0.8 iota_compare_fusion
  8.0 0.8 slice_convert_fusion
  8.8 3.1 %fusion.18 = f32[32,1,128]{2,1,0:T(1,128)S(1)} fusion(bf16[32,128,576]{1,2,0:T(8,128)(2,1)} %param.8, bf16[32,576,1]{1,0,2:T(8,128)(2,1)} %bitcast.22), kind=kOutput, calls=%fused_computation.21 | convolution fusion | flops 4718592 | bytes 4771840 | tf_op jit(solution)/shard_map/bhc,bc->bh/dot_general | solution.py:20
  11.9 10.4 %fusion.2 = (f32[32,128]{1,0:T(8,128)S(1)}, f32[32,128,384]{2,1,0:T(8,128)S(1)}) fusion(pred[32,384]{1,0:T(8,128)(4,1)S(1)} %iota_compare_fusion, bf16[32,128,576]{1,2,0:T(8,128)(2,1)} %param.8, bf16[32,384,576]{1,2,0:T(8,128)(2,1)} %param.10), kind=kOutput, calls=%fused_computation.6 | convolution fusion | flops 1816653824 | bytes 25194496 | tf_op jit(solution)/shard_map/bhc,blc->bhl/dot_general | solution.py:13
  22.3 2.1 %fusion.3 = f32[32,128]{1,0:T(8,128)S(1)} fusion(f32[32,128,384]{2,1,0:T(8,128)S(1)} %get-tuple-element.5, f32[32,128]{1,0:T(8,128)S(1)} %multiply_maximum_fusion, pred[32,384]{1,0:T(8,128)(4,1)S(1)} %iota_compare_fusion), kind=kLoop, calls=%fused_computation.7 | loop fusion | flops 7860224 | bytes 6336512 | tf_op jit(solution)/shard_map/reduce_sum | solution.py:26
  24.4 9.0 %divide_convert_fusion = bf16[32,128,512]{2,1,0:T(8,128)(2,1)} fusion(f32[32,128]{1,0:T(8,128)S(1)} %get-tuple-element.3, f32[32,512]{1,0:T(8,128)S(1)} %slice_convert_fusion, f32[32,128]{1,0:T(8,128)S(1)} %convert_element_type.46, bf16[32,384,576]{1,2,0:T(8,128)(2,1)} %param.10, f32[32,128,384]{2,1,0:T(8,128)S(1)} %get-tuple-element.5, ...), kind=kOutput, calls=%fused_computation.3 | convolution fusion | flops 1626865664 | bytes 23195648 | tf_op jit(solution)/shard_map/bhl,bld->bhd/dot_general | solution.py:27
  33.5 4.7 %copy.14 = bf16[32,128,512]{2,0,1:T(8,128)(2,1)S(1)} copy(bf16[32,128,512]{2,1,0:T(8,128)(2,1)} %divide_convert_fusion) | data formatting | bytes 8388608 | tf_op jit(solution)/shard_map/convert_element_type | solution.py:35
  38.2 0.0 slice-start.2
  38.2 57.9 %all_to_all.18 = bf16[32,128,512]{2,0,1:T(8,128)(2,1)S(1)} all-to-all(bf16[32,128,512]{2,0,1:T(8,128)(2,1)S(1)} %copy.14), channel_id=1, replica_groups=mesh['dp'=8,'tp'=16] {'tp'}, dimensions={1} | all-to-all | bytes 8388608 | tf_op jit(solution)/shard_map/all_to_all | solution.py:41
  96.1 0.6 copy.15
  96.7 0.0 copy-done
  96.7 1.5 convolution_convert_fusion.1
  98.2 0.0 slice-done
  98.2 0.0 slice-done.1
  98.2 10.1 %convolution_convert_fusion = bf16[512,7168]{1,0:T(8,128)(2,1)} fusion(bf16[512,1024]{0,1:T(8,128)(2,1)S(1)} %bitcast.19, bf16[1024,7168]{1,0:T(8,128)(2,1)S(1)} %bitcast.24), kind=kOutput, calls=%fused_computation.2 | convolution fusion | flops 7519862784 | bytes 23068672 | tf_op jit(solution)/shard_map/dot_general | solution.py:47
  108.4 0.0 reduce-scatter.2.cloned.1.call-update
  108.4 0.7 copy-done.3
  109.1 90.9 %reduce-scatter.2.cloned.1.call-done = bf16[32,7168]{1,0:T(8,128)(2,1)} async-done(((bf16[512,7168]{1,0:T(8,128)(2,1)}), bf16[32,7168]{1,0:T(8,128)(2,1)}) %reduce-scatter.2.cloned.1.call-update) | async-done | bytes 458768 | tf_op jit(solution)/shard_map/reduce_scatter | solution.py:46
  200.0 1.1 add_convert_fusion
  201.1 0.0 copy-start.1
  201.1 0.2 fusion.15
  201.3 0.9 fusion.17
  (15 shorter events, 0.1 us)
Async XLA Ops:
  7.2 89.5 %copy-start = (bf16[8,512,128]{2,1,0:T(8,128)(2,1)S(1)}, bf16[8,512,128]{2,1,0:T(8,128)(2,1)}, u32[]{:S(2)}) copy-start(bf16[8,512,128]{2,1,0:T(8,128)(2,1)} %param.13) | copy-start | bytes 3145732
  7.2 192.8 %reduce-scatter.2.cloned.1.call-start = ((), (), s32[]{:S(2)}) async-start(), calls=%async_computation.2 | async-start | bytes 7798784 | tf_op jit(solution)/shard_map/reduce_scatter | solution.py:46
  33.5 64.7 %slice-start = ((s8[14680064]{0:T(1024)(128)(4,1)}), s8[4194304]{0:T(1024)(128)(4,1)S(1)}, s32[]{:S(2)}) async-start(s8[14680064]{0:T(1024)(128)(4,1)} %bitcast.23), calls=%async_computation.3 | async-start | bytes 8388608
  33.5 64.7 %slice-start.1 = ((s8[14680064]{0:T(1024)(128)(4,1)}), s8[4194304]{0:T(1024)(128)(4,1)S(1)}, s32[]{:S(2)}) async-start(s8[14680064]{0:T(1024)(128)(4,1)} %bitcast.23), calls=%async_computation.4 | async-start | bytes 8388608
  38.2 60.0 %slice-start.2 = ((s8[14680064]{0:T(1024)(128)(4,1)}), s8[4194304]{0:T(1024)(128)(4,1)S(1)}, s32[]{:S(2)}) async-start(s8[14680064]{0:T(1024)(128)(4,1)} %bitcast.23), calls=%async_computation.5 | async-start | bytes 8388608
  96.1 2.1 %slice-start.3 = ((s8[14680064]{0:T(1024)(128)(4,1)}), s8[2097152]{0:T(1024)(128)(4,1)S(1)}, s32[]{:S(2)}) async-start(s8[14680064]{0:T(1024)(128)(4,1)} %bitcast.23), calls=%async_computation.6 | async-start | bytes 4194304
  108.4 0.7 copy-start.3
  108.4 91.6 %copy-start.2 = (bf16[32,7168]{1,0:T(8,128)(2,1)S(1)}, bf16[32,7168]{1,0:T(8,128)(2,1)}, u32[]{:S(2)}) copy-start(bf16[32,7168]{1,0:T(8,128)(2,1)} %param.12) | copy-start | bytes 1376260
  201.1 1.2 copy-start.1
Sparse Core Ops, SparseCore 0:
  108.5 91.3 reduce-scatter.1
where the time goes:
time: 211 us; the launch traced here: 209 us
  waiting for transfers between devices  90.9 us (43%)
  blocking collectives  57.9 us (27%)
  matrix products  34.2 us (16%)
  between operations  14.2 us (7%)
  other arithmetic  6.03 us (3%)
  local copies, waits for them, and re-layouts  5.98 us (3%)
    reduce_scatter x1, waiting for transfers between devices, per_device(): lax.psum_scatter(jnp.dot(flattened, out_proj, preferred_element_type=jnp....  90.9 us
    all_to_all x1, blocking collectives, per_device(): lax.all_to_all(attended, 'tp', split_axis=1, concat_axis=0, tiled=True)  57.9 us
    dot_general x1, matrix products, attend_rows(): jnp.einsum('bhc,blc->bhl', queries, key_rows, preferred_element_type=jnp....  10.4 us
    dot_general x1, matrix products, per_device(): jnp.dot(flattened, out_proj, preferred_element_type=jnp.float32)  10.1 us
    dot_general x1, matrix products, attend_rows(): jnp.einsum('bhl,bld->bhd', probs.astype(jnp.bfloat16), key_rows[:, :, :la...  9.04 us
    convert_element_type x1, local copies, waits for them, and re-layouts, attend_rows(): return (summed / totals[:, :, None]).astype(jnp.bfloat16)  4.68 us
  transfers between devices with their start and end apart: 1, of which 1 were waited for; matrix products, arithmetic and copies ran while one was open for 0% of the time, Pallas kernels for 0%

commit v1 on v0

v1 whole, which is shorter than its diff:
```python
import functools

import jax
import jax.numpy as jnp
from jax import lax
from jax.experimental import pallas as pl
from jax.experimental.pallas import tpu as pltpu
from jax.sharding import PartitionSpec as P

softmax_scale = 0.1353
masked_score = -1e30
epsilon = 1e-06

N_X, N_Y, N_CORE = 4, 2, 2
STEP = 4
TILE = 512
WHOLE = pl.BlockSpec(memory_space=pltpu.VMEM)


def moved(array, dx=0, dy=0, dcore=0):
    pairs = []
    for t in range(N_X * N_Y * N_CORE):
        x, y, core = t // (N_Y * N_CORE), t // N_CORE % N_Y, t % N_CORE
        to = ((x + dx) % N_X * N_Y + (y ^ dy)) * N_CORE + (core ^ dcore)
        pairs.append((t, to))
    return lax.ppermute(array, "tp", pairs)


def attend_kernel(first, rows, latent, len_ref, group_ref, q_ref, c_ref, n_ref, *rest):
    outs, (stage, new_wide) = rest[:-2], rest[-2:]
    i = pl.program_id(0)
    heads, slots = q_ref.shape[2], c_ref.shape[2]

    @pl.when(i == 0)
    def _():
        new_wide[...] = n_ref[...].astype(jnp.float32)

    def attend_to(seen):
        every = range(STEP)
        queries = [q_ref[j].T for j in every]
        keys = [c_ref[j, :, :seen] for j in every]
        news = [new_wide[pl.ds(first + i * STEP + j, 1), :] for j in every]
        scores = [
            jnp.dot(q, k, preferred_element_type=jnp.float32) * softmax_scale
            for q, k in zip(queries, keys)
        ]
        new_scores = [
            jnp.sum(q.astype(jnp.float32) * n, axis=1, keepdims=True) * softmax_scale
            for q, n in zip(queries, news)
        ]
        positions = lax.broadcasted_iota(jnp.int32, (1, seen), 1)
        masked = [
            jnp.where(positions < len_ref[first + i * STEP + j], scores[j], masked_score)
            for j in every
        ]
        maxima = [
            jnp.maximum(jnp.max(m, axis=1, keepdims=True), n) for m, n in zip(masked, new_scores)
        ]
        probs = [jnp.exp(m - top) for m, top in zip(masked, maxima)]
        new_probs = [jnp.exp(n - top) for n, top in zip(new_scores, maxima)]
        summed = [
            lax.dot_general(
                p.astype(jnp.bfloat16),
                k[:latent],
                (((1,), (1,)), ((), ())),
                preferred_element_type=jnp.float32,
            )
            for p, k in zip(probs, keys)
        ]
        inverse = [
            1.0 / (jnp.sum(p, axis=1, keepdims=True) + n) for p, n in zip(probs, new_probs)
        ]
        for j in every:
            new_low = new_probs[j].astype(jnp.bfloat16).astype(jnp.float32)
            attended = (summed[j] + new_low * news[j][:, :latent]) * inverse[j]
            for c in range(latent // 128):
                stage[c, pl.ds(i * STEP + j, heads, stride=rows), :] = attended[
                    :, c * 128 : (c + 1) * 128
                ]

    longest = len_ref[first + i * STEP]
    for j in range(1, STEP):
        longest = jnp.maximum(longest, len_ref[first + i * STEP + j])
    for seen in range(128, slots + 1, 128):
        in_reach = (longest > seen - 128) & (longest <= seen)
        pl.when(in_reach)(functools.partial(attend_to, seen))

    @pl.when(i == pl.num_programs(0) - 1)
    def _():
        per = heads // (len(outs) * N_CORE)
        for r, out in enumerate(outs):
            for s in range(N_CORE):
                at = pl.multiple_of(group_ref[r * N_CORE + s] * (per * rows), per * rows)
                for c in range(latent // 128):
                    block = stage[c, pl.ds(at, per * rows), :].reshape(per, rows, 128)
                    out[s * per : (s + 1) * per, :, c * 128 : (c + 1) * 128] = block.astype(
                        jnp.bfloat16
                    )


def attend(lengths, groups, queries, cache, new, latent, first, rows):
    reqs, width, heads = queries.shape
    slots = cache.shape[2]
    chips = N_X * N_Y
    at = first // STEP
    block = (heads // chips, rows, latent)
    return pl.pallas_call(
        functools.partial(attend_kernel, first, rows, latent),
        grid_spec=pltpu.PrefetchScalarGridSpec(
            num_scalar_prefetch=2,
            grid=(rows // STEP,),
            in_specs=[
                pl.BlockSpec((STEP, width, heads), lambda i, *_: (at + i, 0, 0)),
                pl.BlockSpec((STEP, width, slots), lambda i, *_: (at + i, 0, 0)),
                pl.BlockSpec((reqs, width), lambda i, *_: (0, 0)),
            ],
            out_specs=[pl.BlockSpec(block, lambda i, *_: (0, 0, 0))] * chips,
            scratch_shapes=[
                pltpu.VMEM((latent // 128, heads * rows, 128), jnp.float32),
                pltpu.VMEM((reqs, width), jnp.float32),
            ],
        ),
        out_shape=[jax.ShapeDtypeStruct(block, jnp.bfloat16)] * chips,
        compiler_params=pltpu.CompilerParams(vmem_limit_bytes=56 << 20),
        cost_estimate=pl.CostEstimate(
            flops=2 * rows * heads * slots * (width + latent),
            bytes_accessed=2 * rows * (width * (slots + heads) + heads * latent),
            transcendentals=rows * heads * slots,
        ),
        name="attend",
    )(lengths, groups, queries, cache, new)


def project_tile(values, own_ref, other_ref):
    half = own_ref.shape[0]
    return jnp.dot(
        values[:, :half], own_ref[...], preferred_element_type=jnp.float32
    ) + jnp.dot(values[:, half:], other_ref[...], preferred_element_type=jnp.float32)


def lift_project_kernel(count, *refs):
    blocks, (own_up, other_up, own_ref, other_ref, values_out, keep, send, values) = (
        refs[:count],
        refs[count:],
    )
    heads = own_up.shape[0]
    depth = own_up.shape[2]

    @pl.when(pl.program_id(0) == 0)
    def _():
        for h in range(2 * heads):
            up = own_up[h] if h < heads else other_up[h - heads]
            rows = jnp.concatenate([b[h] for b in blocks], axis=0)
            lifted = jnp.dot(rows, up, preferred_element_type=jnp.float32).astype(jnp.bfloat16)
            values[:, h * depth : (h + 1) * depth] = lifted
        values_out[...] = values[...]

    tile = project_tile(values[...], own_ref, other_ref).astype(jnp.bfloat16)
    keep[...] = tile[: keep.shape[0]]
    send[...] = tile[keep.shape[0] :]


def lift_project(blocks, own_up, other_up, own, other, start):
    heads, latent, depth = own_up.shape
    rows = sum(b.shape[1] for b in blocks)
    inner, width = own.shape
    steps = (width - start) // TILE
    at = start // TILE
    half = jax.ShapeDtypeStruct((rows // 2, width - start), jnp.bfloat16)
    return pl.pallas_call(
        functools.partial(lift_project_kernel, len(blocks)),
        grid=(steps,),
        in_specs=[pl.BlockSpec(b.shape, lambda i: (0, 0, 0)) for b in blocks]
        + [pl.BlockSpec(own_up.shape, lambda i: (0, 0, 0))] * 2
        + [pl.BlockSpec((inner, TILE), lambda i: (0, at + i))] * 2,
        out_specs=[pl.BlockSpec((rows, 2 * inner), lambda i: (0, 0))]
        + [pl.BlockSpec((rows // 2, TILE), lambda i: (0, i))] * 2,
        out_shape=[jax.ShapeDtypeStruct((rows, 2 * inner), jnp.bfloat16), half, half],
        scratch_shapes=[pltpu.VMEM((rows, 2 * inner), jnp.bfloat16)],
        compiler_params=pltpu.CompilerParams(vmem_limit_bytes=48 << 20),
        cost_estimate=pl.CostEstimate(
            flops=2 * rows * 2 * heads * latent * depth + 4 * rows * inner * (width - start),
            bytes_accessed=4 * inner * (width - start) + 2 * rows * 2 * heads * latent,
            transcendentals=0,
        ),
        name="lift_project",
    )(*blocks, own_up, other_up, own, other)


def project_kernel(values, own_ref, other_ref, *outs):
    tile = project_tile(values[...], own_ref, other_ref).astype(jnp.bfloat16)
    count, (_, rows, _) = len(outs), outs[0].shape
    for dx, out in enumerate(outs):
        for dy in range(N_Y):
            begin = (dy * count + dx) * rows
            out[dy] = tile[begin : begin + rows]


def project(values, own, other, end):
    rows = values.shape[0]
    inner = own.shape[0]
    each = (N_Y, rows // (N_X * N_Y))
    return pl.pallas_call(
        project_kernel,
        grid=(end // TILE,),
        in_specs=[pl.BlockSpec(values.shape, lambda i: (0, 0))]
        + [pl.BlockSpec((inner, TILE), lambda i: (0, i))] * 2,
        out_specs=[pl.BlockSpec((*each, TILE), lambda i: (0, 0, i))] * N_X,
        out_shape=[jax.ShapeDtypeStruct((*each, end), jnp.bfloat16)] * N_X,
        compiler_params=pltpu.CompilerParams(vmem_limit_bytes=48 << 20),
        cost_estimate=pl.CostEstimate(
            flops=4 * rows * inner * end, bytes_accessed=4 * inner * end, transcendentals=0
        ),
        name="project",
    )(values, own, other)


def split_sum_kernel(a_ref, b_ref, *outs):
    rows = outs[0].shape[0]
    for dx, out in enumerate(outs):
        at = slice(dx * rows, (dx + 1) * rows)
        out[...] = (a_ref[at].astype(jnp.float32) + b_ref[at].astype(jnp.float32)).astype(
            jnp.bfloat16
        )


def split_sum(a, b):
    part = jax.ShapeDtypeStruct((a.shape[0] // N_X, a.shape[1]), jnp.bfloat16)
    return pl.pallas_call(
        split_sum_kernel,
        in_specs=[WHOLE] * 2,
        out_specs=[WHOLE] * N_X,
        out_shape=[part] * N_X,
        compiler_params=pltpu.CompilerParams(vmem_limit_bytes=32 << 20),
        name="split_sum",
    )(a, b)


def pair_sum_kernel(a, b, c, d, keep, send):
    for dy, out in enumerate((keep, send)):
        total = a[dy].astype(jnp.float32) + b[dy].astype(jnp.float32)
        total = total + c[dy].astype(jnp.float32) + d[dy].astype(jnp.float32)
        out[...] = total.astype(jnp.bfloat16)


def pair_sum(parts):
    out = jax.ShapeDtypeStruct(parts[0].shape[1:], jnp.bfloat16)
    return pl.pallas_call(
        pair_sum_kernel,
        in_specs=[WHOLE] * len(parts),
        out_specs=[WHOLE] * 2,
        out_shape=[out] * 2,
        compiler_params=pltpu.CompilerParams(vmem_limit_bytes=32 << 20),
        name="pair_sum",
    )(*parts)


def finish_kernel(count, *refs):
    left, right, (residual, gain, hidden, normed) = refs[:2], refs[2:count], refs[count:]
    split = left[0].shape[1]
    squares = 0.0
    for parts, at in ((left, slice(0, split)), (right, slice(split, residual.shape[1]))):
        total = parts[0][...].astype(jnp.float32)
        for part in parts[1:]:
            total = total + part[...].astype(jnp.float32)
        low = (residual[:, at].astype(jnp.float32) + total).astype(jnp.bfloat16)
        hidden[:, at] = low
        wide = low.astype(jnp.float32)
        squares = squares + jnp.sum(wide * wide, axis=1, keepdims=True)
    factor = lax.rsqrt(squares / residual.shape[1] + epsilon)
    normed[...] = (
        hidden[...].astype(jnp.float32) * factor * gain[...].astype(jnp.float32)
    ).astype(jnp.bfloat16)


def finish(left, right, residual, gain):
    out = jax.ShapeDtypeStruct(residual.shape, jnp.bfloat16)
    count = len(left) + len(right)
    return pl.pallas_call(
        functools.partial(finish_kernel, count),
        in_specs=[WHOLE] * (count + 2),
        out_specs=[WHOLE] * 2,
        out_shape=[out] * 2,
        compiler_params=pltpu.CompilerParams(vmem_limit_bytes=32 << 20),
        name="finish",
    )(*left, *right, residual, gain.reshape(1, -1))


def per_device(queries, new_latent, latent_cache, lengths, residual, value_up, out_proj, norm_gain):
    latent = value_up.shape[1]
    reqs = queries.shape[0]
    width = out_proj.shape[1]
    t = lax.axis_index("tp")
    x, y, core = t // (N_Y * N_CORE), t // N_CORE % N_Y, t % N_CORE
    offsets = [(dx, dy) for dy in range(N_Y) for dx in range(N_X)]
    groups = jnp.stack(
        [
            (((x + dx) % N_X) * N_Y + (y ^ dy)) * N_CORE + (core ^ s)
            for dx, dy in offsets
            for s in range(N_CORE)
        ]
    ).astype(jnp.int32)

    other_up = moved(value_up, dcore=1)
    other_proj = moved(out_proj, dcore=1)

    flat_queries = jnp.swapaxes(queries, 1, 2)
    flat_cache = jnp.swapaxes(latent_cache, 1, 2)
    rows = reqs // 2
    order = [(1, 0), (3, 0), (0, 1), (1, 1), (3, 1), (2, 0), (2, 1)]
    arrived = []
    for first in range(0, reqs, rows):
        blocks = attend(
            lengths, groups, flat_queries, flat_cache, new_latent, latent, first, rows
        )
        got = {(0, 0): blocks[0]}
        for dx, dy in order:
            got[dx, dy] = moved(blocks[offsets.index((dx, dy))], dx=dx, dy=dy)
        arrived.append(got)
    blocks = [got[offset] for offset in offsets for got in arrived]

    split = width // 2
    values, keep, send = lift_project(blocks, value_up, other_up, out_proj, other_proj, split)
    y_sum = moved(send, dy=1)
    by_x = project(values, out_proj, other_proj, split)
    left = [by_x[0]] + [moved(by_x[dx], dx=-dx) for dx in (1, 3, 2)]
    right = split_sum(keep, y_sum)
    right = [right[0]] + [moved(right[dx], dx=-dx) for dx in (1, 3, 2)]
    mine, others = pair_sum(left)
    return tuple(finish([mine, moved(others, dy=1)], right, residual, norm_gain))


def solution(mesh):
    return jax.shard_map(
        per_device,
        mesh=mesh,
        in_specs=(
            P(("dp", "tp"), None, None),
            P(("dp", "tp"), None),
            P(("dp", "tp"), None, None),
            P(("dp", "tp")),
            P(("dp", "tp"), None),
            P("tp", None, None),
            P("tp", None),
            P(),
        ),
        out_specs=(P(("dp", "tp"), None), P(("dp", "tp"), None)),
        check_vma=False,
    )
```

time: 211 us -> 161 us (0.76)
  blocking collectives: 57.9 us -> 0 us
  Pallas kernels: 0 us -> 43.2 us
  starting transfers between devices: 0.04 us -> 36.9 us
  matrix products: 34.2 us -> 0 us
  waiting for transfers between devices: 90.9 us -> 74.9 us
  between operations: 14.2 us -> 0.86 us
  other arithmetic: 6.03 us -> 0 us
  local copies, waits for them, and re-layouts: 5.98 us -> 3.87 us
    reduce_scatter x1 -> x0, waiting for transfers between devices: 90.9 us -> none  [per_device(): lax.psum_scatter(jnp.dot(flattened, out_proj, preferred_element_type=jnp....]
    ppermute x0 -> x24, waiting for transfers between devices: none -> 74.9 us  [moved(): return lax.ppermute(array, 'tp', pairs)]
    all_to_all x1 -> x0, blocking collectives: 57.9 us -> none  [per_device(): lax.all_to_all(attended, 'tp', split_axis=1, concat_axis=0, tiled=True)]
    pallas_call x0 -> x7, Pallas kernels: none -> 43.2 us  [the longest x2 20 us: attend(): pl.pallas_call(functools.partial(attend_kernel, first, rows, latent), gri...]
    ppermute x0 -> x24, starting transfers between devices: none -> 36.9 us  [moved(): return lax.ppermute(array, 'tp', pairs)]
    dot_general x5 -> x0, matrix products: 34.2 us -> none  [the longest x1 10.4 us: attend_rows(): jnp.einsum('bhc,blc->bhl', queries, key_rows, preferred_element_type=jnp....]
    convert_element_type x1 -> x0, local copies, waits for them, and re-layouts: 4.68 us -> none  [attend_rows(): return (summed / totals[:, :, None]).astype(jnp.bfloat16)]
    convert_element_type x6 -> x0, other arithmetic: 2.86 us -> none  [the longest x1 1.12 us: per_device(): hidden = (residual.astype(jnp.float32) + projected).astype(jnp.bfloat16)]
  transfers between devices with their start and end apart: 1 -> 24, of which waited for: 1 -> 14; matrix products, arithmetic and copies ran while one was open for 0% -> 0% of each run, Pallas kernels for 0% -> 19%
where the time goes in v1:
time: 161 us; the launch traced here: 160 us
  waiting for transfers between devices  74.9 us (47%)
  Pallas kernels  43.2 us (27%)
  starting transfers between devices  36.9 us (23%)
  local copies, waits for them, and re-layouts  3.87 us (2%)
    ppermute x24, waiting for transfers between devices, moved(): return lax.ppermute(array, 'tp', pairs)  74.9 us
    ppermute x24, starting transfers between devices, moved(): return lax.ppermute(array, 'tp', pairs)  36.9 us
    pallas_call x2, Pallas kernels, attend(): pl.pallas_call(functools.partial(attend_kernel, first, rows, latent), gri...  20 us
    pallas_call x1, Pallas kernels, lift_project(): pl.pallas_call(functools.partial(lift_project_kernel, len(blocks)), grid=...  12.1 us
    pallas_call x1, Pallas kernels, project(): pl.pallas_call(project_kernel, grid=(end // TILE,), in_specs=[pl.BlockSpe...  9.29 us
  transfers between devices with their start and end apart: 24, of which 14 were waited for; matrix products, arithmetic and copies ran while one was open for 0% of the time, Pallas kernels for 19%

profile of v1, /device:TPU:72, one launch (start us, length us, event | category | flops | bytes accessed | tf_op | source)
XLA Modules:
  0.0 159.7 jit_solution(3540097489398991924)
XLA Ops:
  1.5 10.1 %attend.2 = (bf16[16,16,512]{2,1,0:T(8,128)(2,1)}, bf16[16,16,512]{2,1,0:T(8,128)(2,1)}, bf16[16,16,512]{2,1,0:T(8,128)(2,1)}, bf16[16,16,512]{2,1,0:T(8,128)(2,...) custom-call(s32[32]{0:T(128)} %len_ref.3, ...), custom_call_target="tpu_custom_call" | custom-call | flops 1711276032 | bytes 11534336 | tf_op jit(solution)/shard_map/attend/pallas_call | solution.py:107
  13.1 9.9 %attend.3 = (bf16[16,16,512]{2,1,0:T(8,128)(2,1)}, bf16[16,16,512]{2,1,0:T(8,128)(2,1)}, bf16[16,16,512]{2,1,0:T(8,128)(2,1)}, bf16[16,16,512]{2,1,0:T(8,128)(2,...) custom-call(s32[32]{0:T(128)} %len_ref.3, ...), custom_call_target="tpu_custom_call" | custom-call | flops 1711276032 | bytes 11534336 | tf_op jit(solution)/shard_map/attend/pallas_call | solution.py:107
  24.2 4.2 %collective-permute-start.10 = (bf16[16,16,512]{2,1,0:T(8,128)(2,1)S(1)}, bf16[16,16,512]{2,1,0:T(8,128)(2,1)S(1)}, u32[]{:S(2)}, u32[]{:S(2)}) collective-permute-start(bf16[16,16,512]{2,1,0:T(8,128)(2,1)S(1)} %copy-done.12), channel_id=1, source_target_pairs={{0,10},{1,11},{2,8},{3,9},{4,14},{5,15},{6,12},{7,13},{8,2},{9,3},... | collective-permute-start | bytes 786440 | tf_op jit(solution)/shard_map/ppermute | solution.py:26
  30.1 3.6 %collective-permute-start.12 = (bf16[16,16,512]{2,1,0:T(8,128)(2,1)S(1)}, bf16[16,16,512]{2,1,0:T(8,128)(2,1)S(1)}, u32[]{:S(2)}, u32[]{:S(2)}) collective-permute-start(bf16[16,16,512]{2,1,0:T(8,128)(2,1)S(1)} %copy-done.11), channel_id=1, source_target_pairs={{0,14},{1,15},{2,12},{3,13},{4,2},{5,3},{6,0},{7,1},{8,6},{9,7},{1... | collective-permute-start | bytes 786440 | tf_op jit(solution)/shard_map/ppermute | solution.py:26
  33.7 8.3 %collective-permute-done.10.refs_12_ = bf16[16,16,512]{2,1,0:T(8,128)(2,1)S(1)} collective-permute-done((bf16[16,16,512]{2,1,0:T(8,128)(2,1)S(1)}, bf16[16,16,512]{2,1,0:T(8,128)(2,1)S(1)}, u32[]{:S(2)}, u32[]{:S(2)}) %collective-permute-start.10) | collective-permute-done | bytes 262176 | tf_op jit(solution)/shard_map/ppermute | solution.py:26
  42.0 8.0 %collective-permute-done.11.refs_13_ = bf16[16,16,512]{2,1,0:T(8,128)(2,1)S(1)} collective-permute-done((bf16[16,16,512]{2,1,0:T(8,128)(2,1)}, bf16[16,16,512]{2,1,0:T(8,128)(2,1)S(1)}, u32[]{:S(2)}, u32[]{:S(2)}) %collective-permute-start.11) | collective-permute-done | bytes 262176 | tf_op jit(solution)/shard_map/ppermute | solution.py:26
  50.1 3.1 %collective-permute-done.12.refs_14_ = bf16[16,16,512]{2,1,0:T(8,128)(2,1)S(1)} collective-permute-done((bf16[16,16,512]{2,1,0:T(8,128)(2,1)S(1)}, bf16[16,16,512]{2,1,0:T(8,128)(2,1)S(1)}, u32[]{:S(2)}, u32[]{:S(2)}) %collective-permute-start.12) | collective-permute-done | bytes 262176 | tf_op jit(solution)/shard_map/ppermute | solution.py:26
  53.5 5.2 %collective-permute-done.13.refs_15_ = bf16[16,16,512]{2,1,0:T(8,128)(2,1)S(1)} collective-permute-done((bf16[16,16,512]{2,1,0:T(8,128)(2,1)}, bf16[16,16,512]{2,1,0:T(8,128)(2,1)S(1)}, u32[]{:S(2)}, u32[]{:S(2)}) %collective-permute-start.13) | collective-permute-done | bytes 262176 | tf_op jit(solution)/shard_map/ppermute | solution.py:26
  58.8 2.0 %collective-permute-done.2.refs_4_ = bf16[16,16,512]{2,1,0:T(8,128)(2,1)S(1)} collective-permute-done((bf16[16,16,512]{2,1,0:T(8,128)(2,1)S(1)}, bf16[16,16,512]{2,1,0:T(8,128)(2,1)S(1)}, u32[]{:S(2)}, u32[]{:S(2)}) %collective-permute-start.2) | collective-permute-done | bytes 262176 | tf_op jit(solution)/shard_map/ppermute | solution.py:26
  60.8 3.7 %collective-permute-start.5 = (bf16[16,16,512]{2,1,0:T(8,128)(2,1)}, bf16[16,16,512]{2,1,0:T(8,128)(2,1)S(1)}, u32[]{:S(2)}, u32[]{:S(2)}) collective-permute-start(bf16[16,16,512]{2,1,0:T(8,128)(2,1)} %get-tuple-element.38), channel_id=1, source_target_pairs={{0,12},{1,13},{2,14},{3,15},{4,0},{5,1},{6,2},{7,3},{8,4},{9,5},{1... | collective-permute-start | bytes 786440 | tf_op jit(solution)/shard_map/ppermute | solution.py:26
  64.4 3.3 %collective-permute-start.6 = (bf16[16,16,512]{2,1,0:T(8,128)(2,1)S(1)}, bf16[16,16,512]{2,1,0:T(8,128)(2,1)S(1)}, u32[]{:S(2)}, u32[]{:S(2)}) collective-permute-start(bf16[16,16,512]{2,1,0:T(8,128)(2,1)S(1)} %copy-done.8), channel_id=1, source_target_pairs={{0,2},{1,3},{2,0},{3,1},{4,6},{5,7},{6,4},{7,5},{8,10},{9,11},{10,... | collective-permute-start | bytes 786440 | tf_op jit(solution)/shard_map/ppermute | solution.py:26
  67.7 5.2 %collective-permute-done.4.refs_6_ = bf16[16,16,512]{2,1,0:T(8,128)(2,1)S(1)} collective-permute-done((bf16[16,16,512]{2,1,0:T(8,128)(2,1)S(1)}, bf16[16,16,512]{2,1,0:T(8,128)(2,1)S(1)}, u32[]{:S(2)}, u32[]{:S(2)}) %collective-permute-start.4) | collective-permute-done | bytes 262176 | tf_op jit(solution)/shard_map/ppermute | solution.py:26
  72.9 3.3 %collective-permute-start.7 = (bf16[16,16,512]{2,1,0:T(8,128)(2,1)}, bf16[16,16,512]{2,1,0:T(8,128)(2,1)S(1)}, u32[]{:S(2)}, u32[]{:S(2)}) collective-permute-start(bf16[16,16,512]{2,1,0:T(8,128)(2,1)} %get-tuple-element.40), channel_id=1, source_target_pairs={{0,2},{1,3},{2,0},{3,1},{4,6},{5,7},{6,4},{7,5},{8,10},{9,11},{10,... | collective-permute-start | bytes 786440 | tf_op jit(solution)/shard_map/ppermute | solution.py:26
  77.8 2.6 %collective-permute-start.8 = (bf16[16,16,512]{2,1,0:T(8,128)(2,1)S(1)}, bf16[16,16,512]{2,1,0:T(8,128)(2,1)S(1)}, u32[]{:S(2)}, u32[]{:S(2)}) collective-permute-start(bf16[16,16,512]{2,1,0:T(8,128)(2,1)S(1)} %copy-done.7), channel_id=1, source_target_pairs={{0,6},{1,7},{2,4},{3,5},{4,10},{5,11},{6,8},{7,9},{8,14},{9,15},{1... | collective-permute-start | bytes 786440 | tf_op jit(solution)/shard_map/ppermute | solution.py:26
  81.8 8.9 %collective-permute-done.8.refs_10_ = bf16[16,16,512]{2,1,0:T(8,128)(2,1)S(1)} collective-permute-done((bf16[16,16,512]{2,1,0:T(8,128)(2,1)S(1)}, bf16[16,16,512]{2,1,0:T(8,128)(2,1)S(1)}, u32[]{:S(2)}, u32[]{:S(2)}) %collective-permute-start.8) | collective-permute-done | bytes 262176 | tf_op jit(solution)/shard_map/ppermute | solution.py:26
  90.7 4.0 %collective-permute-done.9.refs_11_ = bf16[16,16,512]{2,1,0:T(8,128)(2,1)S(1)} collective-permute-done((bf16[16,16,512]{2,1,0:T(8,128)(2,1)}, bf16[16,16,512]{2,1,0:T(8,128)(2,1)S(1)}, u32[]{:S(2)}, u32[]{:S(2)}) %collective-permute-start.9) | collective-permute-done | bytes 262176 | tf_op jit(solution)/shard_map/ppermute | solution.py:26
  96.6 12.1 %lift_project.1 = (bf16[256,2048]{1,0:T(8,128)(2,1)}, bf16[128,3584]{1,0:T(8,128)(2,1)S(1)}, bf16[128,3584]{1,0:T(8,128)(2,1)S(1)}) custom-call(bf16[16,16,512]{2,1,0:T(8,128)(2,1)S(1)} %copy-done.2, bf16[16,16,512]{2,1,0:T(8,128)(2,1)S(1)} %copy-done.3, bf16[16,16,512]{2,1,0:T(8,128)(2,1)S(1)} %collective-permute-done.refs_2_, ...), custom_call_target="tpu_custom_call" | custom-call | flops 4294967296 | bytes 18874368 | tf_op jit(solution)/shard_map/lift_project/pallas_call | solution.py:170
  108.7 2.1 %collective-permute-start.20 = (bf16[128,3584]{1,0:T(8,128)(2,1)S(1)}, bf16[128,3584]{1,0:T(8,128)(2,1)S(1)}, u32[]{:S(2)}, u32[]{:S(2)}) collective-permute-start(bf16[128,3584]{1,0:T(8,128)(2,1)S(1)} %get-tuple-element.55), channel_id=1, source_target_pairs={{0,2},{1,3},{2,0},{3,1},{4,6},{5,7},{6,4},{7,5},{8,10},{9,11},{10,... | collective-permute-start | bytes 2752520 | tf_op jit(solution)/shard_map/ppermute | solution.py:26
  112.1 9.3 %project.1 = (bf16[2,32,3584]{2,1,0:T(8,128)(2,1)S(1)}, bf16[2,32,3584]{2,1,0:T(8,128)(2,1)S(1)}, bf16[2,32,3584]{2,1,0:T(8,128)(2,1)S(1)}, bf16[2,32,3584]{2,1,0:T(8,128)(2,1)S(1)}) custom-call(bf16[256,2048]{1,0:T(8,128)(2,1)S(1)} %copy-done, bf16[1024,7168]{1,0:T(8,128)(2,1)} %own_ref.1, bf16[1024,7168]{1,0:T(8,128)(2,1)} %collective-permute-done.15.refs_19_.other_ref), custom_call_target="tpu_custom_call" | custom-call | flops 3758096384 | bytes 14680064 | tf_op jit(solution)/shard_map/project/pallas_call | solution.py:203
  121.4 2.4 %collective-permute-start.16 = (bf16[2,32,3584]{2,1,0:T(8,128)(2,1)S(1)}, bf16[2,32,3584]{2,1,0:T(8,128)(2,1)S(1)}, u32[]{:S(2)}, u32[]{:S(2)}) collective-permute-start(bf16[2,32,3584]{2,1,0:T(8,128)(2,1)S(1)} %get-tuple-element.49), channel_id=1, source_target_pairs={{0,12},{1,13},{2,14},{3,15},{4,0},{5,1},{6,2},{7,3},{8,4},{9,5},{1... | collective-permute-start | bytes 1376264 | tf_op jit(solution)/shard_map/ppermute | solution.py:26
  125.4 17.0 %collective-permute-done.16.b = bf16[2,32,3584]{2,1,0:T(8,128)(2,1)S(1)} collective-permute-done((bf16[2,32,3584]{2,1,0:T(8,128)(2,1)S(1)}, bf16[2,32,3584]{2,1,0:T(8,128)(2,1)S(1)}, u32[]{:S(2)}, u32[]{:S(2)}) %collective-permute-start.16) | collective-permute-done | bytes 458784 | tf_op jit(solution)/shard_map/ppermute | solution.py:26
  142.3 3.4 %collective-permute-done.17.c = bf16[2,32,3584]{2,1,0:T(8,128)(2,1)S(1)} collective-permute-done((bf16[2,32,3584]{2,1,0:T(8,128)(2,1)S(1)}, bf16[2,32,3584]{2,1,0:T(8,128)(2,1)S(1)}, u32[]{:S(2)}, u32[]{:S(2)}) %collective-permute-start.17) | collective-permute-done | bytes 458784 | tf_op jit(solution)/shard_map/ppermute | solution.py:26
  150.2 3.4 %collective-permute-done.19.refs_1_ = bf16[32,3584]{1,0:T(8,128)(2,1)S(1)} collective-permute-done((bf16[32,3584]{1,0:T(8,128)(2,1)S(1)}, bf16[32,3584]{1,0:T(8,128)(2,1)S(1)}, u32[]{:S(2)}, u32[]{:S(2)}) %collective-permute-start.19) | collective-permute-done | bytes 229408 | tf_op jit(solution)/shard_map/ppermute | solution.py:26
  153.9 4.5 %collective-permute-done.22.refs_4_ = bf16[32,3584]{1,0:T(8,128)(2,1)S(1)} collective-permute-done((bf16[32,3584]{1,0:T(8,128)(2,1)S(1)}, bf16[32,3584]{1,0:T(8,128)(2,1)S(1)}, u32[]{:S(2)}, u32[]{:S(2)}) %collective-permute-start.22) | collective-permute-done | bytes 229408 | tf_op jit(solution)/shard_map/ppermute | solution.py:26
  (59 shorter events, 19.2 us)
Async XLA Ops:
  0.6 94.0 %collective-permute-start.15 = (bf16[1024,7168]{1,0:T(8,128)(2,1)}, bf16[1024,7168]{1,0:T(8,128)(2,1)}, u32[]{:S(2)}, u32[]{:S(2)}) collective-permute-start(bf16[1024,7168]{1,0:T(8,128)(2,1)} %own_ref.1), channel_id=1, source_target_pairs={{0,1},{1,0},{2,3},{3,2},{4,5},{5,4},{6,7},{7,6},{8,9},{9,8},{10,11... | collective-permute-start | bytes 44040200 | tf_op jit(solution)/shard_map/ppermute | solution.py:26
  11.6 18.5 %collective-permute-start = (bf16[16,16,512]{2,1,0:T(8,128)(2,1)}, bf16[16,16,512]{2,1,0:T(8,128)(2,1)S(1)}, u32[]{:S(2)}, u32[]{:S(2)}) collective-permute-start(bf16[16,16,512]{2,1,0:T(8,128)(2,1)} %get-tuple-element.33), channel_id=1, source_target_pairs={{0,4},{1,5},{2,6},{3,7},{4,8},{5,9},{6,10},{7,11},{8,12},{9,13},{1... | collective-permute-start | bytes 786440 | tf_op jit(solution)/shard_map/ppermute | solution.py:26
  23.0 10.7 %collective-permute-start.1 = (bf16[16,16,512]{2,1,0:T(8,128)(2,1)}, bf16[16,16,512]{2,1,0:T(8,128)(2,1)S(1)}, u32[]{:S(2)}, u32[]{:S(2)}) collective-permute-start(bf16[16,16,512]{2,1,0:T(8,128)(2,1)} %get-tuple-element.34), channel_id=1, source_target_pairs={{0,4},{1,5},{2,6},{3,7},{4,8},{5,9},{6,10},{7,11},{8,12},{9,13},{1... | collective-permute-start | bytes 786440 | tf_op jit(solution)/shard_map/ppermute | solution.py:26
  24.2 17.8 %collective-permute-start.10 = (bf16[16,16,512]{2,1,0:T(8,128)(2,1)S(1)}, bf16[16,16,512]{2,1,0:T(8,128)(2,1)S(1)}, u32[]{:S(2)}, u32[]{:S(2)}) collective-permute-start(bf16[16,16,512]{2,1,0:T(8,128)(2,1)S(1)} %copy-done.12), channel_id=1, source_target_pairs={{0,10},{1,11},{2,8},{3,9},{4,14},{5,15},{6,12},{7,13},{8,2},{9,3},... | collective-permute-start | bytes 786440 | tf_op jit(solution)/shard_map/ppermute | solution.py:26
  28.3 21.7 %collective-permute-start.11 = (bf16[16,16,512]{2,1,0:T(8,128)(2,1)}, bf16[16,16,512]{2,1,0:T(8,128)(2,1)S(1)}, u32[]{:S(2)}, u32[]{:S(2)}) collective-permute-start(bf16[16,16,512]{2,1,0:T(8,128)(2,1)} %get-tuple-element.44), channel_id=1, source_target_pairs={{0,10},{1,11},{2,8},{3,9},{4,14},{5,15},{6,12},{7,13},{8,2},{9,3},... | collective-permute-start | bytes 786440 | tf_op jit(solution)/shard_map/ppermute | solution.py:26
  30.1 23.1 %collective-permute-start.12 = (bf16[16,16,512]{2,1,0:T(8,128)(2,1)S(1)}, bf16[16,16,512]{2,1,0:T(8,128)(2,1)S(1)}, u32[]{:S(2)}, u32[]{:S(2)}) collective-permute-start(bf16[16,16,512]{2,1,0:T(8,128)(2,1)S(1)} %copy-done.11), channel_id=1, source_target_pairs={{0,14},{1,15},{2,12},{3,13},{4,2},{5,3},{6,0},{7,1},{8,6},{9,7},{1... | collective-permute-start | bytes 786440 | tf_op jit(solution)/shard_map/ppermute | solution.py:26
  33.7 60.9 %collective-permute-start.14 = (bf16[8,512,128]{2,1,0:T(8,128)(2,1)S(1)}, bf16[8,512,128]{2,1,0:T(8,128)(2,1)S(1)}, u32[]{:S(2)}, u32[]{:S(2)}) collective-permute-start(bf16[8,512,128]{2,1,0:T(8,128)(2,1)S(1)} %copy-done.4), channel_id=1, source_target_pairs={{0,1},{1,0},{2,3},{3,2},{4,5},{5,4},{6,7},{7,6},{8,9},{9,8},{10,11... | collective-permute-start | bytes 3145736 | tf_op jit(solution)/shard_map/ppermute | solution.py:26
  42.0 16.7 %collective-permute-start.13 = (bf16[16,16,512]{2,1,0:T(8,128)(2,1)}, bf16[16,16,512]{2,1,0:T(8,128)(2,1)S(1)}, u32[]{:S(2)}, u32[]{:S(2)}) collective-permute-start(bf16[16,16,512]{2,1,0:T(8,128)(2,1)} %get-tuple-element.46), channel_id=1, source_target_pairs={{0,14},{1,15},{2,12},{3,13},{4,2},{5,3},{6,0},{7,1},{8,6},{9,7},{1... | collective-permute-start | bytes 786440 | tf_op jit(solution)/shard_map/ppermute | solution.py:26
  50.0 10.7 %collective-permute-start.2 = (bf16[16,16,512]{2,1,0:T(8,128)(2,1)S(1)}, bf16[16,16,512]{2,1,0:T(8,128)(2,1)S(1)}, u32[]{:S(2)}, u32[]{:S(2)}) collective-permute-start(bf16[16,16,512]{2,1,0:T(8,128)(2,1)S(1)} %copy-done.10), channel_id=1, source_target_pairs={{0,8},{1,9},{2,10},{3,11},{4,12},{5,13},{6,14},{7,15},{8,0},{9,1},... | collective-permute-start | bytes 786440 | tf_op jit(solution)/shard_map/ppermute | solution.py:26
  53.2 11.2 %collective-permute-start.3 = (bf16[16,16,512]{2,1,0:T(8,128)(2,1)}, bf16[16,16,512]{2,1,0:T(8,128)(2,1)S(1)}, u32[]{:S(2)}, u32[]{:S(2)}) collective-permute-start(bf16[16,16,512]{2,1,0:T(8,128)(2,1)} %get-tuple-element.36), channel_id=1, source_target_pairs={{0,8},{1,9},{2,10},{3,11},{4,12},{5,13},{6,14},{7,15},{8,0},{9,1},... | collective-permute-start | bytes 786440 | tf_op jit(solution)/shard_map/ppermute | solution.py:26
  58.8 14.2 %collective-permute-start.4 = (bf16[16,16,512]{2,1,0:T(8,128)(2,1)S(1)}, bf16[16,16,512]{2,1,0:T(8,128)(2,1)S(1)}, u32[]{:S(2)}, u32[]{:S(2)}) collective-permute-start(bf16[16,16,512]{2,1,0:T(8,128)(2,1)S(1)} %copy-done.9), channel_id=1, source_target_pairs={{0,12},{1,13},{2,14},{3,15},{4,0},{5,1},{6,2},{7,3},{8,4},{9,5},{1... | collective-permute-start | bytes 786440 | tf_op jit(solution)/shard_map/ppermute | solution.py:26
  60.8 17.0 %collective-permute-start.5 = (bf16[16,16,512]{2,1,0:T(8,128)(2,1)}, bf16[16,16,512]{2,1,0:T(8,128)(2,1)S(1)}, u32[]{:S(2)}, u32[]{:S(2)}) collective-permute-start(bf16[16,16,512]{2,1,0:T(8,128)(2,1)} %get-tuple-element.38), channel_id=1, source_target_pairs={{0,12},{1,13},{2,14},{3,15},{4,0},{5,1},{6,2},{7,3},{8,4},{9,5},{1... | collective-permute-start | bytes 786440 | tf_op jit(solution)/shard_map/ppermute | solution.py:26
  64.4 16.0 %collective-permute-start.6 = (bf16[16,16,512]{2,1,0:T(8,128)(2,1)S(1)}, bf16[16,16,512]{2,1,0:T(8,128)(2,1)S(1)}, u32[]{:S(2)}, u32[]{:S(2)}) collective-permute-start(bf16[16,16,512]{2,1,0:T(8,128)(2,1)S(1)} %copy-done.8), channel_id=1, source_target_pairs={{0,2},{1,3},{2,0},{3,1},{4,6},{5,7},{6,4},{7,5},{8,10},{9,11},{10,... | collective-permute-start | bytes 786440 | tf_op jit(solution)/shard_map/ppermute | solution.py:26
  72.9 8.9 %collective-permute-start.7 = (bf16[16,16,512]{2,1,0:T(8,128)(2,1)}, bf16[16,16,512]{2,1,0:T(8,128)(2,1)S(1)}, u32[]{:S(2)}, u32[]{:S(2)}) collective-permute-start(bf16[16,16,512]{2,1,0:T(8,128)(2,1)} %get-tuple-element.40), channel_id=1, source_target_pairs={{0,2},{1,3},{2,0},{3,1},{4,6},{5,7},{6,4},{7,5},{8,10},{9,11},{10,... | collective-permute-start | bytes 786440 | tf_op jit(solution)/shard_map/ppermute | solution.py:26
  77.8 12.9 %collective-permute-start.8 = (bf16[16,16,512]{2,1,0:T(8,128)(2,1)S(1)}, bf16[16,16,512]{2,1,0:T(8,128)(2,1)S(1)}, u32[]{:S(2)}, u32[]{:S(2)}) collective-permute-start(bf16[16,16,512]{2,1,0:T(8,128)(2,1)S(1)} %copy-done.7), channel_id=1, source_target_pairs={{0,6},{1,7},{2,4},{3,5},{4,10},{5,11},{6,8},{7,9},{8,14},{9,15},{1... | collective-permute-start | bytes 786440 | tf_op jit(solution)/shard_map/ppermute | solution.py:26
  80.4 14.2 %collective-permute-start.9 = (bf16[16,16,512]{2,1,0:T(8,128)(2,1)}, bf16[16,16,512]{2,1,0:T(8,128)(2,1)S(1)}, u32[]{:S(2)}, u32[]{:S(2)}) collective-permute-start(bf16[16,16,512]{2,1,0:T(8,128)(2,1)} %get-tuple-element.42), channel_id=1, source_target_pairs={{0,6},{1,7},{2,4},{3,5},{4,10},{5,11},{6,8},{7,9},{8,14},{9,15},{1... | collective-permute-start | bytes 786440 | tf_op jit(solution)/shard_map/ppermute | solution.py:26
  108.7 38.6 %collective-permute-start.20 = (bf16[128,3584]{1,0:T(8,128)(2,1)S(1)}, bf16[128,3584]{1,0:T(8,128)(2,1)S(1)}, u32[]{:S(2)}, u32[]{:S(2)}) collective-permute-start(bf16[128,3584]{1,0:T(8,128)(2,1)S(1)} %get-tuple-element.55), channel_id=1, source_target_pairs={{0,2},{1,3},{2,0},{3,1},{4,6},{5,7},{6,4},{7,5},{8,10},{9,11},{10,... | collective-permute-start | bytes 2752520 | tf_op jit(solution)/shard_map/ppermute | solution.py:26
  121.4 20.9 %collective-permute-start.16 = (bf16[2,32,3584]{2,1,0:T(8,128)(2,1)S(1)}, bf16[2,32,3584]{2,1,0:T(8,128)(2,1)S(1)}, u32[]{:S(2)}, u32[]{:S(2)}) collective-permute-start(bf16[2,32,3584]{2,1,0:T(8,128)(2,1)S(1)} %get-tuple-element.49), channel_id=1, source_target_pairs={{0,12},{1,13},{2,14},{3,15},{4,0},{5,1},{6,2},{7,3},{8,4},{9,5},{1... | collective-permute-start | bytes 1376264 | tf_op jit(solution)/shard_map/ppermute | solution.py:26
  123.8 21.9 %collective-permute-start.17 = (bf16[2,32,3584]{2,1,0:T(8,128)(2,1)S(1)}, bf16[2,32,3584]{2,1,0:T(8,128)(2,1)S(1)}, u32[]{:S(2)}, u32[]{:S(2)}) collective-permute-start(bf16[2,32,3584]{2,1,0:T(8,128)(2,1)S(1)} %get-tuple-element.50), channel_id=1, source_target_pairs={{0,4},{1,5},{2,6},{3,7},{4,8},{5,9},{6,10},{7,11},{8,12},{9,13},{1... | collective-permute-start | bytes 1376264 | tf_op jit(solution)/shard_map/ppermute | solution.py:26
  123.8 21.9 %collective-permute-start.18 = (bf16[2,32,3584]{2,1,0:T(8,128)(2,1)S(1)}, bf16[2,32,3584]{2,1,0:T(8,128)(2,1)S(1)}, u32[]{:S(2)}, u32[]{:S(2)}) collective-permute-start(bf16[2,32,3584]{2,1,0:T(8,128)(2,1)S(1)} %get-tuple-element.51), channel_id=1, source_target_pairs={{0,8},{1,9},{2,10},{3,11},{4,12},{5,13},{6,14},{7,15},{8,0},{9,1},... | collective-permute-start | bytes 1376264 | tf_op jit(solution)/shard_map/ppermute | solution.py:26
  146.0 7.6 %collective-permute-start.19 = (bf16[32,3584]{1,0:T(8,128)(2,1)S(1)}, bf16[32,3584]{1,0:T(8,128)(2,1)S(1)}, u32[]{:S(2)}, u32[]{:S(2)}) collective-permute-start(bf16[32,3584]{1,0:T(8,128)(2,1)S(1)} %get-tuple-element.53), channel_id=1, source_target_pairs={{0,2},{1,3},{2,0},{3,1},{4,6},{5,7},{6,4},{7,5},{8,10},{9,11},{10,... | collective-permute-start | bytes 688136 | tf_op jit(solution)/shard_map/ppermute | solution.py:26
  147.5 6.4 %collective-permute-start.21 = (bf16[32,3584]{1,0:T(8,128)(2,1)S(1)}, bf16[32,3584]{1,0:T(8,128)(2,1)S(1)}, u32[]{:S(2)}, u32[]{:S(2)}) collective-permute-start(bf16[32,3584]{1,0:T(8,128)(2,1)S(1)} %get-tuple-element.57), channel_id=1, source_target_pairs={{0,12},{1,13},{2,14},{3,15},{4,0},{5,1},{6,2},{7,3},{8,4},{9,5},{1... | collective-permute-start | bytes 688136 | tf_op jit(solution)/shard_map/ppermute | solution.py:26
  147.9 10.6 %collective-permute-start.22 = (bf16[32,3584]{1,0:T(8,128)(2,1)S(1)}, bf16[32,3584]{1,0:T(8,128)(2,1)S(1)}, u32[]{:S(2)}, u32[]{:S(2)}) collective-permute-start(bf16[32,3584]{1,0:T(8,128)(2,1)S(1)} %get-tuple-element.58), channel_id=1, source_target_pairs={{0,4},{1,5},{2,6},{3,7},{4,8},{5,9},{6,10},{7,11},{8,12},{9,13},{1... | collective-permute-start | bytes 688136 | tf_op jit(solution)/shard_map/ppermute | solution.py:26
  149.6 8.8 %collective-permute-start.23 = (bf16[32,3584]{1,0:T(8,128)(2,1)S(1)}, bf16[32,3584]{1,0:T(8,128)(2,1)S(1)}, u32[]{:S(2)}, u32[]{:S(2)}) collective-permute-start(bf16[32,3584]{1,0:T(8,128)(2,1)S(1)} %get-tuple-element.59), channel_id=1, source_target_pairs={{0,8},{1,9},{2,10},{3,11},{4,12},{5,13},{6,14},{7,15},{8,0},{9,1},... | collective-permute-start | bytes 688136 | tf_op jit(solution)/shard_map/ppermute | solution.py:26
  (13 other events, 439.6 us)

commit v2 on v1

--- a/solution.py
+++ b/solution.py
@@ -12,8 +12,10 @@
 epsilon = 1e-06
 
 N_X, N_Y, N_CORE = 4, 2, 2
+OFFSETS = [(0, 0), (1, 0), (3, 0), (0, 1), (2, 1), (1, 1), (3, 1), (2, 0)]
+IN_FLIGHT = 4
 STEP = 4
-TILE = 512
+TILE = 1792
 WHOLE = pl.BlockSpec(memory_space=pltpu.VMEM)
 
 
@@ -26,7 +28,7 @@
     return lax.ppermute(array, "tp", pairs)
 
 
-def attend_kernel(first, rows, latent, len_ref, group_ref, q_ref, c_ref, n_ref, *rest):
+def attend_kernel(first, rows, latent, len_ref, q_ref, c_ref, n_ref, *rest):
     outs, (stage, new_wide) = rest[:-2], rest[-2:]
     i = pl.program_id(0)
     heads, slots = q_ref.shape[2], c_ref.shape[2]
@@ -88,9 +90,12 @@
     @pl.when(i == pl.num_programs(0) - 1)
     def _():
         per = heads // (len(outs) * N_CORE)
-        for r, out in enumerate(outs):
+        t = lax.axis_index("tp")
+        x, y, core = t // (N_Y * N_CORE), t // N_CORE % N_Y, t % N_CORE
+        for (dx, dy), out in zip(OFFSETS, outs):
+            chip = (x + dx) % N_X * N_Y + (y ^ dy)
             for s in range(N_CORE):
-                at = pl.multiple_of(group_ref[r * N_CORE + s] * (per * rows), per * rows)
+                at = pl.multiple_of((chip * N_CORE + (core ^ s)) * (per * rows), per * rows)
                 for c in range(latent // 128):
                     block = stage[c, pl.ds(at, per * rows), :].reshape(per, rows, 128)
                     out[s * per : (s + 1) * per, :, c * 128 : (c + 1) * 128] = block.astype(
@@ -98,7 +103,7 @@
                     )
 
 
-def attend(lengths, groups, queries, cache, new, latent, first, rows):
+def attend(lengths, queries, cache, new, latent, first, rows):
     reqs, width, heads = queries.shape
     slots = cache.shape[2]
     chips = N_X * N_Y
@@ -107,7 +112,7 @@
     return pl.pallas_call(
         functools.partial(attend_kernel, first, rows, latent),
         grid_spec=pltpu.PrefetchScalarGridSpec(
-            num_scalar_prefetch=2,
+            num_scalar_prefetch=1,
             grid=(rows // STEP,),
             in_specs=[
                 pl.BlockSpec((STEP, width, heads), lambda i, *_: (at + i, 0, 0)),
@@ -121,95 +126,89 @@
             ],
         ),
         out_shape=[jax.ShapeDtypeStruct(block, jnp.bfloat16)] * chips,
-        compiler_params=pltpu.CompilerParams(vmem_limit_bytes=56 << 20),
+        compiler_params=pltpu.CompilerParams(vmem_limit_bytes=20 << 20),
         cost_estimate=pl.CostEstimate(
-            flops=2 * rows * heads * slots * (width + latent),
+            flops=8 * rows * heads * slots * (width + latent),
             bytes_accessed=2 * rows * (width * (slots + heads) + heads * latent),
             transcendentals=rows * heads * slots,
         ),
         name="attend",
-    )(lengths, groups, queries, cache, new)
-
-
-def project_tile(values, own_ref, other_ref):
-    half = own_ref.shape[0]
-    return jnp.dot(
-        values[:, :half], own_ref[...], preferred_element_type=jnp.float32
-    ) + jnp.dot(values[:, half:], other_ref[...], preferred_element_type=jnp.float32)
-
-
-def lift_project_kernel(count, *refs):
-    blocks, (own_up, other_up, own_ref, other_ref, values_out, keep, send, values) = (
-        refs[:count],
-        refs[count:],
-    )
-    heads = own_up.shape[0]
-    depth = own_up.shape[2]
-
-    @pl.when(pl.program_id(0) == 0)
-    def _():
-        for h in range(2 * heads):
-            up = own_up[h] if h < heads else other_up[h - heads]
-            rows = jnp.concatenate([b[h] for b in blocks], axis=0)
-            lifted = jnp.dot(rows, up, preferred_element_type=jnp.float32).astype(jnp.bfloat16)
-            values[:, h * depth : (h + 1) * depth] = lifted
-        values_out[...] = values[...]
-
-    tile = project_tile(values[...], own_ref, other_ref).astype(jnp.bfloat16)
-    keep[...] = tile[: keep.shape[0]]
-    send[...] = tile[keep.shape[0] :]
-
-
-def lift_project(blocks, own_up, other_up, own, other, start):
+    )(lengths, queries, cache, new)
+
+
+def lift_kernel(count, *refs):
+    blocks, (own_up, other_up, *earlier, values) = refs[:count], refs[count:]
+    heads, _, depth = own_up.shape
+    rows = blocks[0].shape[1]
+    blocks = [blocks[OFFSETS.index((dx, dy))] for dy in range(N_Y) for dx in range(N_X)]
+    for h in range(2 * heads):
+        up = own_up[h] if h < heads else other_up[h - heads]
+        stacked = jnp.concatenate([b[h] for b in blocks], axis=0)
+        lifted = jnp.dot(stacked, up, preferred_element_type=jnp.float32).astype(jnp.bfloat16)
+        at = slice(h * depth, (h + 1) * depth)
+        if not earlier:
+            values[:, at] = lifted
+            continue
+        for n in range(count):
+            here = slice(n * rows, (n + 1) * rows)
+            values[2 * n * rows : (2 * n + 1) * rows, at] = earlier[0][here, at]
+            values[(2 * n + 1) * rows : (2 * n + 2) * rows, at] = lifted[here]
+
+
+def lift(blocks, own_up, other_up, *earlier):
     heads, latent, depth = own_up.shape
     rows = sum(b.shape[1] for b in blocks)
-    inner, width = own.shape
-    steps = (width - start) // TILE
-    at = start // TILE
-    half = jax.ShapeDtypeStruct((rows // 2, width - start), jnp.bfloat16)
-    return pl.pallas_call(
-        functools.partial(lift_project_kernel, len(blocks)),
-        grid=(steps,),
-        in_specs=[pl.BlockSpec(b.shape, lambda i: (0, 0, 0)) for b in blocks]
-        + [pl.BlockSpec(own_up.shape, lambda i: (0, 0, 0))] * 2
-        + [pl.BlockSpec((inner, TILE), lambda i: (0, at + i))] * 2,
-        out_specs=[pl.BlockSpec((rows, 2 * inner), lambda i: (0, 0))]
-        + [pl.BlockSpec((rows // 2, TILE), lambda i: (0, i))] * 2,
-        out_shape=[jax.ShapeDtypeStruct((rows, 2 * inner), jnp.bfloat16), half, half],
-        scratch_shapes=[pltpu.VMEM((rows, 2 * inner), jnp.bfloat16)],
-        compiler_params=pltpu.CompilerParams(vmem_limit_bytes=48 << 20),
+    return pl.pallas_call(
+        functools.partial(lift_kernel, len(blocks)),
+        in_specs=[WHOLE] * (len(blocks) + 2 + len(earlier)),
+        out_specs=WHOLE,
+        out_shape=jax.ShapeDtypeStruct((rows * (1 + len(earlier)), 2 * heads * depth), jnp.bfloat16),
+        compiler_params=pltpu.CompilerParams(vmem_limit_bytes=16 << 20),
         cost_estimate=pl.CostEstimate(
-            flops=2 * rows * 2 * heads * latent * depth + 4 * rows * inner * (width - start),
-            bytes_accessed=4 * inner * (width - start) + 2 * rows * 2 * heads * latent,
+            flops=8 * rows * heads * latent * depth,
+            bytes_accessed=4 * rows * heads * latent,
             transcendentals=0,
         ),
-        name="lift_project",
-    )(*blocks, own_up, other_up, own, other)
-
-
-def project_kernel(values, own_ref, other_ref, *outs):
-    tile = project_tile(values[...], own_ref, other_ref).astype(jnp.bfloat16)
-    count, (_, rows, _) = len(outs), outs[0].shape
+        name="lift",
+    )(*blocks, own_up, other_up, *earlier)
+
+
+def project_kernel(start, split, values, own_ref, other_ref, *outs):
+    inner = own_ref.shape[0]
+    at = pl.ds(pl.multiple_of(start + pl.program_id(0) * TILE, TILE), TILE)
+    tile = jnp.dot(values[:, :inner], own_ref[:, at], preferred_element_type=jnp.float32)
+    tile = tile + jnp.dot(values[:, inner:], other_ref[:, at], preferred_element_type=jnp.float32)
+    tile = tile.astype(jnp.bfloat16)
+    if split == "y":
+        rows = tile.shape[0] // N_Y
+        for dy, out in enumerate(outs):
+            out[...] = tile[dy * rows : (dy + 1) * rows]
+        return
+    rows = tile.shape[0] // (N_X * N_Y)
     for dx, out in enumerate(outs):
         for dy in range(N_Y):
-            begin = (dy * count + dx) * rows
+            begin = (dy * N_X + dx) * rows
             out[dy] = tile[begin : begin + rows]
 
 
-def project(values, own, other, end):
+def project(values, own, other, start, end, split):
     rows = values.shape[0]
     inner = own.shape[0]
-    each = (N_Y, rows // (N_X * N_Y))
-    return pl.pallas_call(
-        project_kernel,
-        grid=(end // TILE,),
-        in_specs=[pl.BlockSpec(values.shape, lambda i: (0, 0))]
-        + [pl.BlockSpec((inner, TILE), lambda i: (0, i))] * 2,
-        out_specs=[pl.BlockSpec((*each, TILE), lambda i: (0, 0, i))] * N_X,
-        out_shape=[jax.ShapeDtypeStruct((*each, end), jnp.bfloat16)] * N_X,
-        compiler_params=pltpu.CompilerParams(vmem_limit_bytes=48 << 20),
+    each, index, count = (rows // N_Y,), lambda i: (0, i), N_Y
+    if split == "x":
+        each, index, count = (N_Y, rows // (N_X * N_Y)), lambda i: (0, 0, i), N_X
+    own, other = (pltpu.with_memory_space_constraint(w, pltpu.VMEM) for w in (own, other))
+    return pl.pallas_call(
+        functools.partial(project_kernel, start, split),
+        grid=((end - start) // TILE,),
+        in_specs=[WHOLE] * 3,
+        out_specs=[pl.BlockSpec((*each, TILE), index)] * count,
+        out_shape=[jax.ShapeDtypeStruct((*each, end - start), jnp.bfloat16)] * count,
+        compiler_params=pltpu.CompilerParams(vmem_limit_bytes=12 << 20),
         cost_estimate=pl.CostEstimate(
-            flops=4 * rows * inner * end, bytes_accessed=4 * inner * end, transcendentals=0
+            flops=4 * rows * inner * (end - start),
+            bytes_accessed=2 * rows * (end - start),
+            transcendentals=0,
         ),
         name="project",
     )(values, own, other)
@@ -290,39 +289,29 @@
     latent = value_up.shape[1]
     reqs = queries.shape[0]
     width = out_proj.shape[1]
-    t = lax.axis_index("tp")
-    x, y, core = t // (N_Y * N_CORE), t // N_CORE % N_Y, t % N_CORE
-    offsets = [(dx, dy) for dy in range(N_Y) for dx in range(N_X)]
-    groups = jnp.stack(
-        [
-            (((x + dx) % N_X) * N_Y + (y ^ dy)) * N_CORE + (core ^ s)
-            for dx, dy in offsets
-            for s in range(N_CORE)
-        ]
-    ).astype(jnp.int32)
-
     other_up = moved(value_up, dcore=1)
     other_proj = moved(out_proj, dcore=1)
 
-    flat_queries = jnp.swapaxes(queries, 1, 2)
-    flat_cache = jnp.swapaxes(latent_cache, 1, 2)
+    flat_queries, flat_cache = (
+        pltpu.with_memory_space_constraint(jnp.swapaxes(a, 1, 2), pltpu.HBM)
+        for a in (queries, latent_cache)
+    )
     rows = reqs // 2
-    order = [(1, 0), (3, 0), (0, 1), (1, 1), (3, 1), (2, 0), (2, 1)]
-    arrived = []
+    values, going = [], []
     for first in range(0, reqs, rows):
-        blocks = attend(
-            lengths, groups, flat_queries, flat_cache, new_latent, latent, first, rows
-        )
-        got = {(0, 0): blocks[0]}
-        for dx, dy in order:
-            got[dx, dy] = moved(blocks[offsets.index((dx, dy))], dx=dx, dy=dy)
-        arrived.append(got)
-    blocks = [got[offset] for offset in offsets for got in arrived]
-
-    split = width // 2
-    values, keep, send = lift_project(blocks, value_up, other_up, out_proj, other_proj, split)
+        blocks = attend(lengths, flat_queries, flat_cache, new_latent, latent, first, rows)
+        got = [blocks[0]]
+        for (dx, dy), block in zip(OFFSETS[1:], blocks[1:]):
+            if len(going) >= IN_FLIGHT:
+                block, _ = lax.optimization_barrier((block, going[-IN_FLIGHT]))
+            got.append(moved(block, dx=dx, dy=dy))
+            going.append(got[-1])
+        values = [lift(got, value_up, other_up, *values)]
+
+    half = width // 2
+    keep, send = project(values[0], out_proj, other_proj, half, width, "y")
     y_sum = moved(send, dy=1)
-    by_x = project(values, out_proj, other_proj, split)
+    by_x = project(values[0], out_proj, other_proj, 0, half, "x")
     left = [by_x[0]] + [moved(by_x[dx], dx=-dx) for dx in (1, 3, 2)]
     right = split_sum(keep, y_sum)
     right = [right[0]] + [moved(right[dx], dx=-dx) for dx in (1, 3, 2)]

time: 161 us -> 134 us (0.83)
  Pallas kernels: 43.2 us -> 29.7 us
  waiting for transfers between devices: 74.9 us -> 66.7 us
  starting transfers between devices: 36.9 us -> 33.2 us
  local copies, waits for them, and re-layouts: 3.87 us -> 1.54 us
    pallas_call x2 -> x4, Pallas kernels: 21.4 us -> 10.1 us  [the longest x2 8.69 us: project(): pl.pallas_call(functools.partial(project_kernel, start, split), grid=((en...]
    ppermute x24, waiting for transfers between devices: 74.9 us -> 66.7 us  [moved(): return lax.ppermute(array, 'tp', pairs)]
    ppermute x24, starting transfers between devices: 36.9 us -> 33.2 us  [moved(): return lax.ppermute(array, 'tp', pairs)]
    pallas_call x2, Pallas kernels: 20 us -> 17.8 us  [attend(): pl.pallas_call(functools.partial(attend_kernel, first, rows, latent), gri...]
    unnamed x26 -> x18, local copies, waits for them, and re-layouts: 3.21 us -> 1.53 us
  transfers between devices with their start and end apart: 24 -> 24, of which waited for: 14 -> 12; matrix products, arithmetic and copies ran while one was open for 0% -> 0% of each run, Pallas kernels for 19% -> 18%
where the time goes in v2:
time: 134 us; the launch traced here: 132 us
  waiting for transfers between devices  66.7 us (50%)
  starting transfers between devices  33.2 us (25%)
  Pallas kernels  29.7 us (22%)
  local copies, waits for them, and re-layouts  1.54 us (1%)
    ppermute x24, waiting for transfers between devices, moved(): return lax.ppermute(array, 'tp', pairs)  66.7 us
    ppermute x24, starting transfers between devices, moved(): return lax.ppermute(array, 'tp', pairs)  33.2 us
    pallas_call x2, Pallas kernels, attend(): pl.pallas_call(functools.partial(attend_kernel, first, rows, latent), gri...  17.8 us
    pallas_call x2, Pallas kernels, project(): pl.pallas_call(functools.partial(project_kernel, start, split), grid=((en...  8.69 us
  transfers between devices with their start and end apart: 24, of which 12 were waited for; matrix products, arithmetic and copies ran while one was open for 0% of the time, Pallas kernels for 18%

profile of v2, /device:TPU:72, one launch (start us, length us, event | category | flops | bytes accessed | tf_op | source)
XLA Modules:
  0.0 131.9 jit_solution(18074629560619165058)
XLA Ops:
  2.2 8.5 %attend.3 = (bf16[16,16,512]{2,1,0:T(8,128)(2,1)S(1)}, bf16[16,16,512]{2,1,0:T(8,128)(2,1)S(1)}, bf16[16,16,512]{2,1,0:T(8,128)(2,1)S(1)}, bf16[16,16,512]{2,1,0...) custom-call(s32[32]{0:T(128)S(1)} %copy-done.3, ...), custom_call_target="tpu_custom_call" | custom-call | flops 6845104128 | bytes 11534336 | tf_op jit(solution)/shard_map/attend/pallas_call | solution.py:112
  12.1 2.0 %collective-permute-start.5 = (bf16[16,16,512]{2,1,0:T(8,128)(2,1)S(1)}, bf16[16,16,512]{2,1,0:T(8,128)(2,1)S(1)}, u32[]{:S(2)}, u32[]{:S(2)}) collective-permute-start(bf16[16,16,512]{2,1,0:T(8,128)(2,1)S(1)} %get-tuple-element.51), channel_id=1, source_target_pairs={{0,12},{1,13},{2,14},{3,15},{4,0},{5,1},{6,2},{7,3},{8,4},{9,5},{1... | collective-permute-start | bytes 786440 | tf_op jit(solution)/shard_map/ppermute | solution.py:28
  14.0 2.6 %collective-permute-start.8 = (bf16[16,16,512]{2,1,0:T(8,128)(2,1)S(1)}, bf16[16,16,512]{2,1,0:T(8,128)(2,1)S(1)}, u32[]{:S(2)}, u32[]{:S(2)}) collective-permute-start(bf16[16,16,512]{2,1,0:T(8,128)(2,1)S(1)} %get-tuple-element.56), channel_id=1, source_target_pairs={{0,2},{1,3},{2,0},{3,1},{4,6},{5,7},{6,4},{7,5},{8,10},{9,11},{10,... | collective-permute-start | bytes 786440 | tf_op jit(solution)/shard_map/ppermute | solution.py:28
  18.4 2.3 %collective-permute-done.2.refs_1_ = bf16[16,16,512]{2,1,0:T(8,128)(2,1)S(1)} collective-permute-done((bf16[16,16,512]{2,1,0:T(8,128)(2,1)S(1)}, bf16[16,16,512]{2,1,0:T(8,128)(2,1)S(1)}, u32[]{:S(2)}, u32[]{:S(2)}) %collective-permute-start.2) | collective-permute-done | bytes 262176 | tf_op jit(solution)/shard_map/ppermute | solution.py:28
  20.7 5.0 %collective-permute-done.5.refs_2_ = bf16[16,16,512]{2,1,0:T(8,128)(2,1)S(1)} collective-permute-done((bf16[16,16,512]{2,1,0:T(8,128)(2,1)S(1)}, bf16[16,16,512]{2,1,0:T(8,128)(2,1)S(1)}, u32[]{:S(2)}, u32[]{:S(2)}) %collective-permute-start.5) | collective-permute-done | bytes 262176 | tf_op jit(solution)/shard_map/ppermute | solution.py:28
  25.7 12.1 %collective-permute-done.8.refs_3_ = bf16[16,16,512]{2,1,0:T(8,128)(2,1)S(1)} collective-permute-done((bf16[16,16,512]{2,1,0:T(8,128)(2,1)S(1)}, bf16[16,16,512]{2,1,0:T(8,128)(2,1)S(1)}, u32[]{:S(2)}, u32[]{:S(2)}) %collective-permute-start.8) | collective-permute-done | bytes 262176 | tf_op jit(solution)/shard_map/ppermute | solution.py:28
  39.6 9.3 %attend.2 = (bf16[16,16,512]{2,1,0:T(8,128)(2,1)S(1)}, bf16[16,16,512]{2,1,0:T(8,128)(2,1)S(1)}, bf16[16,16,512]{2,1,0:T(8,128)(2,1)S(1)}, bf16[16,16,512]{2,1,0...) custom-call(s32[32]{0:T(128)S(1)} %copy-done.3, ...), custom_call_target="tpu_custom_call" | custom-call | flops 6845104128 | bytes 11534336 | tf_op jit(solution)/shard_map/attend/pallas_call | solution.py:112
  49.5 2.7 %collective-permute-start.4 = (bf16[16,16,512]{2,1,0:T(8,128)(2,1)S(1)}, bf16[16,16,512]{2,1,0:T(8,128)(2,1)S(1)}, u32[]{:S(2)}, u32[]{:S(2)}) collective-permute-start(bf16[16,16,512]{2,1,0:T(8,128)(2,1)S(1)} %get-tuple-element.48), channel_id=1, source_target_pairs={{0,12},{1,13},{2,14},{3,15},{4,0},{5,1},{6,2},{7,3},{8,4},{9,5},{1... | collective-permute-start | bytes 786440 | tf_op jit(solution)/shard_map/ppermute | solution.py:28
  52.2 2.2 %collective-permute-start.7 = (bf16[16,16,512]{2,1,0:T(8,128)(2,1)S(1)}, bf16[16,16,512]{2,1,0:T(8,128)(2,1)S(1)}, u32[]{:S(2)}, u32[]{:S(2)}) collective-permute-start(bf16[16,16,512]{2,1,0:T(8,128)(2,1)S(1)} %get-tuple-element.53), channel_id=1, source_target_pairs={{0,2},{1,3},{2,0},{3,1},{4,6},{5,7},{6,4},{7,5},{8,10},{9,11},{10,... | collective-permute-start | bytes 786440 | tf_op jit(solution)/shard_map/ppermute | solution.py:28
  54.4 5.1 %collective-permute-done.1.refs_1_ = bf16[16,16,512]{2,1,0:T(8,128)(2,1)S(1)} collective-permute-done((bf16[16,16,512]{2,1,0:T(8,128)(2,1)S(1)}, bf16[16,16,512]{2,1,0:T(8,128)(2,1)S(1)}, u32[]{:S(2)}, u32[]{:S(2)}) %collective-permute-start.1) | collective-permute-done | bytes 262176 | tf_op jit(solution)/shard_map/ppermute | solution.py:28
  60.2 12.1 %collective-permute-done.7.refs_3_ = bf16[16,16,512]{2,1,0:T(8,128)(2,1)S(1)} collective-permute-done((bf16[16,16,512]{2,1,0:T(8,128)(2,1)S(1)}, bf16[16,16,512]{2,1,0:T(8,128)(2,1)S(1)}, u32[]{:S(2)}, u32[]{:S(2)}) %collective-permute-start.7) | collective-permute-done | bytes 262176 | tf_op jit(solution)/shard_map/ppermute | solution.py:28
  72.3 4.3 %collective-permute-start.12 = (bf16[16,16,512]{2,1,0:T(8,128)(2,1)S(1)}, bf16[16,16,512]{2,1,0:T(8,128)(2,1)S(1)}, u32[]{:S(2)}, u32[]{:S(2)}) collective-permute-start(bf16[16,16,512]{2,1,0:T(8,128)(2,1)S(1)} %get-tuple-element.62), channel_id=1, source_target_pairs={{0,14},{1,15},{2,12},{3,13},{4,2},{5,3},{6,0},{7,1},{8,6},{9,7},{1... | collective-permute-start | bytes 786440 | tf_op jit(solution)/shard_map/ppermute | solution.py:28
  78.5 2.6 %collective-permute-done.12.refs_6_ = bf16[16,16,512]{2,1,0:T(8,128)(2,1)S(1)} collective-permute-done((bf16[16,16,512]{2,1,0:T(8,128)(2,1)S(1)}, bf16[16,16,512]{2,1,0:T(8,128)(2,1)S(1)}, u32[]{:S(2)}, u32[]{:S(2)}) %collective-permute-start.12) | collective-permute-done | bytes 262176 | tf_op jit(solution)/shard_map/ppermute | solution.py:28
  81.1 3.3 %collective-permute-done.13.refs_7_ = bf16[16,16,512]{2,1,0:T(8,128)(2,1)S(1)} collective-permute-done((bf16[16,16,512]{2,1,0:T(8,128)(2,1)S(1)}, bf16[16,16,512]{2,1,0:T(8,128)(2,1)S(1)}, u32[]{:S(2)}, u32[]{:S(2)}) %collective-permute-start.13) | collective-permute-done | bytes 262176 | tf_op jit(solution)/shard_map/ppermute | solution.py:28
  85.3 4.4 %project.3 = (bf16[128,3584]{1,0:T(8,128)(2,1)S(1)}, bf16[128,3584]{1,0:T(8,128)(2,1)S(1)}) custom-call(bf16[256,2048]{1,0:T(8,128)(2,1)S(1)} %lift.3.values, bf16[1024,7168]{1,0:T(8,128)(2,1)S(1)} %bitcast.3, bf16[1024,7168]{1,0:T(8,128)(2,1)S(1)} %collective-permute-done.15.other_ref), custom_call_target="tpu_custom_call" | custom-call | flops 3758096384 | bytes 1835008 | tf_op jit(solution)/shard_map/project/pallas_call | solution.py:201
  90.4 4.3 %project.2 = (bf16[2,32,3584]{2,1,0:T(8,128)(2,1)S(1)}, bf16[2,32,3584]{2,1,0:T(8,128)(2,1)S(1)}, bf16[2,32,3584]{2,1,0:T(8,128)(2,1)S(1)}, bf16[2,32,3584]{2,1,0:T(8,128)(2,1)S(1)}) custom-call(bf16[256,2048]{1,0:T(8,128)(2,1)S(1)} %lift.3.values, bf16[1024,7168]{1,0:T(8,128)(2,1)S(1)} %bitcast.3, bf16[1024,7168]{1,0:T(8,128)(2,1)S(1)} %collective-permute-done.15.other_ref), custom_call_target="tpu_custom_call" | custom-call | flops 3758096384 | bytes 1835008 | tf_op jit(solution)/shard_map/project/pallas_call | solution.py:201
  94.8 2.6 %collective-permute-start.16 = (bf16[2,32,3584]{2,1,0:T(8,128)(2,1)S(1)}, bf16[2,32,3584]{2,1,0:T(8,128)(2,1)S(1)}, u32[]{:S(2)}, u32[]{:S(2)}) collective-permute-start(bf16[2,32,3584]{2,1,0:T(8,128)(2,1)S(1)} %get-tuple-element.67), channel_id=1, source_target_pairs={{0,12},{1,13},{2,14},{3,15},{4,0},{5,1},{6,2},{7,3},{8,4},{9,5},{1... | collective-permute-start | bytes 1376264 | tf_op jit(solution)/shard_map/ppermute | solution.py:28
  97.3 2.0 %collective-permute-start.18 = (bf16[2,32,3584]{2,1,0:T(8,128)(2,1)S(1)}, bf16[2,32,3584]{2,1,0:T(8,128)(2,1)S(1)}, u32[]{:S(2)}, u32[]{:S(2)}) collective-permute-start(bf16[2,32,3584]{2,1,0:T(8,128)(2,1)S(1)} %get-tuple-element.69), channel_id=1, source_target_pairs={{0,8},{1,9},{2,10},{3,11},{4,12},{5,13},{6,14},{7,15},{8,0},{9,1},... | collective-permute-start | bytes 1376264 | tf_op jit(solution)/shard_map/ppermute | solution.py:28
  99.3 7.6 %collective-permute-done.16.b = bf16[2,32,3584]{2,1,0:T(8,128)(2,1)S(1)} collective-permute-done((bf16[2,32,3584]{2,1,0:T(8,128)(2,1)S(1)}, bf16[2,32,3584]{2,1,0:T(8,128)(2,1)S(1)}, u32[]{:S(2)}, u32[]{:S(2)}) %collective-permute-start.16) | collective-permute-done | bytes 458784 | tf_op jit(solution)/shard_map/ppermute | solution.py:28
  106.9 9.3 %collective-permute-done.17.c = bf16[2,32,3584]{2,1,0:T(8,128)(2,1)S(1)} collective-permute-done((bf16[2,32,3584]{2,1,0:T(8,128)(2,1)S(1)}, bf16[2,32,3584]{2,1,0:T(8,128)(2,1)S(1)}, u32[]{:S(2)}, u32[]{:S(2)}) %collective-permute-start.17) | collective-permute-done | bytes 458784 | tf_op jit(solution)/shard_map/ppermute | solution.py:28
  116.4 4.1 %collective-permute-start.19 = (bf16[32,3584]{1,0:T(8,128)(2,1)S(1)}, bf16[32,3584]{1,0:T(8,128)(2,1)S(1)}, u32[]{:S(2)}, u32[]{:S(2)}) collective-permute-start(bf16[32,3584]{1,0:T(8,128)(2,1)S(1)} %get-tuple-element.71), channel_id=1, source_target_pairs={{0,2},{1,3},{2,0},{3,1},{4,6},{5,7},{6,4},{7,5},{8,10},{9,11},{10,... | collective-permute-start | bytes 688136 | tf_op jit(solution)/shard_map/ppermute | solution.py:28
  120.9 1.9 %collective-permute-start.22 = (bf16[32,3584]{1,0:T(8,128)(2,1)S(1)}, bf16[32,3584]{1,0:T(8,128)(2,1)S(1)}, u32[]{:S(2)}, u32[]{:S(2)}) collective-permute-start(bf16[32,3584]{1,0:T(8,128)(2,1)S(1)} %get-tuple-element.76), channel_id=1, source_target_pairs={{0,4},{1,5},{2,6},{3,7},{4,8},{5,9},{6,10},{7,11},{8,12},{9,13},{1... | collective-permute-start | bytes 688136 | tf_op jit(solution)/shard_map/ppermute | solution.py:28
  124.5 2.3 %collective-permute-done.21.refs_3_ = bf16[32,3584]{1,0:T(8,128)(2,1)S(1)} collective-permute-done((bf16[32,3584]{1,0:T(8,128)(2,1)S(1)}, bf16[32,3584]{1,0:T(8,128)(2,1)S(1)}, u32[]{:S(2)}, u32[]{:S(2)}) %collective-permute-start.21) | collective-permute-done | bytes 229408 | tf_op jit(solution)/shard_map/ppermute | solution.py:28
  126.8 3.8 %collective-permute-done.22.refs_4_ = bf16[32,3584]{1,0:T(8,128)(2,1)S(1)} collective-permute-done((bf16[32,3584]{1,0:T(8,128)(2,1)S(1)}, bf16[32,3584]{1,0:T(8,128)(2,1)S(1)}, u32[]{:S(2)}, u32[]{:S(2)}) %collective-permute-start.22) | collective-permute-done | bytes 229408 | tf_op jit(solution)/shard_map/ppermute | solution.py:28
  (53 shorter events, 14.9 us)
Async XLA Ops:
  0.6 84.6 %collective-permute-start.15 = (bf16[1024,7168]{1,0:T(8,128)(2,1)}, bf16[1024,7168]{1,0:T(8,128)(2,1)S(1)}, u32[]{:S(2)}, u32[]{:S(2)}) collective-permute-start(bf16[1024,7168]{1,0:T(8,128)(2,1)} %own_ref.3), channel_id=1, source_target_pairs={{0,1},{1,0},{2,3},{3,2},{4,5},{5,4},{6,7},{7,6},{8,9},{9,8},{10,11... | collective-permute-start | bytes 44040200 | tf_op jit(solution)/shard_map/ppermute | solution.py:28
  10.7 10.0 %collective-permute-start.2 = (bf16[16,16,512]{2,1,0:T(8,128)(2,1)S(1)}, bf16[16,16,512]{2,1,0:T(8,128)(2,1)S(1)}, u32[]{:S(2)}, u32[]{:S(2)}) collective-permute-start(bf16[16,16,512]{2,1,0:T(8,128)(2,1)S(1)} %get-tuple-element.46), channel_id=1, source_target_pairs={{0,4},{1,5},{2,6},{3,7},{4,8},{5,9},{6,10},{7,11},{8,12},{9,13},{1... | collective-permute-start | bytes 786440 | tf_op jit(solution)/shard_map/ppermute | solution.py:28
  12.1 13.6 %collective-permute-start.5 = (bf16[16,16,512]{2,1,0:T(8,128)(2,1)S(1)}, bf16[16,16,512]{2,1,0:T(8,128)(2,1)S(1)}, u32[]{:S(2)}, u32[]{:S(2)}) collective-permute-start(bf16[16,16,512]{2,1,0:T(8,128)(2,1)S(1)} %get-tuple-element.51), channel_id=1, source_target_pairs={{0,12},{1,13},{2,14},{3,15},{4,0},{5,1},{6,2},{7,3},{8,4},{9,5},{1... | collective-permute-start | bytes 786440 | tf_op jit(solution)/shard_map/ppermute | solution.py:28
  14.0 23.8 %collective-permute-start.8 = (bf16[16,16,512]{2,1,0:T(8,128)(2,1)S(1)}, bf16[16,16,512]{2,1,0:T(8,128)(2,1)S(1)}, u32[]{:S(2)}, u32[]{:S(2)}) collective-permute-start(bf16[16,16,512]{2,1,0:T(8,128)(2,1)S(1)} %get-tuple-element.56), channel_id=1, source_target_pairs={{0,2},{1,3},{2,0},{3,1},{4,6},{5,7},{6,4},{7,5},{8,10},{9,11},{10,... | collective-permute-start | bytes 786440 | tf_op jit(solution)/shard_map/ppermute | solution.py:28
  16.6 22.9 %collective-permute-start = (bf16[16,16,512]{2,1,0:T(8,128)(2,1)S(1)}, bf16[16,16,512]{2,1,0:T(8,128)(2,1)S(1)}, u32[]{:S(2)}, u32[]{:S(2)}) collective-permute-start(bf16[16,16,512]{2,1,0:T(8,128)(2,1)S(1)} %get-tuple-element.42), channel_id=1, source_target_pairs={{0,10},{1,11},{2,8},{3,9},{4,14},{5,15},{6,12},{7,13},{8,2},{9,3},... | collective-permute-start | bytes 786440 | tf_op jit(solution)/shard_map/ppermute | solution.py:28
  20.7 55.9 %collective-permute-start.14 = (bf16[8,512,128]{2,1,0:T(8,128)(2,1)S(1)}, bf16[8,512,128]{2,1,0:T(8,128)(2,1)S(1)}, u32[]{:S(2)}, u32[]{:S(2)}) collective-permute-start(bf16[8,512,128]{2,1,0:T(8,128)(2,1)S(1)} %copy-done), channel_id=1, source_target_pairs={{0,1},{1,0},{2,3},{3,2},{4,5},{5,4},{6,7},{7,6},{8,9},{9,8},{10,11... | collective-permute-start | bytes 3145736 | tf_op jit(solution)/shard_map/ppermute | solution.py:28
  25.7 23.2 %collective-permute-start.3 = (bf16[16,16,512]{2,1,0:T(8,128)(2,1)S(1)}, bf16[16,16,512]{2,1,0:T(8,128)(2,1)S(1)}, u32[]{:S(2)}, u32[]{:S(2)}) collective-permute-start(bf16[16,16,512]{2,1,0:T(8,128)(2,1)S(1)} %get-tuple-element.47), channel_id=1, source_target_pairs={{0,6},{1,7},{2,4},{3,5},{4,10},{5,11},{6,8},{7,9},{8,14},{9,15},{1... | collective-permute-start | bytes 786440 | tf_op jit(solution)/shard_map/ppermute | solution.py:28
  37.8 11.7 %collective-permute-start.6 = (bf16[16,16,512]{2,1,0:T(8,128)(2,1)S(1)}, bf16[16,16,512]{2,1,0:T(8,128)(2,1)S(1)}, u32[]{:S(2)}, u32[]{:S(2)}) collective-permute-start(bf16[16,16,512]{2,1,0:T(8,128)(2,1)S(1)} %get-tuple-element.52), channel_id=1, source_target_pairs={{0,14},{1,15},{2,12},{3,13},{4,2},{5,3},{6,0},{7,1},{8,6},{9,7},{1... | collective-permute-start | bytes 786440 | tf_op jit(solution)/shard_map/ppermute | solution.py:28
  39.5 12.7 %collective-permute-start.9 = (bf16[16,16,512]{2,1,0:T(8,128)(2,1)S(1)}, bf16[16,16,512]{2,1,0:T(8,128)(2,1)S(1)}, u32[]{:S(2)}, u32[]{:S(2)}) collective-permute-start(bf16[16,16,512]{2,1,0:T(8,128)(2,1)S(1)} %get-tuple-element.57), channel_id=1, source_target_pairs={{0,8},{1,9},{2,10},{3,11},{4,12},{5,13},{6,14},{7,15},{8,0},{9,1},... | collective-permute-start | bytes 786440 | tf_op jit(solution)/shard_map/ppermute | solution.py:28
  48.9 10.6 %collective-permute-start.1 = (bf16[16,16,512]{2,1,0:T(8,128)(2,1)S(1)}, bf16[16,16,512]{2,1,0:T(8,128)(2,1)S(1)}, u32[]{:S(2)}, u32[]{:S(2)}) collective-permute-start(bf16[16,16,512]{2,1,0:T(8,128)(2,1)S(1)} %get-tuple-element.43), channel_id=1, source_target_pairs={{0,4},{1,5},{2,6},{3,7},{4,8},{5,9},{6,10},{7,11},{8,12},{9,13},{1... | collective-permute-start | bytes 786440 | tf_op jit(solution)/shard_map/ppermute | solution.py:28
  49.5 10.7 %collective-permute-start.4 = (bf16[16,16,512]{2,1,0:T(8,128)(2,1)S(1)}, bf16[16,16,512]{2,1,0:T(8,128)(2,1)S(1)}, u32[]{:S(2)}, u32[]{:S(2)}) collective-permute-start(bf16[16,16,512]{2,1,0:T(8,128)(2,1)S(1)} %get-tuple-element.48), channel_id=1, source_target_pairs={{0,12},{1,13},{2,14},{3,15},{4,0},{5,1},{6,2},{7,3},{8,4},{9,5},{1... | collective-permute-start | bytes 786440 | tf_op jit(solution)/shard_map/ppermute | solution.py:28
  52.2 20.0 %collective-permute-start.7 = (bf16[16,16,512]{2,1,0:T(8,128)(2,1)S(1)}, bf16[16,16,512]{2,1,0:T(8,128)(2,1)S(1)}, u32[]{:S(2)}, u32[]{:S(2)}) collective-permute-start(bf16[16,16,512]{2,1,0:T(8,128)(2,1)S(1)} %get-tuple-element.53), channel_id=1, source_target_pairs={{0,2},{1,3},{2,0},{3,1},{4,6},{5,7},{6,4},{7,5},{8,10},{9,11},{10,... | collective-permute-start | bytes 786440 | tf_op jit(solution)/shard_map/ppermute | solution.py:28
  59.5 19.0 %collective-permute-start.10 = (bf16[16,16,512]{2,1,0:T(8,128)(2,1)S(1)}, bf16[16,16,512]{2,1,0:T(8,128)(2,1)S(1)}, u32[]{:S(2)}, u32[]{:S(2)}) collective-permute-start(bf16[16,16,512]{2,1,0:T(8,128)(2,1)S(1)} %get-tuple-element.58), channel_id=1, source_target_pairs={{0,10},{1,11},{2,8},{3,9},{4,14},{5,15},{6,12},{7,13},{8,2},{9,3},... | collective-permute-start | bytes 786440 | tf_op jit(solution)/shard_map/ppermute | solution.py:28
  60.2 18.4 %collective-permute-start.11 = (bf16[16,16,512]{2,1,0:T(8,128)(2,1)S(1)}, bf16[16,16,512]{2,1,0:T(8,128)(2,1)S(1)}, u32[]{:S(2)}, u32[]{:S(2)}) collective-permute-start(bf16[16,16,512]{2,1,0:T(8,128)(2,1)S(1)} %get-tuple-element.60), channel_id=1, source_target_pairs={{0,6},{1,7},{2,4},{3,5},{4,10},{5,11},{6,8},{7,9},{8,14},{9,15},{1... | collective-permute-start | bytes 786440 | tf_op jit(solution)/shard_map/ppermute | solution.py:28
  72.3 8.9 %collective-permute-start.12 = (bf16[16,16,512]{2,1,0:T(8,128)(2,1)S(1)}, bf16[16,16,512]{2,1,0:T(8,128)(2,1)S(1)}, u32[]{:S(2)}, u32[]{:S(2)}) collective-permute-start(bf16[16,16,512]{2,1,0:T(8,128)(2,1)S(1)} %get-tuple-element.62), channel_id=1, source_target_pairs={{0,14},{1,15},{2,12},{3,13},{4,2},{5,3},{6,0},{7,1},{8,6},{9,7},{1... | collective-permute-start | bytes 786440 | tf_op jit(solution)/shard_map/ppermute | solution.py:28
  76.6 7.9 %collective-permute-start.13 = (bf16[16,16,512]{2,1,0:T(8,128)(2,1)S(1)}, bf16[16,16,512]{2,1,0:T(8,128)(2,1)S(1)}, u32[]{:S(2)}, u32[]{:S(2)}) collective-permute-start(bf16[16,16,512]{2,1,0:T(8,128)(2,1)S(1)} %get-tuple-element.64), channel_id=1, source_target_pairs={{0,8},{1,9},{2,10},{3,11},{4,12},{5,13},{6,14},{7,15},{8,0},{9,1},... | collective-permute-start | bytes 786440 | tf_op jit(solution)/shard_map/ppermute | solution.py:28
  89.7 30.8 %collective-permute-start.20 = (bf16[128,3584]{1,0:T(8,128)(2,1)S(1)}, bf16[128,3584]{1,0:T(8,128)(2,1)S(1)}, u32[]{:S(2)}, u32[]{:S(2)}) collective-permute-start(bf16[128,3584]{1,0:T(8,128)(2,1)S(1)} %get-tuple-element.73), channel_id=1, source_target_pairs={{0,2},{1,3},{2,0},{3,1},{4,6},{5,7},{6,4},{7,5},{8,10},{9,11},{10,... | collective-permute-start | bytes 2752520 | tf_op jit(solution)/shard_map/ppermute | solution.py:28
  94.8 12.1 %collective-permute-start.16 = (bf16[2,32,3584]{2,1,0:T(8,128)(2,1)S(1)}, bf16[2,32,3584]{2,1,0:T(8,128)(2,1)S(1)}, u32[]{:S(2)}, u32[]{:S(2)}) collective-permute-start(bf16[2,32,3584]{2,1,0:T(8,128)(2,1)S(1)} %get-tuple-element.67), channel_id=1, source_target_pairs={{0,12},{1,13},{2,14},{3,15},{4,0},{5,1},{6,2},{7,3},{8,4},{9,5},{1... | collective-permute-start | bytes 1376264 | tf_op jit(solution)/shard_map/ppermute | solution.py:28
  97.3 18.9 %collective-permute-start.17 = (bf16[2,32,3584]{2,1,0:T(8,128)(2,1)S(1)}, bf16[2,32,3584]{2,1,0:T(8,128)(2,1)S(1)}, u32[]{:S(2)}, u32[]{:S(2)}) collective-permute-start(bf16[2,32,3584]{2,1,0:T(8,128)(2,1)S(1)} %get-tuple-element.68), channel_id=1, source_target_pairs={{0,4},{1,5},{2,6},{3,7},{4,8},{5,9},{6,10},{7,11},{8,12},{9,13},{1... | collective-permute-start | bytes 1376264 | tf_op jit(solution)/shard_map/ppermute | solution.py:28
  97.3 18.9 %collective-permute-start.18 = (bf16[2,32,3584]{2,1,0:T(8,128)(2,1)S(1)}, bf16[2,32,3584]{2,1,0:T(8,128)(2,1)S(1)}, u32[]{:S(2)}, u32[]{:S(2)}) collective-permute-start(bf16[2,32,3584]{2,1,0:T(8,128)(2,1)S(1)} %get-tuple-element.69), channel_id=1, source_target_pairs={{0,8},{1,9},{2,10},{3,11},{4,12},{5,13},{6,14},{7,15},{8,0},{9,1},... | collective-permute-start | bytes 1376264 | tf_op jit(solution)/shard_map/ppermute | solution.py:28
  116.4 8.1 %collective-permute-start.19 = (bf16[32,3584]{1,0:T(8,128)(2,1)S(1)}, bf16[32,3584]{1,0:T(8,128)(2,1)S(1)}, u32[]{:S(2)}, u32[]{:S(2)}) collective-permute-start(bf16[32,3584]{1,0:T(8,128)(2,1)S(1)} %get-tuple-element.71), channel_id=1, source_target_pairs={{0,2},{1,3},{2,0},{3,1},{4,6},{5,7},{6,4},{7,5},{8,10},{9,11},{10,... | collective-permute-start | bytes 688136 | tf_op jit(solution)/shard_map/ppermute | solution.py:28
  120.7 6.1 %collective-permute-start.21 = (bf16[32,3584]{1,0:T(8,128)(2,1)S(1)}, bf16[32,3584]{1,0:T(8,128)(2,1)S(1)}, u32[]{:S(2)}, u32[]{:S(2)}) collective-permute-start(bf16[32,3584]{1,0:T(8,128)(2,1)S(1)} %get-tuple-element.75), channel_id=1, source_target_pairs={{0,12},{1,13},{2,14},{3,15},{4,0},{5,1},{6,2},{7,3},{8,4},{9,5},{1... | collective-permute-start | bytes 688136 | tf_op jit(solution)/shard_map/ppermute | solution.py:28
  120.9 9.7 %collective-permute-start.22 = (bf16[32,3584]{1,0:T(8,128)(2,1)S(1)}, bf16[32,3584]{1,0:T(8,128)(2,1)S(1)}, u32[]{:S(2)}, u32[]{:S(2)}) collective-permute-start(bf16[32,3584]{1,0:T(8,128)(2,1)S(1)} %get-tuple-element.76), channel_id=1, source_target_pairs={{0,4},{1,5},{2,6},{3,7},{4,8},{5,9},{6,10},{7,11},{8,12},{9,13},{1... | collective-permute-start | bytes 688136 | tf_op jit(solution)/shard_map/ppermute | solution.py:28
  122.8 7.8 %collective-permute-start.23 = (bf16[32,3584]{1,0:T(8,128)(2,1)S(1)}, bf16[32,3584]{1,0:T(8,128)(2,1)S(1)}, u32[]{:S(2)}, u32[]{:S(2)}) collective-permute-start(bf16[32,3584]{1,0:T(8,128)(2,1)S(1)} %get-tuple-element.77), channel_id=1, source_target_pairs={{0,8},{1,9},{2,10},{3,11},{4,12},{5,13},{6,14},{7,15},{8,0},{9,1},... | collective-permute-start | bytes 688136 | tf_op jit(solution)/shard_map/ppermute | solution.py:28
  (9 other events, 240.9 us)

commit v3 on v2

v3 whole, which is shorter than its diff:
```python
import functools

import jax
import jax.numpy as jnp
from jax import lax
from jax.experimental import pallas as pl
from jax.experimental.pallas import tpu as pltpu
from jax.sharding import PartitionSpec as P

softmax_scale = 0.1353
masked_score = -1e30
epsilon = 1e-06

N_X, N_Y, N_CORE = 4, 2, 2
STEP = 4
FLUSH = 16
STEPS = 2
WHOLE = pl.BlockSpec(memory_space=pltpu.VMEM)


def moved(array, dx=0, dy=0, dcore=0):
    pairs = []
    for t in range(N_X * N_Y * N_CORE):
        x, y, core = t // (N_Y * N_CORE), t // N_CORE % N_Y, t % N_CORE
        to = ((x + dx) % N_X * N_Y + (y ^ dy)) * N_CORE + (core ^ dcore)
        pairs.append((t, to))
    return lax.ppermute(array, "tp", pairs)


def attend_kernel(latent, len_ref, q_ref, c_ref, n_ref, *rest):
    outs, (stage, new_wide) = rest[:-2], rest[-2:]
    i = pl.program_id(0)
    heads, slots = q_ref.shape[2], c_ref.shape[2]
    rows = n_ref.shape[0]

    @pl.when(i == 0)
    def _():
        new_wide[...] = n_ref[...].astype(jnp.float32)

    def attend_to(seen):
        every = range(STEP)
        queries = [q_ref[j].T for j in every]
        keys = [c_ref[j, :, :seen] for j in every]
        news = [new_wide[pl.ds(i * STEP + j, 1), :] for j in every]
        scores = [
            jnp.dot(q, k, preferred_element_type=jnp.float32) * softmax_scale
            for q, k in zip(queries, keys)
        ]
        new_scores = [
            jnp.sum(q.astype(jnp.float32) * n, axis=1, keepdims=True) * softmax_scale
            for q, n in zip(queries, news)
        ]
        positions = lax.broadcasted_iota(jnp.int32, (1, seen), 1)
        masked = [
            jnp.where(positions < len_ref[i * STEP + j], scores[j], masked_score)
            for j in every
        ]
        maxima = [
            jnp.maximum(jnp.max(m, axis=1, keepdims=True), n) for m, n in zip(masked, new_scores)
        ]
        probs = [jnp.exp(m - top) for m, top in zip(masked, maxima)]
        new_probs = [jnp.exp(n - top) for n, top in zip(new_scores, maxima)]
        summed = [
            lax.dot_general(
                p.astype(jnp.bfloat16),
                k[:latent],
                (((1,), (1,)), ((), ())),
                preferred_element_type=jnp.float32,
            )
            for p, k in zip(probs, keys)
        ]
        inverse = [
            1.0 / (jnp.sum(p, axis=1, keepdims=True) + n) for p, n in zip(probs, new_probs)
        ]
        for j in every:
            new_low = new_probs[j].astype(jnp.bfloat16).astype(jnp.float32)
            attended = (summed[j] + new_low * news[j][:, :latent]) * inverse[j]
            for c in range(latent // 128):
                stage[c, pl.ds(i % (FLUSH // STEP) * STEP + j, heads, stride=FLUSH), :] = attended[
                    :, c * 128 : (c + 1) * 128
                ]

    longest = len_ref[i * STEP]
    for j in range(1, STEP):
        longest = jnp.maximum(longest, len_ref[i * STEP + j])
    for seen in range(128, slots + 1, 128):
        in_reach = (longest > seen - 128) & (longest <= seen)
        pl.when(in_reach)(functools.partial(attend_to, seen))

    def flush(begin):
        per = heads // (N_X * N_Y * N_CORE)
        t = lax.axis_index("tp")
        x, y, core = t // (N_Y * N_CORE), t // N_CORE % N_Y, t % N_CORE
        for dx in range(N_X):
            for dy in range(N_Y):
                chip = (x + dx) % N_X * N_Y + (y ^ dy)
                for out, to in ((outs[dx].at[dy], core), (outs[N_X + dy].at[dx], core ^ 1)):
                    at = pl.multiple_of((chip * N_CORE + to) * (per * FLUSH), per * FLUSH)
                    for c in range(latent // 128):
                        block = stage[c, pl.ds(at, per * FLUSH), :].reshape(per, FLUSH, 128)
                        out[:, begin : begin + FLUSH, c * 128 : (c + 1) * 128] = block.astype(
                            jnp.bfloat16
                        )

    for begin in range(0, rows, FLUSH):
        pl.when((i + 1) * STEP == begin + FLUSH)(functools.partial(flush, begin))


def attend(lengths, queries, cache, new, latent):
    rows, width, heads = queries.shape
    slots = cache.shape[2]
    block = (heads // (N_X * N_Y * N_CORE), rows, latent)
    shapes = [(N_Y, *block)] * N_X + [(N_X, *block)] * N_Y
    return pl.pallas_call(
        functools.partial(attend_kernel, latent),
        grid_spec=pltpu.PrefetchScalarGridSpec(
            num_scalar_prefetch=1,
            grid=(rows // STEP,),
            in_specs=[
                pl.BlockSpec((STEP, width, heads), lambda i, *_: (i, 0, 0)),
                pl.BlockSpec((STEP, width, slots), lambda i, *_: (i, 0, 0)),
                pl.BlockSpec((rows, width), lambda i, *_: (0, 0)),
            ],
            out_specs=[pl.BlockSpec(shape, lambda i, *_: (0, 0, 0, 0)) for shape in shapes],
            scratch_shapes=[
                pltpu.VMEM((latent // 128, heads * FLUSH, 128), jnp.float32),
                pltpu.VMEM((rows, width), jnp.float32),
            ],
        ),
        out_shape=[jax.ShapeDtypeStruct(shape, jnp.bfloat16) for shape in shapes],
        compiler_params=pltpu.CompilerParams(vmem_limit_bytes=18 << 20),
        cost_estimate=pl.CostEstimate(
            flops=8 * rows * heads * slots * (width + latent),
            bytes_accessed=2 * rows * (width * (slots + heads) + heads * latent),
            transcendentals=rows * heads * slots,
        ),
        name="attend",
    )(lengths, queries, cache, new)


def regroup_kernel(count, picks, *refs):
    ins, outs = refs[:count], refs[count:]
    for out, pick in zip(outs, picks):
        for to, (n, at) in enumerate(pick):
            out[to] = ins[n][at]


def regroup(arrays, picks):
    block = arrays[0].shape[1:]
    return pl.pallas_call(
        functools.partial(regroup_kernel, len(arrays), picks),
        in_specs=[WHOLE] * len(arrays),
        out_specs=[WHOLE] * len(picks),
        out_shape=[jax.ShapeDtypeStruct((len(p), *block), jnp.bfloat16) for p in picks],
        compiler_params=pltpu.CompilerParams(vmem_limit_bytes=8 << 20),
        name="regroup",
    )(*arrays)


def lift_kernel(count, picks, *refs):
    arrays, (own_up, other_up, values) = refs[:count], refs[count:]
    heads, _, depth = own_up.shape
    for s, up in enumerate((own_up, other_up)):
        for h in range(heads):
            rows = jnp.concatenate([arrays[n][at, h] for n, at in picks[s]], axis=0)
            lifted = jnp.dot(rows, up[h], preferred_element_type=jnp.float32)
            at = (s * heads + h) * depth
            values[:, at : at + depth] = lifted.astype(jnp.bfloat16)


def lift(arrays, picks, own_up, other_up):
    heads, latent, depth = own_up.shape
    rows = len(picks[0]) * arrays[0].shape[2]
    return pl.pallas_call(
        functools.partial(lift_kernel, len(arrays), picks),
        in_specs=[WHOLE] * (len(arrays) + 2),
        out_specs=WHOLE,
        out_shape=jax.ShapeDtypeStruct((rows, N_CORE * heads * depth), jnp.bfloat16),
        compiler_params=pltpu.CompilerParams(vmem_limit_bytes=10 << 20),
        cost_estimate=pl.CostEstimate(
            flops=4 * rows * heads * latent * depth,
            bytes_accessed=4 * rows * heads * latent,
            transcendentals=0,
        ),
        name="lift",
    )(*arrays, own_up, other_up)


def project_kernel(start, split, values, own_ref, other_ref, *outs):
    inner, width = own_ref.shape[0], outs[0].shape[-1]
    at = pl.ds(pl.multiple_of(start + pl.program_id(0) * width, 128), width)
    tile = jnp.dot(values[:, :inner], own_ref[:, at], preferred_element_type=jnp.float32)
    tile = tile + jnp.dot(values[:, inner:], other_ref[:, at], preferred_element_type=jnp.float32)
    tile = tile.astype(jnp.bfloat16)
    if split == "y":
        begin = 0
        for out in outs:
            out[...] = tile[begin : begin + out.shape[0]]
            begin += out.shape[0]
        return
    rows = tile.shape[0] // (N_X * N_Y)
    for dx, out in enumerate(outs):
        for dy in range(N_Y):
            begin = (dy * N_X + dx) * rows
            out[dy] = tile[begin : begin + rows]


def project(values, own, other, start, end, split):
    rows = values.shape[0]
    inner = own.shape[0]
    blocks, index = [(rows // 2,), (rows // 4,), (rows // 4,)], lambda i: (0, i)
    if split == "x":
        blocks, index = [(N_Y, rows // (N_X * N_Y))] * N_X, lambda i: (0, 0, i)
    own, other = (pltpu.with_memory_space_constraint(w, pltpu.VMEM) for w in (own, other))
    return pl.pallas_call(
        functools.partial(project_kernel, start, split),
        grid=(STEPS,),
        in_specs=[WHOLE] * 3,
        out_specs=[pl.BlockSpec((*b, (end - start) // STEPS), index) for b in blocks],
        out_shape=[jax.ShapeDtypeStruct((*b, end - start), jnp.bfloat16) for b in blocks],
        compiler_params=pltpu.CompilerParams(vmem_limit_bytes=18 << 20),
        cost_estimate=pl.CostEstimate(
            flops=4 * rows * inner * (end - start),
            bytes_accessed=2 * rows * (end - start),
            transcendentals=0,
        ),
        name="project",
    )(values, own, other)


def split_sum_kernel(a_ref, b_ref, c_ref, *outs):
    rows = outs[0].shape[0]
    for dx, out in enumerate(outs):
        ref, at = (b_ref, dx) if dx < N_X // 2 else (c_ref, dx - N_X // 2)
        low = ref[at * rows : (at + 1) * rows].astype(jnp.float32)
        out[...] = (a_ref[dx * rows : (dx + 1) * rows].astype(jnp.float32) + low).astype(
            jnp.bfloat16
        )


def split_sum(a, b, c):
    part = jax.ShapeDtypeStruct((a.shape[0] // N_X, a.shape[1]), jnp.bfloat16)
    return pl.pallas_call(
        split_sum_kernel,
        in_specs=[WHOLE] * 3,
        out_specs=[WHOLE] * N_X,
        out_shape=[part] * N_X,
        compiler_params=pltpu.CompilerParams(vmem_limit_bytes=8 << 20),
        name="split_sum",
    )(a, b, c)


def pair_sum_kernel(a, b, c, d, keep, send):
    for dy, out in enumerate((keep, send)):
        total = a[dy].astype(jnp.float32) + b[dy].astype(jnp.float32)
        total = total + c[dy].astype(jnp.float32) + d[dy].astype(jnp.float32)
        out[...] = total.astype(jnp.bfloat16)


def pair_sum(parts):
    out = jax.ShapeDtypeStruct(parts[0].shape[1:], jnp.bfloat16)
    return pl.pallas_call(
        pair_sum_kernel,
        in_specs=[WHOLE] * len(parts),
        out_specs=[WHOLE] * 2,
        out_shape=[out] * 2,
        compiler_params=pltpu.CompilerParams(vmem_limit_bytes=8 << 20),
        name="pair_sum",
    )(*parts)


def finish_kernel(count, *refs):
    left, right, (residual, gain, hidden, normed) = refs[:2], refs[2:count], refs[count:]
    split = left[0].shape[1]
    squares = 0.0
    for parts, at in ((left, slice(0, split)), (right, slice(split, residual.shape[1]))):
        total = parts[0][...].astype(jnp.float32)
        for part in parts[1:]:
            total = total + part[...].astype(jnp.float32)
        low = (residual[:, at].astype(jnp.float32) + total).astype(jnp.bfloat16)
        hidden[:, at] = low
        wide = low.astype(jnp.float32)
        squares = squares + jnp.sum(wide * wide, axis=1, keepdims=True)
    factor = lax.rsqrt(squares / residual.shape[1] + epsilon)
    normed[...] = (
        hidden[...].astype(jnp.float32) * factor * gain[...].astype(jnp.float32)
    ).astype(jnp.bfloat16)


def finish(left, right, residual, gain):
    out = jax.ShapeDtypeStruct(residual.shape, jnp.bfloat16)
    count = len(left) + len(right)
    return pl.pallas_call(
        functools.partial(finish_kernel, count),
        in_specs=[WHOLE] * (count + 2),
        out_specs=[WHOLE] * 2,
        out_shape=[out] * 2,
        compiler_params=pltpu.CompilerParams(vmem_limit_bytes=8 << 20),
        name="finish",
    )(*left, *right, residual, gain.reshape(1, -1))


def per_device(queries, new_latent, latent_cache, lengths, residual, value_up, out_proj, norm_gain):
    latent = value_up.shape[1]
    width = out_proj.shape[1]
    flat_queries, flat_cache = (
        pltpu.with_memory_space_constraint(jnp.swapaxes(a, 1, 2), pltpu.HBM)
        for a in (queries, latent_cache)
    )
    new_latent = pltpu.with_memory_space_constraint(new_latent, pltpu.HBM)
    lengths = pltpu.with_memory_space_constraint(lengths, pltpu.HBM)
    other_proj = moved(out_proj, dcore=1)
    other_up = moved(value_up, dcore=1)
    blocks = list(attend(lengths, flat_queries, flat_cache, new_latent, latent))
    blocks[N_X - 1], _ = lax.optimization_barrier((blocks[N_X - 1], other_up))

    by_y = [blocks[N_X], moved(blocks[N_X + 1], dy=1)]
    by_x = [blocks[0]] + [moved(blocks[dx], dx=dx) for dx in range(1, N_X)]
    spread = regroup(by_y, [[(dy, dx) for dy in range(N_Y)] for dx in range(1, N_X)])
    spread = [moved(spread[dx - 1], dx=dx) for dx in range(1, N_X)]
    (crossed,) = regroup(by_x, [[(dx, 1) for dx in range(N_X)]])
    crossed = moved(crossed, dy=1)

    arrays = [*by_x, crossed, *by_y, *spread]
    own = [(dx, 0) for dx in range(N_X)] + [(N_X, dx) for dx in range(N_X)]
    other = []
    for dy in range(N_Y):
        other.append((N_X + 1 + dy, 0))
        other += [(N_X + 1 + N_Y + dx - 1, dy) for dx in range(1, N_X)]
    values = lift(arrays, (own, other), value_up, other_up)

    split = width * 4 // 7
    sums = project(values, out_proj, other_proj, 0, split, "x")
    left = [sums[0]] + [moved(sums[dx], dx=-dx) for dx in (1, 3, 2)]
    values, _ = lax.optimization_barrier((values, sums[0]))
    keep, *send = project(values, out_proj, other_proj, split, width, "y")
    right = split_sum(keep, *(moved(s, dy=1) for s in send))
    right = [right[0]] + [moved(right[dx], dx=-dx) for dx in (1, 3, 2)]
    mine, others = pair_sum(left)
    return tuple(finish([mine, moved(others, dy=1)], right, residual, norm_gain))


def solution(mesh):
    return jax.shard_map(
        per_device,
        mesh=mesh,
        in_specs=(
            P(("dp", "tp"), None, None),
            P(("dp", "tp"), None),
            P(("dp", "tp"), None, None),
            P(("dp", "tp")),
            P(("dp", "tp"), None),
            P("tp", None, None),
            P("tp", None),
            P(),
        ),
        out_specs=(P(("dp", "tp"), None), P(("dp", "tp"), None)),
        check_vma=False,
    )
```

time: 134 us -> 125 us (0.933)
  starting transfers between devices: 33.2 us -> 29.9 us
  waiting for transfers between devices: 66.7 us -> 64.9 us
  Pallas kernels: 29.7 us -> 28.2 us
  local copies, waits for them, and re-layouts: 1.54 us -> 0.04 us
    ppermute x24 -> x19, starting transfers between devices: 33.2 us -> 29.9 us  [moved(): return lax.ppermute(array, 'tp', pairs)]
    ppermute x24 -> x19, waiting for transfers between devices: 66.7 us -> 64.9 us  [moved(): return lax.ppermute(array, 'tp', pairs)]
    unnamed x18 -> x14, local copies, waits for them, and re-layouts: 1.53 us -> 0.03 us
    pallas_call x7, Pallas kernels: 28.1 us -> 26.7 us  [the longest x1 16.6 us: attend(): pl.pallas_call(functools.partial(attend_kernel, latent), grid_spec=pltpu....]
  transfers between devices with their start and end apart: 24 -> 19, of which waited for: 12 -> 9; matrix products, arithmetic and copies ran while one was open for 0% -> 0% of each run, Pallas kernels for 18% -> 18%
where the time goes in v3:
time: 125 us; the launch traced here: 124 us
  waiting for transfers between devices  64.9 us (52%)
  starting transfers between devices  29.9 us (24%)
  Pallas kernels  28.2 us (23%)
    ppermute x19, waiting for transfers between devices, moved(): return lax.ppermute(array, 'tp', pairs)  64.9 us
    ppermute x19, starting transfers between devices, moved(): return lax.ppermute(array, 'tp', pairs)  29.9 us
    pallas_call x1, Pallas kernels, attend(): pl.pallas_call(functools.partial(attend_kernel, latent), grid_spec=pltpu....  16.6 us
    pallas_call x2, Pallas kernels, project(): pl.pallas_call(functools.partial(project_kernel, start, split), grid=(STE...  8.52 us
  transfers between devices with their start and end apart: 19, of which 9 were waited for; matrix products, arithmetic and copies ran while one was open for 0% of the time, Pallas kernels for 18%

profile of v3, /device:TPU:72, one launch (start us, length us, event | category | flops | bytes accessed | tf_op | source)
XLA Modules:
  0.0 123.9 jit_solution(7795818383632832613)
XLA Ops:
  1.2 16.6 %attend.1 = (bf16[2,8,32,512]{3,2,1,0:T(8,128)(2,1)S(1)}, bf16[2,8,32,512]{3,2,1,0:T(8,128)(2,1)S(1)}, bf16[2,8,32,512]{3,2,1,0:T(8,128)(2,1)S(1)}, bf16[2,8,32,...) custom-call(s32[32]{0:T(128)} %len_ref.1, ...), custom_call_target="tpu_custom_call" | custom-call | flops 13690208256 | bytes 23068672 | tf_op jit(solution)/shard_map/attend/pallas_call | solution.py:114
  17.9 1.6 %collective-permute-start = (bf16[2,8,32,512]{3,2,1,0:T(8,128)(2,1)S(1)}, bf16[2,8,32,512]{3,2,1,0:T(8,128)(2,1)S(1)}, u32[]{:S(2)}, u32[]{:S(2)}) collective-permute-start(bf16[2,8,32,512]{3,2,1,0:T(8,128)(2,1)S(1)} %get-tuple-element.27), channel_id=1, source_target_pairs={{0,4},{1,5},{2,6},{3,7},{4,8},{5,9},{6,10},{7,11},{8,12},{9,13},{1... | collective-permute-start | bytes 1572872 | tf_op jit(solution)/shard_map/ppermute | solution.py:27
  19.4 2.7 %collective-permute-start.1 = (bf16[2,8,32,512]{3,2,1,0:T(8,128)(2,1)S(1)}, bf16[2,8,32,512]{3,2,1,0:T(8,128)(2,1)S(1)}, u32[]{:S(2)}, u32[]{:S(2)}) collective-permute-start(bf16[2,8,32,512]{3,2,1,0:T(8,128)(2,1)S(1)} %get-tuple-element.28), channel_id=1, source_target_pairs={{0,8},{1,9},{2,10},{3,11},{4,12},{5,13},{6,14},{7,15},{8,0},{9,1},... | collective-permute-start | bytes 1572872 | tf_op jit(solution)/shard_map/ppermute | solution.py:27
  22.1 2.4 %collective-permute-start.5 = (bf16[4,8,32,512]{3,2,1,0:T(8,128)(2,1)S(1)}, bf16[4,8,32,512]{3,2,1,0:T(8,128)(2,1)S(1)}, u32[]{:S(2)}, u32[]{:S(2)}) collective-permute-start(bf16[4,8,32,512]{3,2,1,0:T(8,128)(2,1)S(1)} %get-tuple-element.32), channel_id=1, source_target_pairs={{0,2},{1,3},{2,0},{3,1},{4,6},{5,7},{6,4},{7,5},{8,10},{9,11},{10,... | collective-permute-start | bytes 3145736 | tf_op jit(solution)/shard_map/ppermute | solution.py:27
  24.6 2.8 %collective-permute-start.3 = (bf16[2,8,32,512]{3,2,1,0:T(8,128)(2,1)S(1)}, bf16[2,8,32,512]{3,2,1,0:T(8,128)(2,1)S(1)}, u32[]{:S(2)}, u32[]{:S(2)}) collective-permute-start(bf16[2,8,32,512]{3,2,1,0:T(8,128)(2,1)S(1)} %get-tuple-element.30), channel_id=1, source_target_pairs={{0,12},{1,13},{2,14},{3,15},{4,0},{5,1},{6,2},{7,3},{8,4},{9,5},{1... | collective-permute-start | bytes 1572872 | tf_op jit(solution)/shard_map/ppermute | solution.py:27
  27.3 5.5 %collective-permute-done.refs_1_ = bf16[2,8,32,512]{3,2,1,0:T(8,128)(2,1)S(1)} collective-permute-done((bf16[2,8,32,512]{3,2,1,0:T(8,128)(2,1)S(1)}, bf16[2,8,32,512]{3,2,1,0:T(8,128)(2,1)S(1)}, u32[]{:S(2)}, u32[]{:S(2)}) %collective-permute-start) | collective-permute-done | bytes 524320 | tf_op jit(solution)/shard_map/ppermute | solution.py:27
  32.9 12.3 %collective-permute-done.1.refs_2_ = bf16[2,8,32,512]{3,2,1,0:T(8,128)(2,1)S(1)} collective-permute-done((bf16[2,8,32,512]{3,2,1,0:T(8,128)(2,1)S(1)}, bf16[2,8,32,512]{3,2,1,0:T(8,128)(2,1)S(1)}, u32[]{:S(2)}, u32[]{:S(2)}) %collective-permute-start.1) | collective-permute-done | bytes 524320 | tf_op jit(solution)/shard_map/ppermute | solution.py:27
  45.2 2.5 %collective-permute-start.4 = (bf16[4,8,32,512]{3,2,1,0:T(8,128)(2,1)S(1)}, bf16[4,8,32,512]{3,2,1,0:T(8,128)(2,1)S(1)}, u32[]{:S(2)}, u32[]{:S(2)}) collective-permute-start(bf16[4,8,32,512]{3,2,1,0:T(8,128)(2,1)S(1)} %regroup.2), channel_id=1, source_target_pairs={{0,2},{1,3},{2,0},{3,1},{4,6},{5,7},{6,4},{7,5},{8,10},{9,11},{10,... | collective-permute-start | bytes 3145736 | tf_op jit(solution)/shard_map/ppermute | solution.py:27
  49.5 2.2 %collective-permute-start.7 = (bf16[2,8,32,512]{3,2,1,0:T(8,128)(2,1)S(1)}, bf16[2,8,32,512]{3,2,1,0:T(8,128)(2,1)S(1)}, u32[]{:S(2)}, u32[]{:S(2)}) collective-permute-start(bf16[2,8,32,512]{3,2,1,0:T(8,128)(2,1)S(1)} %get-tuple-element.34), channel_id=1, source_target_pairs={{0,8},{1,9},{2,10},{3,11},{4,12},{5,13},{6,14},{7,15},{8,0},{9,1},... | collective-permute-start | bytes 1572872 | tf_op jit(solution)/shard_map/ppermute | solution.py:27
  52.7 9.4 %collective-permute-done.6.refs_7_ = bf16[2,8,32,512]{3,2,1,0:T(8,128)(2,1)S(1)} collective-permute-done((bf16[2,8,32,512]{3,2,1,0:T(8,128)(2,1)S(1)}, bf16[2,8,32,512]{3,2,1,0:T(8,128)(2,1)S(1)}, u32[]{:S(2)}, u32[]{:S(2)}) %collective-permute-start.6) | collective-permute-done | bytes 524320 | tf_op jit(solution)/shard_map/ppermute | solution.py:27
  62.1 12.1 %collective-permute-done.7.refs_8_ = bf16[2,8,32,512]{3,2,1,0:T(8,128)(2,1)S(1)} collective-permute-done((bf16[2,8,32,512]{3,2,1,0:T(8,128)(2,1)S(1)}, bf16[2,8,32,512]{3,2,1,0:T(8,128)(2,1)S(1)}, u32[]{:S(2)}, u32[]{:S(2)}) %collective-permute-start.7) | collective-permute-done | bytes 524320 | tf_op jit(solution)/shard_map/ppermute | solution.py:27
  75.6 4.8 %project.2 = (bf16[2,32,4096]{2,1,0:T(8,128)(2,1)S(1)}, bf16[2,32,4096]{2,1,0:T(8,128)(2,1)S(1)}, bf16[2,32,4096]{2,1,0:T(8,128)(2,1)S(1)}, bf16[2,32,4096]{2,1,0:T(8,128)(2,1)S(1)}) custom-call(bf16[256,2048]{1,0:T(8,128)(2,1)S(1)} %lift.1.values, bf16[1024,7168]{1,0:T(8,128)(2,1)S(1)} %bitcast.3, bf16[1024,7168]{1,0:T(8,128)(2,1)S(1)} %collective-permute-done.9.other_ref), custom_call_target="tpu_custom_call" | custom-call | flops 4294967296 | bytes 2097152 | tf_op jit(solution)/shard_map/project/pallas_call | solution.py:215
  80.4 2.2 %collective-permute-start.10 = (bf16[2,32,4096]{2,1,0:T(8,128)(2,1)S(1)}, bf16[2,32,4096]{2,1,0:T(8,128)(2,1)S(1)}, u32[]{:S(2)}, u32[]{:S(2)}) collective-permute-start(bf16[2,32,4096]{2,1,0:T(8,128)(2,1)S(1)} %get-tuple-element.37), channel_id=1, source_target_pairs={{0,12},{1,13},{2,14},{3,15},{4,0},{5,1},{6,2},{7,3},{8,4},{9,5},{1... | collective-permute-start | bytes 1572872 | tf_op jit(solution)/shard_map/ppermute | solution.py:27
  82.6 2.1 %collective-permute-start.12 = (bf16[2,32,4096]{2,1,0:T(8,128)(2,1)S(1)}, bf16[2,32,4096]{2,1,0:T(8,128)(2,1)S(1)}, u32[]{:S(2)}, u32[]{:S(2)}) collective-permute-start(bf16[2,32,4096]{2,1,0:T(8,128)(2,1)S(1)} %get-tuple-element.39), channel_id=1, source_target_pairs={{0,8},{1,9},{2,10},{3,11},{4,12},{5,13},{6,14},{7,15},{8,0},{9,1},... | collective-permute-start | bytes 1572872 | tf_op jit(solution)/shard_map/ppermute | solution.py:27
  84.8 3.7 %project.3 = (bf16[128,3072]{1,0:T(8,128)(2,1)S(1)}, bf16[64,3072]{1,0:T(8,128)(2,1)S(1)}, bf16[64,3072]{1,0:T(8,128)(2,1)S(1)}) custom-call(bf16[256,2048]{1,0:T(8,128)(2,1)S(1)} %lift.1.values, bf16[1024,7168]{1,0:T(8,128)(2,1)S(1)} %bitcast.3, bf16[1024,7168]{1,0:T(8,128)(2,1)S(1)} %collective-permute-done.9.other_ref), custom_call_target="tpu_custom_call" | custom-call | flops 3221225472 | bytes 1572864 | tf_op jit(solution)/shard_map/project/pallas_call | solution.py:215
  88.5 2.1 %collective-permute-start.14 = (bf16[64,3072]{1,0:T(8,128)(2,1)S(1)}, bf16[64,3072]{1,0:T(8,128)(2,1)S(1)}, u32[]{:S(2)}, u32[]{:S(2)}) collective-permute-start(bf16[64,3072]{1,0:T(8,128)(2,1)S(1)} %get-tuple-element.44), channel_id=1, source_target_pairs={{0,2},{1,3},{2,0},{3,1},{4,6},{5,7},{6,4},{7,5},{8,10},{9,11},{10,... | collective-permute-start | bytes 1179656 | tf_op jit(solution)/shard_map/ppermute | solution.py:27
  90.6 1.5 %collective-permute-start.15 = (bf16[64,3072]{1,0:T(8,128)(2,1)S(1)}, bf16[64,3072]{1,0:T(8,128)(2,1)S(1)}, u32[]{:S(2)}, u32[]{:S(2)}) collective-permute-start(bf16[64,3072]{1,0:T(8,128)(2,1)S(1)} %get-tuple-element.45), channel_id=1, source_target_pairs={{0,2},{1,3},{2,0},{3,1},{4,6},{5,7},{6,4},{7,5},{8,10},{9,11},{10,... | collective-permute-start | bytes 1179656 | tf_op jit(solution)/shard_map/ppermute | solution.py:27
  92.1 13.1 %collective-permute-done.10.b = bf16[2,32,4096]{2,1,0:T(8,128)(2,1)S(1)} collective-permute-done((bf16[2,32,4096]{2,1,0:T(8,128)(2,1)S(1)}, bf16[2,32,4096]{2,1,0:T(8,128)(2,1)S(1)}, u32[]{:S(2)}, u32[]{:S(2)}) %collective-permute-start.10) | collective-permute-done | bytes 524320 | tf_op jit(solution)/shard_map/ppermute | solution.py:27
  105.2 3.4 %collective-permute-done.11.c = bf16[2,32,4096]{2,1,0:T(8,128)(2,1)S(1)} collective-permute-done((bf16[2,32,4096]{2,1,0:T(8,128)(2,1)S(1)}, bf16[2,32,4096]{2,1,0:T(8,128)(2,1)S(1)}, u32[]{:S(2)}, u32[]{:S(2)}) %collective-permute-start.11) | collective-permute-done | bytes 524320 | tf_op jit(solution)/shard_map/ppermute | solution.py:27
  108.9 2.3 %collective-permute-start.13 = (bf16[32,4096]{1,0:T(8,128)(2,1)S(1)}, bf16[32,4096]{1,0:T(8,128)(2,1)S(1)}, u32[]{:S(2)}, u32[]{:S(2)}) collective-permute-start(bf16[32,4096]{1,0:T(8,128)(2,1)S(1)} %get-tuple-element.41), channel_id=1, source_target_pairs={{0,2},{1,3},{2,0},{3,1},{4,6},{5,7},{6,4},{7,5},{8,10},{9,11},{10,... | collective-permute-start | bytes 786440 | tf_op jit(solution)/shard_map/ppermute | solution.py:27
  111.8 1.7 %collective-permute-start.17 = (bf16[32,3072]{1,0:T(8,128)(2,1)S(1)}, bf16[32,3072]{1,0:T(8,128)(2,1)S(1)}, u32[]{:S(2)}, u32[]{:S(2)}) collective-permute-start(bf16[32,3072]{1,0:T(8,128)(2,1)S(1)} %get-tuple-element.48), channel_id=1, source_target_pairs={{0,4},{1,5},{2,6},{3,7},{4,8},{5,9},{6,10},{7,11},{8,12},{9,13},{1... | collective-permute-start | bytes 589832 | tf_op jit(solution)/shard_map/ppermute | solution.py:27
  114.1 4.9 %collective-permute-done.16.refs_3_ = bf16[32,3072]{1,0:T(8,128)(2,1)S(1)} collective-permute-done((bf16[32,3072]{1,0:T(8,128)(2,1)S(1)}, bf16[32,3072]{1,0:T(8,128)(2,1)S(1)}, u32[]{:S(2)}, u32[]{:S(2)}) %collective-permute-start.16) | collective-permute-done | bytes 196640 | tf_op jit(solution)/shard_map/ppermute | solution.py:27
  119.0 3.6 %collective-permute-done.17.refs_4_ = bf16[32,3072]{1,0:T(8,128)(2,1)S(1)} collective-permute-done((bf16[32,3072]{1,0:T(8,128)(2,1)S(1)}, bf16[32,3072]{1,0:T(8,128)(2,1)S(1)}, u32[]{:S(2)}, u32[]{:S(2)}) %collective-permute-start.17) | collective-permute-done | bytes 196640 | tf_op jit(solution)/shard_map/ppermute | solution.py:27
  122.6 1.3 %finish.1 = (bf16[32,7168]{1,0:T(8,128)(2,1)}, bf16[32,7168]{1,0:T(8,128)(2,1)}) custom-call(bf16[32,4096]{1,0:T(8,128)(2,1)S(1)} %get-tuple-element.40.refs_0_, bf16[32,4096]{1,0:T(8,128)(2,1)S(1)} %collective-permute-done.13.refs_1_, bf16[32,3072]{1,0:T(8,128)(2,1)S(1)} %get-tuple-element.46.refs_2_, bf16[32,3072]{1,0:T(8,128)(2,1)S(1)} %collective-permute-done.16.refs_3_, ...), custom_call_target="tpu_custom_call" | custom-call | tf_op jit(solution)/shard_map/finish/pallas_call | solution.py:293
  (39 shorter events, 6.2 us)
Async XLA Ops:
  0.6 74.9 %collective-permute-start.9 = (bf16[1024,7168]{1,0:T(8,128)(2,1)}, bf16[1024,7168]{1,0:T(8,128)(2,1)S(1)}, u32[]{:S(2)}, u32[]{:S(2)}) collective-permute-start(bf16[1024,7168]{1,0:T(8,128)(2,1)} %own_ref.3), channel_id=1, source_target_pairs={{0,1},{1,0},{2,3},{3,2},{4,5},{5,4},{6,7},{7,6},{8,9},{9,8},{10,11... | collective-permute-start | bytes 44040200 | tf_op jit(solution)/shard_map/ppermute | solution.py:27
  0.7 23.9 %collective-permute-start.2 = (bf16[8,512,128]{2,1,0:T(8,128)(2,1)}, bf16[8,512,128]{2,1,0:T(8,128)(2,1)S(1)}, u32[]{:S(2)}, u32[]{:S(2)}) collective-permute-start(bf16[8,512,128]{2,1,0:T(8,128)(2,1)} %refs_10_.1), channel_id=1, source_target_pairs={{0,1},{1,0},{2,3},{3,2},{4,5},{5,4},{6,7},{7,6},{8,9},{9,8},{10,11... | collective-permute-start | bytes 3145736 | tf_op jit(solution)/shard_map/ppermute | solution.py:27
  1.2 74.3 %slice-start = ((s8[14680064]{0:T(1024)(128)(4,1)}), s8[4194304]{0:T(1024)(128)(4,1)S(1)}, s32[]{:S(2)}) async-start(s8[14680064]{0:T(1024)(128)(4,1)} %bitcast.2), calls=%async_computation | async-start | bytes 8388608
  1.2 73.1 %copy-start = (bf16[8,512,128]{2,1,0:T(8,128)(2,1)S(1)}, bf16[8,512,128]{2,1,0:T(8,128)(2,1)}, u32[]{:S(2)}) copy-start(bf16[8,512,128]{2,1,0:T(8,128)(2,1)} %refs_10_.1) | copy-start | bytes 3145732
  1.2 74.3 %slice-start.1 = ((s8[14680064]{0:T(1024)(128)(4,1)}), s8[4194304]{0:T(1024)(128)(4,1)S(1)}, s32[]{:S(2)}) async-start(s8[14680064]{0:T(1024)(128)(4,1)} %bitcast.2), calls=%async_computation.1 | async-start | bytes 8388608
  1.2 74.3 %slice-start.2 = ((s8[14680064]{0:T(1024)(128)(4,1)}), s8[4194304]{0:T(1024)(128)(4,1)S(1)}, s32[]{:S(2)}) async-start(s8[14680064]{0:T(1024)(128)(4,1)} %bitcast.2), calls=%async_computation.2 | async-start | bytes 8388608
  1.2 74.3 %slice-start.3 = ((s8[14680064]{0:T(1024)(128)(4,1)}), s8[2097152]{0:T(1024)(128)(4,1)S(1)}, s32[]{:S(2)}) async-start(s8[14680064]{0:T(1024)(128)(4,1)} %bitcast.2), calls=%async_computation.3 | async-start | bytes 4194304
  17.9 15.0 %collective-permute-start = (bf16[2,8,32,512]{3,2,1,0:T(8,128)(2,1)S(1)}, bf16[2,8,32,512]{3,2,1,0:T(8,128)(2,1)S(1)}, u32[]{:S(2)}, u32[]{:S(2)}) collective-permute-start(bf16[2,8,32,512]{3,2,1,0:T(8,128)(2,1)S(1)} %get-tuple-element.27), channel_id=1, source_target_pairs={{0,4},{1,5},{2,6},{3,7},{4,8},{5,9},{6,10},{7,11},{8,12},{9,13},{1... | collective-permute-start | bytes 1572872 | tf_op jit(solution)/shard_map/ppermute | solution.py:27
  19.4 25.7 %collective-permute-start.1 = (bf16[2,8,32,512]{3,2,1,0:T(8,128)(2,1)S(1)}, bf16[2,8,32,512]{3,2,1,0:T(8,128)(2,1)S(1)}, u32[]{:S(2)}, u32[]{:S(2)}) collective-permute-start(bf16[2,8,32,512]{3,2,1,0:T(8,128)(2,1)S(1)} %get-tuple-element.28), channel_id=1, source_target_pairs={{0,8},{1,9},{2,10},{3,11},{4,12},{5,13},{6,14},{7,15},{8,0},{9,1},... | collective-permute-start | bytes 1572872 | tf_op jit(solution)/shard_map/ppermute | solution.py:27
  22.1 26.0 %collective-permute-start.5 = (bf16[4,8,32,512]{3,2,1,0:T(8,128)(2,1)S(1)}, bf16[4,8,32,512]{3,2,1,0:T(8,128)(2,1)S(1)}, u32[]{:S(2)}, u32[]{:S(2)}) collective-permute-start(bf16[4,8,32,512]{3,2,1,0:T(8,128)(2,1)S(1)} %get-tuple-element.32), channel_id=1, source_target_pairs={{0,2},{1,3},{2,0},{3,1},{4,6},{5,7},{6,4},{7,5},{8,10},{9,11},{10,... | collective-permute-start | bytes 3145736 | tf_op jit(solution)/shard_map/ppermute | solution.py:27
  24.6 20.6 %collective-permute-start.3 = (bf16[2,8,32,512]{3,2,1,0:T(8,128)(2,1)S(1)}, bf16[2,8,32,512]{3,2,1,0:T(8,128)(2,1)S(1)}, u32[]{:S(2)}, u32[]{:S(2)}) collective-permute-start(bf16[2,8,32,512]{3,2,1,0:T(8,128)(2,1)S(1)} %get-tuple-element.30), channel_id=1, source_target_pairs={{0,12},{1,13},{2,14},{3,15},{4,0},{5,1},{6,2},{7,3},{8,4},{9,5},{1... | collective-permute-start | bytes 1572872 | tf_op jit(solution)/shard_map/ppermute | solution.py:27
  45.2 29.1 %collective-permute-start.4 = (bf16[4,8,32,512]{3,2,1,0:T(8,128)(2,1)S(1)}, bf16[4,8,32,512]{3,2,1,0:T(8,128)(2,1)S(1)}, u32[]{:S(2)}, u32[]{:S(2)}) collective-permute-start(bf16[4,8,32,512]{3,2,1,0:T(8,128)(2,1)S(1)} %regroup.2), channel_id=1, source_target_pairs={{0,2},{1,3},{2,0},{3,1},{4,6},{5,7},{6,4},{7,5},{8,10},{9,11},{10,... | collective-permute-start | bytes 3145736 | tf_op jit(solution)/shard_map/ppermute | solution.py:27
  48.2 13.9 %collective-permute-start.6 = (bf16[2,8,32,512]{3,2,1,0:T(8,128)(2,1)S(1)}, bf16[2,8,32,512]{3,2,1,0:T(8,128)(2,1)S(1)}, u32[]{:S(2)}, u32[]{:S(2)}) collective-permute-start(bf16[2,8,32,512]{3,2,1,0:T(8,128)(2,1)S(1)} %get-tuple-element.33), channel_id=1, source_target_pairs={{0,4},{1,5},{2,6},{3,7},{4,8},{5,9},{6,10},{7,11},{8,12},{9,13},{1... | collective-permute-start | bytes 1572872 | tf_op jit(solution)/shard_map/ppermute | solution.py:27
  49.5 24.8 %collective-permute-start.7 = (bf16[2,8,32,512]{3,2,1,0:T(8,128)(2,1)S(1)}, bf16[2,8,32,512]{3,2,1,0:T(8,128)(2,1)S(1)}, u32[]{:S(2)}, u32[]{:S(2)}) collective-permute-start(bf16[2,8,32,512]{3,2,1,0:T(8,128)(2,1)S(1)} %get-tuple-element.34), channel_id=1, source_target_pairs={{0,8},{1,9},{2,10},{3,11},{4,12},{5,13},{6,14},{7,15},{8,0},{9,1},... | collective-permute-start | bytes 1572872 | tf_op jit(solution)/shard_map/ppermute | solution.py:27
  51.7 22.6 %collective-permute-start.8 = (bf16[2,8,32,512]{3,2,1,0:T(8,128)(2,1)S(1)}, bf16[2,8,32,512]{3,2,1,0:T(8,128)(2,1)S(1)}, u32[]{:S(2)}, u32[]{:S(2)}) collective-permute-start(bf16[2,8,32,512]{3,2,1,0:T(8,128)(2,1)S(1)} %get-tuple-element.35), channel_id=1, source_target_pairs={{0,12},{1,13},{2,14},{3,15},{4,0},{5,1},{6,2},{7,3},{8,4},{9,5},{1... | collective-permute-start | bytes 1572872 | tf_op jit(solution)/shard_map/ppermute | solution.py:27
  80.4 24.8 %collective-permute-start.10 = (bf16[2,32,4096]{2,1,0:T(8,128)(2,1)S(1)}, bf16[2,32,4096]{2,1,0:T(8,128)(2,1)S(1)}, u32[]{:S(2)}, u32[]{:S(2)}) collective-permute-start(bf16[2,32,4096]{2,1,0:T(8,128)(2,1)S(1)} %get-tuple-element.37), channel_id=1, source_target_pairs={{0,12},{1,13},{2,14},{3,15},{4,0},{5,1},{6,2},{7,3},{8,4},{9,5},{1... | collective-permute-start | bytes 1572872 | tf_op jit(solution)/shard_map/ppermute | solution.py:27
  82.6 26.0 %collective-permute-start.11 = (bf16[2,32,4096]{2,1,0:T(8,128)(2,1)S(1)}, bf16[2,32,4096]{2,1,0:T(8,128)(2,1)S(1)}, u32[]{:S(2)}, u32[]{:S(2)}) collective-permute-start(bf16[2,32,4096]{2,1,0:T(8,128)(2,1)S(1)} %get-tuple-element.38), channel_id=1, source_target_pairs={{0,4},{1,5},{2,6},{3,7},{4,8},{5,9},{6,10},{7,11},{8,12},{9,13},{1... | collective-permute-start | bytes 1572872 | tf_op jit(solution)/shard_map/ppermute | solution.py:27
  82.6 26.0 %collective-permute-start.12 = (bf16[2,32,4096]{2,1,0:T(8,128)(2,1)S(1)}, bf16[2,32,4096]{2,1,0:T(8,128)(2,1)S(1)}, u32[]{:S(2)}, u32[]{:S(2)}) collective-permute-start(bf16[2,32,4096]{2,1,0:T(8,128)(2,1)S(1)} %get-tuple-element.39), channel_id=1, source_target_pairs={{0,8},{1,9},{2,10},{3,11},{4,12},{5,13},{6,14},{7,15},{8,0},{9,1},... | collective-permute-start | bytes 1572872 | tf_op jit(solution)/shard_map/ppermute | solution.py:27
  88.5 22.7 %collective-permute-start.14 = (bf16[64,3072]{1,0:T(8,128)(2,1)S(1)}, bf16[64,3072]{1,0:T(8,128)(2,1)S(1)}, u32[]{:S(2)}, u32[]{:S(2)}) collective-permute-start(bf16[64,3072]{1,0:T(8,128)(2,1)S(1)} %get-tuple-element.44), channel_id=1, source_target_pairs={{0,2},{1,3},{2,0},{3,1},{4,6},{5,7},{6,4},{7,5},{8,10},{9,11},{10,... | collective-permute-start | bytes 1179656 | tf_op jit(solution)/shard_map/ppermute | solution.py:27
  90.6 20.6 %collective-permute-start.15 = (bf16[64,3072]{1,0:T(8,128)(2,1)S(1)}, bf16[64,3072]{1,0:T(8,128)(2,1)S(1)}, u32[]{:S(2)}, u32[]{:S(2)}) collective-permute-start(bf16[64,3072]{1,0:T(8,128)(2,1)S(1)} %get-tuple-element.45), channel_id=1, source_target_pairs={{0,2},{1,3},{2,0},{3,1},{4,6},{5,7},{6,4},{7,5},{8,10},{9,11},{10,... | collective-permute-start | bytes 1179656 | tf_op jit(solution)/shard_map/ppermute | solution.py:27
  108.9 13.7 %collective-permute-start.13 = (bf16[32,4096]{1,0:T(8,128)(2,1)S(1)}, bf16[32,4096]{1,0:T(8,128)(2,1)S(1)}, u32[]{:S(2)}, u32[]{:S(2)}) collective-permute-start(bf16[32,4096]{1,0:T(8,128)(2,1)S(1)} %get-tuple-element.41), channel_id=1, source_target_pairs={{0,2},{1,3},{2,0},{3,1},{4,6},{5,7},{6,4},{7,5},{8,10},{9,11},{10,... | collective-permute-start | bytes 786440 | tf_op jit(solution)/shard_map/ppermute | solution.py:27
  111.4 7.6 %collective-permute-start.16 = (bf16[32,3072]{1,0:T(8,128)(2,1)S(1)}, bf16[32,3072]{1,0:T(8,128)(2,1)S(1)}, u32[]{:S(2)}, u32[]{:S(2)}) collective-permute-start(bf16[32,3072]{1,0:T(8,128)(2,1)S(1)} %get-tuple-element.47), channel_id=1, source_target_pairs={{0,12},{1,13},{2,14},{3,15},{4,0},{5,1},{6,2},{7,3},{8,4},{9,5},{1... | collective-permute-start | bytes 589832 | tf_op jit(solution)/shard_map/ppermute | solution.py:27
  111.8 10.8 %collective-permute-start.17 = (bf16[32,3072]{1,0:T(8,128)(2,1)S(1)}, bf16[32,3072]{1,0:T(8,128)(2,1)S(1)}, u32[]{:S(2)}, u32[]{:S(2)}) collective-permute-start(bf16[32,3072]{1,0:T(8,128)(2,1)S(1)} %get-tuple-element.48), channel_id=1, source_target_pairs={{0,4},{1,5},{2,6},{3,7},{4,8},{5,9},{6,10},{7,11},{8,12},{9,13},{1... | collective-permute-start | bytes 589832 | tf_op jit(solution)/shard_map/ppermute | solution.py:27
  113.5 9.1 %collective-permute-start.18 = (bf16[32,3072]{1,0:T(8,128)(2,1)S(1)}, bf16[32,3072]{1,0:T(8,128)(2,1)S(1)}, u32[]{:S(2)}, u32[]{:S(2)}) collective-permute-start(bf16[32,3072]{1,0:T(8,128)(2,1)S(1)} %get-tuple-element.49), channel_id=1, source_target_pairs={{0,8},{1,9},{2,10},{3,11},{4,12},{5,13},{6,14},{7,15},{8,0},{9,1},... | collective-permute-start | bytes 589832 | tf_op jit(solution)/shard_map/ppermute | solution.py:27
  (2 other events, 67.2 us)

commit v4 on v3

--- a/solution.py
+++ b/solution.py
@@ -312,7 +312,7 @@
     other_proj = moved(out_proj, dcore=1)
     other_up = moved(value_up, dcore=1)
     blocks = list(attend(lengths, flat_queries, flat_cache, new_latent, latent))
-    blocks[N_X - 1], _ = lax.optimization_barrier((blocks[N_X - 1], other_up))
+    blocks[2], _ = lax.optimization_barrier((blocks[2], other_up))
 
     by_y = [blocks[N_X], moved(blocks[N_X + 1], dy=1)]
     by_x = [blocks[0]] + [moved(blocks[dx], dx=dx) for dx in range(1, N_X)]

time: 125 us -> 124 us (level)
  starting transfers between devices: 29.9 us -> 27.5 us
  waiting for transfers between devices: 64.9 us -> 66.8 us
    ppermute x19, starting transfers between devices: 29.9 us -> 27.5 us  [moved(): return lax.ppermute(array, 'tp', pairs)]
    ppermute x19, waiting for transfers between devices: 64.9 us -> 66.8 us  [moved(): return lax.ppermute(array, 'tp', pairs)]
  transfers between devices with their start and end apart: 19 -> 19, of which waited for: 9 -> 10; matrix products, arithmetic and copies ran while one was open for 0% -> 0% of each run, Pallas kernels for 18% -> 18%
where the time goes in v4:
time: 124 us; the launch traced here: 123 us
  waiting for transfers between devices  66.8 us (54%)
  Pallas kernels  28.4 us (23%)
  starting transfers between devices  27.5 us (22%)
    ppermute x19, waiting for transfers between devices, moved(): return lax.ppermute(array, 'tp', pairs)  66.8 us
    ppermute x19, starting transfers between devices, moved(): return lax.ppermute(array, 'tp', pairs)  27.5 us
    pallas_call x1, Pallas kernels, attend(): pl.pallas_call(functools.partial(attend_kernel, latent), grid_spec=pltpu....  16.7 us
    pallas_call x2, Pallas kernels, project(): pl.pallas_call(functools.partial(project_kernel, start, split), grid=(STE...  8.52 us
  transfers between devices with their start and end apart: 19, of which 10 were waited for; matrix products, arithmetic and copies ran while one was open for 0% of the time, Pallas kernels for 18%

profile of v4, /device:TPU:72, one launch (start us, length us, event | category | flops | bytes accessed | tf_op | source)
XLA Modules:
  0.0 123.5 jit_solution(12079922258340056922)
XLA Ops:
  1.2 16.7 %attend.1 = (bf16[2,8,32,512]{3,2,1,0:T(8,128)(2,1)S(1)}, bf16[2,8,32,512]{3,2,1,0:T(8,128)(2,1)S(1)}, bf16[2,8,32,512]{3,2,1,0:T(8,128)(2,1)S(1)}, bf16[2,8,32,...) custom-call(s32[32]{0:T(128)} %len_ref.1, ...), custom_call_target="tpu_custom_call" | custom-call | flops 13690208256 | bytes 23068672 | tf_op jit(solution)/shard_map/attend/pallas_call | solution.py:114
  18.0 1.7 %collective-permute-start = (bf16[2,8,32,512]{3,2,1,0:T(8,128)(2,1)S(1)}, bf16[2,8,32,512]{3,2,1,0:T(8,128)(2,1)S(1)}, u32[]{:S(2)}, u32[]{:S(2)}) collective-permute-start(bf16[2,8,32,512]{3,2,1,0:T(8,128)(2,1)S(1)} %get-tuple-element.27), channel_id=1, source_target_pairs={{0,4},{1,5},{2,6},{3,7},{4,8},{5,9},{6,10},{7,11},{8,12},{9,13},{1... | collective-permute-start | bytes 1572872 | tf_op jit(solution)/shard_map/ppermute | solution.py:27
  19.7 1.6 %collective-permute-start.3 = (bf16[2,8,32,512]{3,2,1,0:T(8,128)(2,1)S(1)}, bf16[2,8,32,512]{3,2,1,0:T(8,128)(2,1)S(1)}, u32[]{:S(2)}, u32[]{:S(2)}) collective-permute-start(bf16[2,8,32,512]{3,2,1,0:T(8,128)(2,1)S(1)} %get-tuple-element.30), channel_id=1, source_target_pairs={{0,12},{1,13},{2,14},{3,15},{4,0},{5,1},{6,2},{7,3},{8,4},{9,5},{1... | collective-permute-start | bytes 1572872 | tf_op jit(solution)/shard_map/ppermute | solution.py:27
  21.3 2.5 %collective-permute-start.5 = (bf16[4,8,32,512]{3,2,1,0:T(8,128)(2,1)S(1)}, bf16[4,8,32,512]{3,2,1,0:T(8,128)(2,1)S(1)}, u32[]{:S(2)}, u32[]{:S(2)}) collective-permute-start(bf16[4,8,32,512]{3,2,1,0:T(8,128)(2,1)S(1)} %get-tuple-element.32), channel_id=1, source_target_pairs={{0,2},{1,3},{2,0},{3,1},{4,6},{5,7},{6,4},{7,5},{8,10},{9,11},{10,... | collective-permute-start | bytes 3145736 | tf_op jit(solution)/shard_map/ppermute | solution.py:27
  24.6 3.0 %collective-permute-start.2 = (bf16[2,8,32,512]{3,2,1,0:T(8,128)(2,1)S(1)}, bf16[2,8,32,512]{3,2,1,0:T(8,128)(2,1)S(1)}, u32[]{:S(2)}, u32[]{:S(2)}) collective-permute-start(bf16[2,8,32,512]{3,2,1,0:T(8,128)(2,1)S(1)} %get-tuple-element.29), channel_id=1, source_target_pairs={{0,8},{1,9},{2,10},{3,11},{4,12},{5,13},{6,14},{7,15},{8,0},{9,1},... | collective-permute-start | bytes 1572872 | tf_op jit(solution)/shard_map/ppermute | solution.py:27
  27.6 5.6 %collective-permute-done.refs_1_ = bf16[2,8,32,512]{3,2,1,0:T(8,128)(2,1)S(1)} collective-permute-done((bf16[2,8,32,512]{3,2,1,0:T(8,128)(2,1)S(1)}, bf16[2,8,32,512]{3,2,1,0:T(8,128)(2,1)S(1)}, u32[]{:S(2)}, u32[]{:S(2)}) %collective-permute-start) | collective-permute-done | bytes 524320 | tf_op jit(solution)/shard_map/ppermute | solution.py:27
  33.2 10.6 %collective-permute-done.3.refs_3_ = bf16[2,8,32,512]{3,2,1,0:T(8,128)(2,1)S(1)} collective-permute-done((bf16[2,8,32,512]{3,2,1,0:T(8,128)(2,1)S(1)}, bf16[2,8,32,512]{3,2,1,0:T(8,128)(2,1)S(1)}, u32[]{:S(2)}, u32[]{:S(2)}) %collective-permute-start.3) | collective-permute-done | bytes 524320 | tf_op jit(solution)/shard_map/ppermute | solution.py:27
  43.8 1.8 %collective-permute-done.2.refs_2_ = bf16[2,8,32,512]{3,2,1,0:T(8,128)(2,1)S(1)} collective-permute-done((bf16[2,8,32,512]{3,2,1,0:T(8,128)(2,1)S(1)}, bf16[2,8,32,512]{3,2,1,0:T(8,128)(2,1)S(1)}, u32[]{:S(2)}, u32[]{:S(2)}) %collective-permute-start.2) | collective-permute-done | bytes 524320 | tf_op jit(solution)/shard_map/ppermute | solution.py:27
  45.6 2.1 %collective-permute-start.4 = (bf16[4,8,32,512]{3,2,1,0:T(8,128)(2,1)S(1)}, bf16[4,8,32,512]{3,2,1,0:T(8,128)(2,1)S(1)}, u32[]{:S(2)}, u32[]{:S(2)}) collective-permute-start(bf16[4,8,32,512]{3,2,1,0:T(8,128)(2,1)S(1)} %regroup.2), channel_id=1, source_target_pairs={{0,2},{1,3},{2,0},{3,1},{4,6},{5,7},{6,4},{7,5},{8,10},{9,11},{10,... | collective-permute-start | bytes 3145736 | tf_op jit(solution)/shard_map/ppermute | solution.py:27
  49.1 2.2 %collective-permute-start.7 = (bf16[2,8,32,512]{3,2,1,0:T(8,128)(2,1)S(1)}, bf16[2,8,32,512]{3,2,1,0:T(8,128)(2,1)S(1)}, u32[]{:S(2)}, u32[]{:S(2)}) collective-permute-start(bf16[2,8,32,512]{3,2,1,0:T(8,128)(2,1)S(1)} %get-tuple-element.34), channel_id=1, source_target_pairs={{0,8},{1,9},{2,10},{3,11},{4,12},{5,13},{6,14},{7,15},{8,0},{9,1},... | collective-permute-start | bytes 1572872 | tf_op jit(solution)/shard_map/ppermute | solution.py:27
  51.8 21.8 %collective-permute-done.6.refs_7_ = bf16[2,8,32,512]{3,2,1,0:T(8,128)(2,1)S(1)} collective-permute-done((bf16[2,8,32,512]{3,2,1,0:T(8,128)(2,1)S(1)}, bf16[2,8,32,512]{3,2,1,0:T(8,128)(2,1)S(1)}, u32[]{:S(2)}, u32[]{:S(2)}) %collective-permute-start.6) | collective-permute-done | bytes 524320 | tf_op jit(solution)/shard_map/ppermute | solution.py:27
  75.5 4.8 %project.2 = (bf16[2,32,4096]{2,1,0:T(8,128)(2,1)S(1)}, bf16[2,32,4096]{2,1,0:T(8,128)(2,1)S(1)}, bf16[2,32,4096]{2,1,0:T(8,128)(2,1)S(1)}, bf16[2,32,4096]{2,1,0:T(8,128)(2,1)S(1)}) custom-call(bf16[256,2048]{1,0:T(8,128)(2,1)S(1)} %lift.1.values, bf16[1024,7168]{1,0:T(8,128)(2,1)S(1)} %bitcast.3, bf16[1024,7168]{1,0:T(8,128)(2,1)S(1)} %collective-permute-done.9.other_ref), custom_call_target="tpu_custom_call" | custom-call | flops 4294967296 | bytes 2097152 | tf_op jit(solution)/shard_map/project/pallas_call | solution.py:215
  80.4 2.7 %collective-permute-start.10 = (bf16[2,32,4096]{2,1,0:T(8,128)(2,1)S(1)}, bf16[2,32,4096]{2,1,0:T(8,128)(2,1)S(1)}, u32[]{:S(2)}, u32[]{:S(2)}) collective-permute-start(bf16[2,32,4096]{2,1,0:T(8,128)(2,1)S(1)} %get-tuple-element.37), channel_id=1, source_target_pairs={{0,12},{1,13},{2,14},{3,15},{4,0},{5,1},{6,2},{7,3},{8,4},{9,5},{1... | collective-permute-start | bytes 1572872 | tf_op jit(solution)/shard_map/ppermute | solution.py:27
  83.1 1.5 %collective-permute-start.12 = (bf16[2,32,4096]{2,1,0:T(8,128)(2,1)S(1)}, bf16[2,32,4096]{2,1,0:T(8,128)(2,1)S(1)}, u32[]{:S(2)}, u32[]{:S(2)}) collective-permute-start(bf16[2,32,4096]{2,1,0:T(8,128)(2,1)S(1)} %get-tuple-element.39), channel_id=1, source_target_pairs={{0,8},{1,9},{2,10},{3,11},{4,12},{5,13},{6,14},{7,15},{8,0},{9,1},... | collective-permute-start | bytes 1572872 | tf_op jit(solution)/shard_map/ppermute | solution.py:27
  84.6 3.7 %project.3 = (bf16[128,3072]{1,0:T(8,128)(2,1)S(1)}, bf16[64,3072]{1,0:T(8,128)(2,1)S(1)}, bf16[64,3072]{1,0:T(8,128)(2,1)S(1)}) custom-call(bf16[256,2048]{1,0:T(8,128)(2,1)S(1)} %lift.1.values, bf16[1024,7168]{1,0:T(8,128)(2,1)S(1)} %bitcast.3, bf16[1024,7168]{1,0:T(8,128)(2,1)S(1)} %collective-permute-done.9.other_ref), custom_call_target="tpu_custom_call" | custom-call | flops 3221225472 | bytes 1572864 | tf_op jit(solution)/shard_map/project/pallas_call | solution.py:215
  88.3 2.3 %collective-permute-start.14 = (bf16[64,3072]{1,0:T(8,128)(2,1)S(1)}, bf16[64,3072]{1,0:T(8,128)(2,1)S(1)}, u32[]{:S(2)}, u32[]{:S(2)}) collective-permute-start(bf16[64,3072]{1,0:T(8,128)(2,1)S(1)} %get-tuple-element.44), channel_id=1, source_target_pairs={{0,2},{1,3},{2,0},{3,1},{4,6},{5,7},{6,4},{7,5},{8,10},{9,11},{10,... | collective-permute-start | bytes 1179656 | tf_op jit(solution)/shard_map/ppermute | solution.py:27
  90.6 1.3 %collective-permute-start.15 = (bf16[64,3072]{1,0:T(8,128)(2,1)S(1)}, bf16[64,3072]{1,0:T(8,128)(2,1)S(1)}, u32[]{:S(2)}, u32[]{:S(2)}) collective-permute-start(bf16[64,3072]{1,0:T(8,128)(2,1)S(1)} %get-tuple-element.45), channel_id=1, source_target_pairs={{0,2},{1,3},{2,0},{3,1},{4,6},{5,7},{6,4},{7,5},{8,10},{9,11},{10,... | collective-permute-start | bytes 1179656 | tf_op jit(solution)/shard_map/ppermute | solution.py:27
  91.9 13.7 %collective-permute-done.10.b = bf16[2,32,4096]{2,1,0:T(8,128)(2,1)S(1)} collective-permute-done((bf16[2,32,4096]{2,1,0:T(8,128)(2,1)S(1)}, bf16[2,32,4096]{2,1,0:T(8,128)(2,1)S(1)}, u32[]{:S(2)}, u32[]{:S(2)}) %collective-permute-start.10) | collective-permute-done | bytes 524320 | tf_op jit(solution)/shard_map/ppermute | solution.py:27
  105.7 3.4 %collective-permute-done.11.c = bf16[2,32,4096]{2,1,0:T(8,128)(2,1)S(1)} collective-permute-done((bf16[2,32,4096]{2,1,0:T(8,128)(2,1)S(1)}, bf16[2,32,4096]{2,1,0:T(8,128)(2,1)S(1)}, u32[]{:S(2)}, u32[]{:S(2)}) %collective-permute-start.11) | collective-permute-done | bytes 524320 | tf_op jit(solution)/shard_map/ppermute | solution.py:27
  109.3 1.4 %collective-permute-start.13 = (bf16[32,4096]{1,0:T(8,128)(2,1)S(1)}, bf16[32,4096]{1,0:T(8,128)(2,1)S(1)}, u32[]{:S(2)}, u32[]{:S(2)}) collective-permute-start(bf16[32,4096]{1,0:T(8,128)(2,1)S(1)} %get-tuple-element.41), channel_id=1, source_target_pairs={{0,2},{1,3},{2,0},{3,1},{4,6},{5,7},{6,4},{7,5},{8,10},{9,11},{10,... | collective-permute-start | bytes 786440 | tf_op jit(solution)/shard_map/ppermute | solution.py:27
  111.3 1.7 %collective-permute-start.17 = (bf16[32,3072]{1,0:T(8,128)(2,1)S(1)}, bf16[32,3072]{1,0:T(8,128)(2,1)S(1)}, u32[]{:S(2)}, u32[]{:S(2)}) collective-permute-start(bf16[32,3072]{1,0:T(8,128)(2,1)S(1)} %get-tuple-element.48), channel_id=1, source_target_pairs={{0,4},{1,5},{2,6},{3,7},{4,8},{5,9},{6,10},{7,11},{8,12},{9,13},{1... | collective-permute-start | bytes 589832 | tf_op jit(solution)/shard_map/ppermute | solution.py:27
  113.7 4.9 %collective-permute-done.16.refs_3_ = bf16[32,3072]{1,0:T(8,128)(2,1)S(1)} collective-permute-done((bf16[32,3072]{1,0:T(8,128)(2,1)S(1)}, bf16[32,3072]{1,0:T(8,128)(2,1)S(1)}, u32[]{:S(2)}, u32[]{:S(2)}) %collective-permute-start.16) | collective-permute-done | bytes 196640 | tf_op jit(solution)/shard_map/ppermute | solution.py:27
  118.5 3.6 %collective-permute-done.17.refs_4_ = bf16[32,3072]{1,0:T(8,128)(2,1)S(1)} collective-permute-done((bf16[32,3072]{1,0:T(8,128)(2,1)S(1)}, bf16[32,3072]{1,0:T(8,128)(2,1)S(1)}, u32[]{:S(2)}, u32[]{:S(2)}) %collective-permute-start.17) | collective-permute-done | bytes 196640 | tf_op jit(solution)/shard_map/ppermute | solution.py:27
  122.2 1.3 %finish.1 = (bf16[32,7168]{1,0:T(8,128)(2,1)}, bf16[32,7168]{1,0:T(8,128)(2,1)}) custom-call(bf16[32,4096]{1,0:T(8,128)(2,1)S(1)} %get-tuple-element.40.refs_0_, bf16[32,4096]{1,0:T(8,128)(2,1)S(1)} %collective-permute-done.13.refs_1_, bf16[32,3072]{1,0:T(8,128)(2,1)S(1)} %get-tuple-element.46.refs_2_, bf16[32,3072]{1,0:T(8,128)(2,1)S(1)} %collective-permute-done.16.refs_3_, ...), custom_call_target="tpu_custom_call" | custom-call | tf_op jit(solution)/shard_map/finish/pallas_call | solution.py:293
  (39 shorter events, 6.6 us)
Async XLA Ops:
  0.6 74.9 %collective-permute-start.9 = (bf16[1024,7168]{1,0:T(8,128)(2,1)}, bf16[1024,7168]{1,0:T(8,128)(2,1)S(1)}, u32[]{:S(2)}, u32[]{:S(2)}) collective-permute-start(bf16[1024,7168]{1,0:T(8,128)(2,1)} %own_ref.3), channel_id=1, source_target_pairs={{0,1},{1,0},{2,3},{3,2},{4,5},{5,4},{6,7},{7,6},{8,9},{9,8},{10,11... | collective-permute-start | bytes 44040200 | tf_op jit(solution)/shard_map/ppermute | solution.py:27
  0.7 23.9 %collective-permute-start.1 = (bf16[8,512,128]{2,1,0:T(8,128)(2,1)}, bf16[8,512,128]{2,1,0:T(8,128)(2,1)S(1)}, u32[]{:S(2)}, u32[]{:S(2)}) collective-permute-start(bf16[8,512,128]{2,1,0:T(8,128)(2,1)} %refs_10_.1), channel_id=1, source_target_pairs={{0,1},{1,0},{2,3},{3,2},{4,5},{5,4},{6,7},{7,6},{8,9},{9,8},{10,11... | collective-permute-start | bytes 3145736 | tf_op jit(solution)/shard_map/ppermute | solution.py:27
  1.2 74.3 %slice-start = ((s8[14680064]{0:T(1024)(128)(4,1)}), s8[4194304]{0:T(1024)(128)(4,1)S(1)}, s32[]{:S(2)}) async-start(s8[14680064]{0:T(1024)(128)(4,1)} %bitcast.2), calls=%async_computation | async-start | bytes 8388608
  1.2 73.0 %copy-start = (bf16[8,512,128]{2,1,0:T(8,128)(2,1)S(1)}, bf16[8,512,128]{2,1,0:T(8,128)(2,1)}, u32[]{:S(2)}) copy-start(bf16[8,512,128]{2,1,0:T(8,128)(2,1)} %refs_10_.1) | copy-start | bytes 3145732
  1.2 74.3 %slice-start.1 = ((s8[14680064]{0:T(1024)(128)(4,1)}), s8[4194304]{0:T(1024)(128)(4,1)S(1)}, s32[]{:S(2)}) async-start(s8[14680064]{0:T(1024)(128)(4,1)} %bitcast.2), calls=%async_computation.1 | async-start | bytes 8388608
  1.2 74.3 %slice-start.2 = ((s8[14680064]{0:T(1024)(128)(4,1)}), s8[4194304]{0:T(1024)(128)(4,1)S(1)}, s32[]{:S(2)}) async-start(s8[14680064]{0:T(1024)(128)(4,1)} %bitcast.2), calls=%async_computation.2 | async-start | bytes 8388608
  1.2 74.3 %slice-start.3 = ((s8[14680064]{0:T(1024)(128)(4,1)}), s8[2097152]{0:T(1024)(128)(4,1)S(1)}, s32[]{:S(2)}) async-start(s8[14680064]{0:T(1024)(128)(4,1)} %bitcast.2), calls=%async_computation.3 | async-start | bytes 4194304
  18.0 15.2 %collective-permute-start = (bf16[2,8,32,512]{3,2,1,0:T(8,128)(2,1)S(1)}, bf16[2,8,32,512]{3,2,1,0:T(8,128)(2,1)S(1)}, u32[]{:S(2)}, u32[]{:S(2)}) collective-permute-start(bf16[2,8,32,512]{3,2,1,0:T(8,128)(2,1)S(1)} %get-tuple-element.27), channel_id=1, source_target_pairs={{0,4},{1,5},{2,6},{3,7},{4,8},{5,9},{6,10},{7,11},{8,12},{9,13},{1... | collective-permute-start | bytes 1572872 | tf_op jit(solution)/shard_map/ppermute | solution.py:27
  19.7 24.1 %collective-permute-start.3 = (bf16[2,8,32,512]{3,2,1,0:T(8,128)(2,1)S(1)}, bf16[2,8,32,512]{3,2,1,0:T(8,128)(2,1)S(1)}, u32[]{:S(2)}, u32[]{:S(2)}) collective-permute-start(bf16[2,8,32,512]{3,2,1,0:T(8,128)(2,1)S(1)} %get-tuple-element.30), channel_id=1, source_target_pairs={{0,12},{1,13},{2,14},{3,15},{4,0},{5,1},{6,2},{7,3},{8,4},{9,5},{1... | collective-permute-start | bytes 1572872 | tf_op jit(solution)/shard_map/ppermute | solution.py:27
  21.3 26.5 %collective-permute-start.5 = (bf16[4,8,32,512]{3,2,1,0:T(8,128)(2,1)S(1)}, bf16[4,8,32,512]{3,2,1,0:T(8,128)(2,1)S(1)}, u32[]{:S(2)}, u32[]{:S(2)}) collective-permute-start(bf16[4,8,32,512]{3,2,1,0:T(8,128)(2,1)S(1)} %get-tuple-element.32), channel_id=1, source_target_pairs={{0,2},{1,3},{2,0},{3,1},{4,6},{5,7},{6,4},{7,5},{8,10},{9,11},{10,... | collective-permute-start | bytes 3145736 | tf_op jit(solution)/shard_map/ppermute | solution.py:27
  24.6 21.0 %collective-permute-start.2 = (bf16[2,8,32,512]{3,2,1,0:T(8,128)(2,1)S(1)}, bf16[2,8,32,512]{3,2,1,0:T(8,128)(2,1)S(1)}, u32[]{:S(2)}, u32[]{:S(2)}) collective-permute-start(bf16[2,8,32,512]{3,2,1,0:T(8,128)(2,1)S(1)} %get-tuple-element.29), channel_id=1, source_target_pairs={{0,8},{1,9},{2,10},{3,11},{4,12},{5,13},{6,14},{7,15},{8,0},{9,1},... | collective-permute-start | bytes 1572872 | tf_op jit(solution)/shard_map/ppermute | solution.py:27
  45.6 28.6 %collective-permute-start.4 = (bf16[4,8,32,512]{3,2,1,0:T(8,128)(2,1)S(1)}, bf16[4,8,32,512]{3,2,1,0:T(8,128)(2,1)S(1)}, u32[]{:S(2)}, u32[]{:S(2)}) collective-permute-start(bf16[4,8,32,512]{3,2,1,0:T(8,128)(2,1)S(1)} %regroup.2), channel_id=1, source_target_pairs={{0,2},{1,3},{2,0},{3,1},{4,6},{5,7},{6,4},{7,5},{8,10},{9,11},{10,... | collective-permute-start | bytes 3145736 | tf_op jit(solution)/shard_map/ppermute | solution.py:27
  47.9 25.7 %collective-permute-start.6 = (bf16[2,8,32,512]{3,2,1,0:T(8,128)(2,1)S(1)}, bf16[2,8,32,512]{3,2,1,0:T(8,128)(2,1)S(1)}, u32[]{:S(2)}, u32[]{:S(2)}) collective-permute-start(bf16[2,8,32,512]{3,2,1,0:T(8,128)(2,1)S(1)} %get-tuple-element.33), channel_id=1, source_target_pairs={{0,4},{1,5},{2,6},{3,7},{4,8},{5,9},{6,10},{7,11},{8,12},{9,13},{1... | collective-permute-start | bytes 1572872 | tf_op jit(solution)/shard_map/ppermute | solution.py:27
  49.1 24.5 %collective-permute-start.7 = (bf16[2,8,32,512]{3,2,1,0:T(8,128)(2,1)S(1)}, bf16[2,8,32,512]{3,2,1,0:T(8,128)(2,1)S(1)}, u32[]{:S(2)}, u32[]{:S(2)}) collective-permute-start(bf16[2,8,32,512]{3,2,1,0:T(8,128)(2,1)S(1)} %get-tuple-element.34), channel_id=1, source_target_pairs={{0,8},{1,9},{2,10},{3,11},{4,12},{5,13},{6,14},{7,15},{8,0},{9,1},... | collective-permute-start | bytes 1572872 | tf_op jit(solution)/shard_map/ppermute | solution.py:27
  51.3 23.0 %collective-permute-start.8 = (bf16[2,8,32,512]{3,2,1,0:T(8,128)(2,1)S(1)}, bf16[2,8,32,512]{3,2,1,0:T(8,128)(2,1)S(1)}, u32[]{:S(2)}, u32[]{:S(2)}) collective-permute-start(bf16[2,8,32,512]{3,2,1,0:T(8,128)(2,1)S(1)} %get-tuple-element.35), channel_id=1, source_target_pairs={{0,12},{1,13},{2,14},{3,15},{4,0},{5,1},{6,2},{7,3},{8,4},{9,5},{1... | collective-permute-start | bytes 1572872 | tf_op jit(solution)/shard_map/ppermute | solution.py:27
  80.4 25.3 %collective-permute-start.10 = (bf16[2,32,4096]{2,1,0:T(8,128)(2,1)S(1)}, bf16[2,32,4096]{2,1,0:T(8,128)(2,1)S(1)}, u32[]{:S(2)}, u32[]{:S(2)}) collective-permute-start(bf16[2,32,4096]{2,1,0:T(8,128)(2,1)S(1)} %get-tuple-element.37), channel_id=1, source_target_pairs={{0,12},{1,13},{2,14},{3,15},{4,0},{5,1},{6,2},{7,3},{8,4},{9,5},{1... | collective-permute-start | bytes 1572872 | tf_op jit(solution)/shard_map/ppermute | solution.py:27
  83.1 26.0 %collective-permute-start.11 = (bf16[2,32,4096]{2,1,0:T(8,128)(2,1)S(1)}, bf16[2,32,4096]{2,1,0:T(8,128)(2,1)S(1)}, u32[]{:S(2)}, u32[]{:S(2)}) collective-permute-start(bf16[2,32,4096]{2,1,0:T(8,128)(2,1)S(1)} %get-tuple-element.38), channel_id=1, source_target_pairs={{0,4},{1,5},{2,6},{3,7},{4,8},{5,9},{6,10},{7,11},{8,12},{9,13},{1... | collective-permute-start | bytes 1572872 | tf_op jit(solution)/shard_map/ppermute | solution.py:27
  83.1 26.0 %collective-permute-start.12 = (bf16[2,32,4096]{2,1,0:T(8,128)(2,1)S(1)}, bf16[2,32,4096]{2,1,0:T(8,128)(2,1)S(1)}, u32[]{:S(2)}, u32[]{:S(2)}) collective-permute-start(bf16[2,32,4096]{2,1,0:T(8,128)(2,1)S(1)} %get-tuple-element.39), channel_id=1, source_target_pairs={{0,8},{1,9},{2,10},{3,11},{4,12},{5,13},{6,14},{7,15},{8,0},{9,1},... | collective-permute-start | bytes 1572872 | tf_op jit(solution)/shard_map/ppermute | solution.py:27
  88.3 22.5 %collective-permute-start.14 = (bf16[64,3072]{1,0:T(8,128)(2,1)S(1)}, bf16[64,3072]{1,0:T(8,128)(2,1)S(1)}, u32[]{:S(2)}, u32[]{:S(2)}) collective-permute-start(bf16[64,3072]{1,0:T(8,128)(2,1)S(1)} %get-tuple-element.44), channel_id=1, source_target_pairs={{0,2},{1,3},{2,0},{3,1},{4,6},{5,7},{6,4},{7,5},{8,10},{9,11},{10,... | collective-permute-start | bytes 1179656 | tf_op jit(solution)/shard_map/ppermute | solution.py:27
  90.6 20.2 %collective-permute-start.15 = (bf16[64,3072]{1,0:T(8,128)(2,1)S(1)}, bf16[64,3072]{1,0:T(8,128)(2,1)S(1)}, u32[]{:S(2)}, u32[]{:S(2)}) collective-permute-start(bf16[64,3072]{1,0:T(8,128)(2,1)S(1)} %get-tuple-element.45), channel_id=1, source_target_pairs={{0,2},{1,3},{2,0},{3,1},{4,6},{5,7},{6,4},{7,5},{8,10},{9,11},{10,... | collective-permute-start | bytes 1179656 | tf_op jit(solution)/shard_map/ppermute | solution.py:27
  109.3 12.8 %collective-permute-start.13 = (bf16[32,4096]{1,0:T(8,128)(2,1)S(1)}, bf16[32,4096]{1,0:T(8,128)(2,1)S(1)}, u32[]{:S(2)}, u32[]{:S(2)}) collective-permute-start(bf16[32,4096]{1,0:T(8,128)(2,1)S(1)} %get-tuple-element.41), channel_id=1, source_target_pairs={{0,2},{1,3},{2,0},{3,1},{4,6},{5,7},{6,4},{7,5},{8,10},{9,11},{10,... | collective-permute-start | bytes 786440 | tf_op jit(solution)/shard_map/ppermute | solution.py:27
  111.0 7.6 %collective-permute-start.16 = (bf16[32,3072]{1,0:T(8,128)(2,1)S(1)}, bf16[32,3072]{1,0:T(8,128)(2,1)S(1)}, u32[]{:S(2)}, u32[]{:S(2)}) collective-permute-start(bf16[32,3072]{1,0:T(8,128)(2,1)S(1)} %get-tuple-element.47), channel_id=1, source_target_pairs={{0,12},{1,13},{2,14},{3,15},{4,0},{5,1},{6,2},{7,3},{8,4},{9,5},{1... | collective-permute-start | bytes 589832 | tf_op jit(solution)/shard_map/ppermute | solution.py:27
  111.3 10.8 %collective-permute-start.17 = (bf16[32,3072]{1,0:T(8,128)(2,1)S(1)}, bf16[32,3072]{1,0:T(8,128)(2,1)S(1)}, u32[]{:S(2)}, u32[]{:S(2)}) collective-permute-start(bf16[32,3072]{1,0:T(8,128)(2,1)S(1)} %get-tuple-element.48), channel_id=1, source_target_pairs={{0,4},{1,5},{2,6},{3,7},{4,8},{5,9},{6,10},{7,11},{8,12},{9,13},{1... | collective-permute-start | bytes 589832 | tf_op jit(solution)/shard_map/ppermute | solution.py:27
  113.1 9.1 %collective-permute-start.18 = (bf16[32,3072]{1,0:T(8,128)(2,1)S(1)}, bf16[32,3072]{1,0:T(8,128)(2,1)S(1)}, u32[]{:S(2)}, u32[]{:S(2)}) collective-permute-start(bf16[32,3072]{1,0:T(8,128)(2,1)S(1)} %get-tuple-element.49), channel_id=1, source_target_pairs={{0,8},{1,9},{2,10},{3,11},{4,12},{5,13},{6,14},{7,15},{8,0},{9,1},... | collective-permute-start | bytes 589832 | tf_op jit(solution)/shard_map/ppermute | solution.py:27
  (2 other events, 66.6 us)

commit v5 on v4

--- a/solution.py
+++ b/solution.py
@@ -250,30 +250,40 @@
     )(a, b, c)
 
 
-def pair_sum_kernel(a, b, c, d, keep, send):
-    for dy, out in enumerate((keep, send)):
+def pair_sum_kernel(a, b, c, d, keep, *send):
+    for dy in range(N_Y):
         total = a[dy].astype(jnp.float32) + b[dy].astype(jnp.float32)
         total = total + c[dy].astype(jnp.float32) + d[dy].astype(jnp.float32)
-        out[...] = total.astype(jnp.bfloat16)
+        total = total.astype(jnp.bfloat16)
+        if dy == 0:
+            keep[...] = total
+            continue
+        width = send[0].shape[1]
+        for n, out in enumerate(send):
+            out[...] = total[:, n * width : (n + 1) * width]
 
 
 def pair_sum(parts):
-    out = jax.ShapeDtypeStruct(parts[0].shape[1:], jnp.bfloat16)
+    _, rows, width = parts[0].shape
+    outs = [jax.ShapeDtypeStruct((rows, w), jnp.bfloat16) for w in (width, width // 2, width // 2)]
     return pl.pallas_call(
         pair_sum_kernel,
         in_specs=[WHOLE] * len(parts),
-        out_specs=[WHOLE] * 2,
-        out_shape=[out] * 2,
+        out_specs=[WHOLE] * 3,
+        out_shape=outs,
         compiler_params=pltpu.CompilerParams(vmem_limit_bytes=8 << 20),
         name="pair_sum",
     )(*parts)
 
 
 def finish_kernel(count, *refs):
-    left, right, (residual, gain, hidden, normed) = refs[:2], refs[2:count], refs[count:]
-    split = left[0].shape[1]
+    (mine, *pieces), right, (residual, gain, hidden, normed) = refs[:3], refs[3:count], refs[count:]
+    split, width = mine.shape[1], pieces[0].shape[1]
+    columns = [slice(n * width, (n + 1) * width) for n in range(len(pieces))]
+    sums = [([mine.at[:, at], piece], at) for piece, at in zip(pieces, columns)]
+    sums.append((right, slice(split, residual.shape[1])))
     squares = 0.0
-    for parts, at in ((left, slice(0, split)), (right, slice(split, residual.shape[1]))):
+    for parts, at in sums:
         total = parts[0][...].astype(jnp.float32)
         for part in parts[1:]:
             total = total + part[...].astype(jnp.float32)
@@ -329,15 +339,16 @@
         other += [(N_X + 1 + N_Y + dx - 1, dy) for dx in range(1, N_X)]
     values = lift(arrays, (own, other), value_up, other_up)
 
-    split = width * 4 // 7
+    split = width * 17 // 28
     sums = project(values, out_proj, other_proj, 0, split, "x")
     left = [sums[0]] + [moved(sums[dx], dx=-dx) for dx in (1, 3, 2)]
     values, _ = lax.optimization_barrier((values, sums[0]))
     keep, *send = project(values, out_proj, other_proj, split, width, "y")
     right = split_sum(keep, *(moved(s, dy=1) for s in send))
     right = [right[0]] + [moved(right[dx], dx=-dx) for dx in (1, 3, 2)]
-    mine, others = pair_sum(left)
-    return tuple(finish([mine, moved(others, dy=1)], right, residual, norm_gain))
+    mine, *others = pair_sum(left)
+    left = [mine] + [moved(o, dy=1) for o in others]
+    return tuple(finish(left, right, residual, norm_gain))
 
 
 def solution(mesh):

time: 124 us -> 124 us (level)
  waiting for transfers between devices: 66.8 us -> 61.3 us
  starting transfers between devices: 27.5 us -> 31.7 us
    ppermute x19 -> x20, waiting for transfers between devices: 66.8 us -> 61.3 us  [moved(): return lax.ppermute(array, 'tp', pairs)]
    ppermute x19 -> x20, starting transfers between devices: 27.5 us -> 31.7 us  [moved(): return lax.ppermute(array, 'tp', pairs)]
  transfers between devices with their start and end apart: 19 -> 20, of which waited for: 10 -> 9; matrix products, arithmetic and copies ran while one was open for 0% -> 0% of each run, Pallas kernels for 18% -> 18%
where the time goes in v5:
time: 124 us; the launch traced here: 123 us
  waiting for transfers between devices  61.3 us (49%)
  starting transfers between devices  31.7 us (26%)
  Pallas kernels  29 us (23%)
    ppermute x20, waiting for transfers between devices, moved(): return lax.ppermute(array, 'tp', pairs)  61.3 us
    ppermute x20, starting transfers between devices, moved(): return lax.ppermute(array, 'tp', pairs)  31.7 us
    pallas_call x1, Pallas kernels, attend(): pl.pallas_call(functools.partial(attend_kernel, latent), grid_spec=pltpu....  16.6 us
    pallas_call x2, Pallas kernels, project(): pl.pallas_call(functools.partial(project_kernel, start, split), grid=(STE...  9.28 us
  transfers between devices with their start and end apart: 20, of which 9 were waited for; matrix products, arithmetic and copies ran while one was open for 0% of the time, Pallas kernels for 18%

profile of v5, /device:TPU:72, one launch (start us, length us, event | category | flops | bytes accessed | tf_op | source)
XLA Modules:
  0.0 122.9 jit_solution(16335001466347000718)
XLA Ops:
  1.2 16.6 %attend.1 = (bf16[2,8,32,512]{3,2,1,0:T(8,128)(2,1)S(1)}, bf16[2,8,32,512]{3,2,1,0:T(8,128)(2,1)S(1)}, bf16[2,8,32,512]{3,2,1,0:T(8,128)(2,1)S(1)}, bf16[2,8,32,...) custom-call(s32[32]{0:T(128)} %len_ref.1, ...), custom_call_target="tpu_custom_call" | custom-call | flops 13690208256 | bytes 23068672 | tf_op jit(solution)/shard_map/attend/pallas_call | solution.py:114
  17.9 1.7 %collective-permute-start = (bf16[2,8,32,512]{3,2,1,0:T(8,128)(2,1)S(1)}, bf16[2,8,32,512]{3,2,1,0:T(8,128)(2,1)S(1)}, u32[]{:S(2)}, u32[]{:S(2)}) collective-permute-start(bf16[2,8,32,512]{3,2,1,0:T(8,128)(2,1)S(1)} %get-tuple-element.28), channel_id=1, source_target_pairs={{0,4},{1,5},{2,6},{3,7},{4,8},{5,9},{6,10},{7,11},{8,12},{9,13},{1... | collective-permute-start | bytes 1572872 | tf_op jit(solution)/shard_map/ppermute | solution.py:27
  19.6 2.0 %collective-permute-start.5 = (bf16[4,8,32,512]{3,2,1,0:T(8,128)(2,1)S(1)}, bf16[4,8,32,512]{3,2,1,0:T(8,128)(2,1)S(1)}, u32[]{:S(2)}, u32[]{:S(2)}) collective-permute-start(bf16[4,8,32,512]{3,2,1,0:T(8,128)(2,1)S(1)} %get-tuple-element.33), channel_id=1, source_target_pairs={{0,2},{1,3},{2,0},{3,1},{4,6},{5,7},{6,4},{7,5},{8,10},{9,11},{10,... | collective-permute-start | bytes 3145736 | tf_op jit(solution)/shard_map/ppermute | solution.py:27
  21.6 1.7 %collective-permute-start.3 = (bf16[2,8,32,512]{3,2,1,0:T(8,128)(2,1)S(1)}, bf16[2,8,32,512]{3,2,1,0:T(8,128)(2,1)S(1)}, u32[]{:S(2)}, u32[]{:S(2)}) collective-permute-start(bf16[2,8,32,512]{3,2,1,0:T(8,128)(2,1)S(1)} %get-tuple-element.31), channel_id=1, source_target_pairs={{0,12},{1,13},{2,14},{3,15},{4,0},{5,1},{6,2},{7,3},{8,4},{9,5},{1... | collective-permute-start | bytes 1572872 | tf_op jit(solution)/shard_map/ppermute | solution.py:27
  24.6 3.0 %collective-permute-start.2 = (bf16[2,8,32,512]{3,2,1,0:T(8,128)(2,1)S(1)}, bf16[2,8,32,512]{3,2,1,0:T(8,128)(2,1)S(1)}, u32[]{:S(2)}, u32[]{:S(2)}) collective-permute-start(bf16[2,8,32,512]{3,2,1,0:T(8,128)(2,1)S(1)} %get-tuple-element.30), channel_id=1, source_target_pairs={{0,8},{1,9},{2,10},{3,11},{4,12},{5,13},{6,14},{7,15},{8,0},{9,1},... | collective-permute-start | bytes 1572872 | tf_op jit(solution)/shard_map/ppermute | solution.py:27
  27.6 5.6 %collective-permute-done.refs_1_ = bf16[2,8,32,512]{3,2,1,0:T(8,128)(2,1)S(1)} collective-permute-done((bf16[2,8,32,512]{3,2,1,0:T(8,128)(2,1)S(1)}, bf16[2,8,32,512]{3,2,1,0:T(8,128)(2,1)S(1)}, u32[]{:S(2)}, u32[]{:S(2)}) %collective-permute-start) | collective-permute-done | bytes 524320 | tf_op jit(solution)/shard_map/ppermute | solution.py:27
  33.2 12.7 %collective-permute-done.3.refs_3_ = bf16[2,8,32,512]{3,2,1,0:T(8,128)(2,1)S(1)} collective-permute-done((bf16[2,8,32,512]{3,2,1,0:T(8,128)(2,1)S(1)}, bf16[2,8,32,512]{3,2,1,0:T(8,128)(2,1)S(1)}, u32[]{:S(2)}, u32[]{:S(2)}) %collective-permute-start.3) | collective-permute-done | bytes 524320 | tf_op jit(solution)/shard_map/ppermute | solution.py:27
  45.9 2.1 %collective-permute-start.4 = (bf16[4,8,32,512]{3,2,1,0:T(8,128)(2,1)S(1)}, bf16[4,8,32,512]{3,2,1,0:T(8,128)(2,1)S(1)}, u32[]{:S(2)}, u32[]{:S(2)}) collective-permute-start(bf16[4,8,32,512]{3,2,1,0:T(8,128)(2,1)S(1)} %regroup.2), channel_id=1, source_target_pairs={{0,2},{1,3},{2,0},{3,1},{4,6},{5,7},{6,4},{7,5},{8,10},{9,11},{10,... | collective-permute-start | bytes 3145736 | tf_op jit(solution)/shard_map/ppermute | solution.py:27
  48.2 1.9 %collective-permute-start.6 = (bf16[2,8,32,512]{3,2,1,0:T(8,128)(2,1)S(1)}, bf16[2,8,32,512]{3,2,1,0:T(8,128)(2,1)S(1)}, u32[]{:S(2)}, u32[]{:S(2)}) collective-permute-start(bf16[2,8,32,512]{3,2,1,0:T(8,128)(2,1)S(1)} %get-tuple-element.34), channel_id=1, source_target_pairs={{0,4},{1,5},{2,6},{3,7},{4,8},{5,9},{6,10},{7,11},{8,12},{9,13},{1... | collective-permute-start | bytes 1572872 | tf_op jit(solution)/shard_map/ppermute | solution.py:27
  50.1 2.4 %collective-permute-start.7 = (bf16[2,8,32,512]{3,2,1,0:T(8,128)(2,1)S(1)}, bf16[2,8,32,512]{3,2,1,0:T(8,128)(2,1)S(1)}, u32[]{:S(2)}, u32[]{:S(2)}) collective-permute-start(bf16[2,8,32,512]{3,2,1,0:T(8,128)(2,1)S(1)} %get-tuple-element.35), channel_id=1, source_target_pairs={{0,8},{1,9},{2,10},{3,11},{4,12},{5,13},{6,14},{7,15},{8,0},{9,1},... | collective-permute-start | bytes 1572872 | tf_op jit(solution)/shard_map/ppermute | solution.py:27
  52.8 21.1 %collective-permute-done.6.refs_7_ = bf16[2,8,32,512]{3,2,1,0:T(8,128)(2,1)S(1)} collective-permute-done((bf16[2,8,32,512]{3,2,1,0:T(8,128)(2,1)S(1)}, bf16[2,8,32,512]{3,2,1,0:T(8,128)(2,1)S(1)}, u32[]{:S(2)}, u32[]{:S(2)}) %collective-permute-start.6) | collective-permute-done | bytes 524320 | tf_op jit(solution)/shard_map/ppermute | solution.py:27
  75.9 5.5 %project.2 = (bf16[2,32,4352]{2,1,0:T(8,128)(2,1)S(1)}, bf16[2,32,4352]{2,1,0:T(8,128)(2,1)S(1)}, bf16[2,32,4352]{2,1,0:T(8,128)(2,1)S(1)}, bf16[2,32,4352]{2,1,0:T(8,128)(2,1)S(1)}) custom-call(bf16[256,2048]{1,0:T(8,128)(2,1)S(1)} %lift.1.values, bf16[1024,7168]{1,0:T(8,128)(2,1)S(1)} %bitcast.3, bf16[1024,7168]{1,0:T(8,128)(2,1)S(1)} %collective-permute-done.9.other_ref), custom_call_target="tpu_custom_call" | custom-call | flops 4563402752 | bytes 2228224 | tf_op jit(solution)/shard_map/project/pallas_call | solution.py:215
  81.4 2.7 %collective-permute-start.10 = (bf16[2,32,4352]{2,1,0:T(8,128)(2,1)S(1)}, bf16[2,32,4352]{2,1,0:T(8,128)(2,1)S(1)}, u32[]{:S(2)}, u32[]{:S(2)}) collective-permute-start(bf16[2,32,4352]{2,1,0:T(8,128)(2,1)S(1)} %get-tuple-element.38), channel_id=1, source_target_pairs={{0,12},{1,13},{2,14},{3,15},{4,0},{5,1},{6,2},{7,3},{8,4},{9,5},{1... | collective-permute-start | bytes 1671176 | tf_op jit(solution)/shard_map/ppermute | solution.py:27
  84.1 1.5 %collective-permute-start.12 = (bf16[2,32,4352]{2,1,0:T(8,128)(2,1)S(1)}, bf16[2,32,4352]{2,1,0:T(8,128)(2,1)S(1)}, u32[]{:S(2)}, u32[]{:S(2)}) collective-permute-start(bf16[2,32,4352]{2,1,0:T(8,128)(2,1)S(1)} %get-tuple-element.40), channel_id=1, source_target_pairs={{0,8},{1,9},{2,10},{3,11},{4,12},{5,13},{6,14},{7,15},{8,0},{9,1},... | collective-permute-start | bytes 1671176 | tf_op jit(solution)/shard_map/ppermute | solution.py:27
  85.7 3.8 %project.3 = (bf16[128,2816]{1,0:T(8,128)(2,1)S(1)}, bf16[64,2816]{1,0:T(8,128)(2,1)S(1)}, bf16[64,2816]{1,0:T(8,128)(2,1)S(1)}) custom-call(bf16[256,2048]{1,0:T(8,128)(2,1)S(1)} %lift.1.values, bf16[1024,7168]{1,0:T(8,128)(2,1)S(1)} %bitcast.3, bf16[1024,7168]{1,0:T(8,128)(2,1)S(1)} %collective-permute-done.9.other_ref), custom_call_target="tpu_custom_call" | custom-call | flops 2952790016 | bytes 1441792 | tf_op jit(solution)/shard_map/project/pallas_call | solution.py:215
  89.5 2.1 %collective-permute-start.15 = (bf16[64,2816]{1,0:T(8,128)(2,1)S(1)}, bf16[64,2816]{1,0:T(8,128)(2,1)S(1)}, u32[]{:S(2)}, u32[]{:S(2)}) collective-permute-start(bf16[64,2816]{1,0:T(8,128)(2,1)S(1)} %get-tuple-element.46), channel_id=1, source_target_pairs={{0,2},{1,3},{2,0},{3,1},{4,6},{5,7},{6,4},{7,5},{8,10},{9,11},{10,... | collective-permute-start | bytes 1081352 | tf_op jit(solution)/shard_map/ppermute | solution.py:27
  91.5 1.5 %collective-permute-start.16 = (bf16[64,2816]{1,0:T(8,128)(2,1)S(1)}, bf16[64,2816]{1,0:T(8,128)(2,1)S(1)}, u32[]{:S(2)}, u32[]{:S(2)}) collective-permute-start(bf16[64,2816]{1,0:T(8,128)(2,1)S(1)} %get-tuple-element.47), channel_id=1, source_target_pairs={{0,2},{1,3},{2,0},{3,1},{4,6},{5,7},{6,4},{7,5},{8,10},{9,11},{10,... | collective-permute-start | bytes 1081352 | tf_op jit(solution)/shard_map/ppermute | solution.py:27
  93.1 9.3 %collective-permute-done.15.b_ref = bf16[64,2816]{1,0:T(8,128)(2,1)S(1)} collective-permute-done((bf16[64,2816]{1,0:T(8,128)(2,1)S(1)}, bf16[64,2816]{1,0:T(8,128)(2,1)S(1)}, u32[]{:S(2)}, u32[]{:S(2)}) %collective-permute-start.15) | collective-permute-done | bytes 360480 | tf_op jit(solution)/shard_map/ppermute | solution.py:27
  102.4 6.1 %collective-permute-done.16.c_ref = bf16[64,2816]{1,0:T(8,128)(2,1)S(1)} collective-permute-done((bf16[64,2816]{1,0:T(8,128)(2,1)S(1)}, bf16[64,2816]{1,0:T(8,128)(2,1)S(1)}, u32[]{:S(2)}, u32[]{:S(2)}) %collective-permute-start.16) | collective-permute-done | bytes 360480 | tf_op jit(solution)/shard_map/ppermute | solution.py:27
  108.7 1.8 %collective-permute-start.17 = (bf16[32,2816]{1,0:T(8,128)(2,1)S(1)}, bf16[32,2816]{1,0:T(8,128)(2,1)S(1)}, u32[]{:S(2)}, u32[]{:S(2)}) collective-permute-start(bf16[32,2816]{1,0:T(8,128)(2,1)S(1)} %get-tuple-element.49), channel_id=1, source_target_pairs={{0,12},{1,13},{2,14},{3,15},{4,0},{5,1},{6,2},{7,3},{8,4},{9,5},{1... | collective-permute-start | bytes 540680 | tf_op jit(solution)/shard_map/ppermute | solution.py:27
  111.1 2.0 %collective-permute-start.19 = (bf16[32,2816]{1,0:T(8,128)(2,1)S(1)}, bf16[32,2816]{1,0:T(8,128)(2,1)S(1)}, u32[]{:S(2)}, u32[]{:S(2)}) collective-permute-start(bf16[32,2816]{1,0:T(8,128)(2,1)S(1)} %get-tuple-element.51), channel_id=1, source_target_pairs={{0,8},{1,9},{2,10},{3,11},{4,12},{5,13},{6,14},{7,15},{8,0},{9,1},... | collective-permute-start | bytes 540680 | tf_op jit(solution)/shard_map/ppermute | solution.py:27
  113.4 1.7 %collective-permute-start.13 = (bf16[32,2176]{1,0:T(8,128)(2,1)S(1)}, bf16[32,2176]{1,0:T(8,128)(2,1)S(1)}, u32[]{:S(2)}, u32[]{:S(2)}) collective-permute-start(bf16[32,2176]{1,0:T(8,128)(2,1)S(1)} %get-tuple-element.42), channel_id=1, source_target_pairs={{0,2},{1,3},{2,0},{3,1},{4,6},{5,7},{6,4},{7,5},{8,10},{9,11},{10,... | collective-permute-start | bytes 417800 | tf_op jit(solution)/shard_map/ppermute | solution.py:27
  115.1 1.9 %collective-permute-start.14 = (bf16[32,2176]{1,0:T(8,128)(2,1)S(1)}, bf16[32,2176]{1,0:T(8,128)(2,1)S(1)}, u32[]{:S(2)}, u32[]{:S(2)}) collective-permute-start(bf16[32,2176]{1,0:T(8,128)(2,1)S(1)} %get-tuple-element.43), channel_id=1, source_target_pairs={{0,2},{1,3},{2,0},{3,1},{4,6},{5,7},{6,4},{7,5},{8,10},{9,11},{10,... | collective-permute-start | bytes 417800 | tf_op jit(solution)/shard_map/ppermute | solution.py:27
  117.0 3.2 %collective-permute-done.18.refs_5_ = bf16[32,2816]{1,0:T(8,128)(2,1)S(1)} collective-permute-done((bf16[32,2816]{1,0:T(8,128)(2,1)S(1)}, bf16[32,2816]{1,0:T(8,128)(2,1)S(1)}, u32[]{:S(2)}, u32[]{:S(2)}) %collective-permute-start.18) | collective-permute-done | bytes 180256 | tf_op jit(solution)/shard_map/ppermute | solution.py:27
  (41 shorter events, 8.0 us)
Async XLA Ops:
  0.6 75.2 %collective-permute-start.9 = (bf16[1024,7168]{1,0:T(8,128)(2,1)}, bf16[1024,7168]{1,0:T(8,128)(2,1)S(1)}, u32[]{:S(2)}, u32[]{:S(2)}) collective-permute-start(bf16[1024,7168]{1,0:T(8,128)(2,1)} %own_ref.3), channel_id=1, source_target_pairs={{0,1},{1,0},{2,3},{3,2},{4,5},{5,4},{6,7},{7,6},{8,9},{9,8},{10,11... | collective-permute-start | bytes 44040200 | tf_op jit(solution)/shard_map/ppermute | solution.py:27
  0.7 23.9 %collective-permute-start.1 = (bf16[8,512,128]{2,1,0:T(8,128)(2,1)}, bf16[8,512,128]{2,1,0:T(8,128)(2,1)S(1)}, u32[]{:S(2)}, u32[]{:S(2)}) collective-permute-start(bf16[8,512,128]{2,1,0:T(8,128)(2,1)} %refs_10_.1), channel_id=1, source_target_pairs={{0,1},{1,0},{2,3},{3,2},{4,5},{5,4},{6,7},{7,6},{8,9},{9,8},{10,11... | collective-permute-start | bytes 3145736 | tf_op jit(solution)/shard_map/ppermute | solution.py:27
  1.2 74.6 %slice-start = ((s8[14680064]{0:T(1024)(128)(4,1)}), s8[4194304]{0:T(1024)(128)(4,1)S(1)}, s32[]{:S(2)}) async-start(s8[14680064]{0:T(1024)(128)(4,1)} %bitcast.2), calls=%async_computation | async-start | bytes 8388608
  1.2 74.6 %slice-start.1 = ((s8[14680064]{0:T(1024)(128)(4,1)}), s8[4194304]{0:T(1024)(128)(4,1)S(1)}, s32[]{:S(2)}) async-start(s8[14680064]{0:T(1024)(128)(4,1)} %bitcast.2), calls=%async_computation.1 | async-start | bytes 8388608
  1.2 74.7 %slice-start.2 = ((s8[14680064]{0:T(1024)(128)(4,1)}), s8[4194304]{0:T(1024)(128)(4,1)S(1)}, s32[]{:S(2)}) async-start(s8[14680064]{0:T(1024)(128)(4,1)} %bitcast.2), calls=%async_computation.2 | async-start | bytes 8388608
  1.2 74.7 %slice-start.3 = ((s8[14680064]{0:T(1024)(128)(4,1)}), s8[2097152]{0:T(1024)(128)(4,1)S(1)}, s32[]{:S(2)}) async-start(s8[14680064]{0:T(1024)(128)(4,1)} %bitcast.2), calls=%async_computation.3 | async-start | bytes 4194304
  17.9 15.3 %collective-permute-start = (bf16[2,8,32,512]{3,2,1,0:T(8,128)(2,1)S(1)}, bf16[2,8,32,512]{3,2,1,0:T(8,128)(2,1)S(1)}, u32[]{:S(2)}, u32[]{:S(2)}) collective-permute-start(bf16[2,8,32,512]{3,2,1,0:T(8,128)(2,1)S(1)} %get-tuple-element.28), channel_id=1, source_target_pairs={{0,4},{1,5},{2,6},{3,7},{4,8},{5,9},{6,10},{7,11},{8,12},{9,13},{1... | collective-permute-start | bytes 1572872 | tf_op jit(solution)/shard_map/ppermute | solution.py:27
  19.6 28.5 %collective-permute-start.5 = (bf16[4,8,32,512]{3,2,1,0:T(8,128)(2,1)S(1)}, bf16[4,8,32,512]{3,2,1,0:T(8,128)(2,1)S(1)}, u32[]{:S(2)}, u32[]{:S(2)}) collective-permute-start(bf16[4,8,32,512]{3,2,1,0:T(8,128)(2,1)S(1)} %get-tuple-element.33), channel_id=1, source_target_pairs={{0,2},{1,3},{2,0},{3,1},{4,6},{5,7},{6,4},{7,5},{8,10},{9,11},{10,... | collective-permute-start | bytes 3145736 | tf_op jit(solution)/shard_map/ppermute | solution.py:27
  21.6 24.3 %collective-permute-start.3 = (bf16[2,8,32,512]{3,2,1,0:T(8,128)(2,1)S(1)}, bf16[2,8,32,512]{3,2,1,0:T(8,128)(2,1)S(1)}, u32[]{:S(2)}, u32[]{:S(2)}) collective-permute-start(bf16[2,8,32,512]{3,2,1,0:T(8,128)(2,1)S(1)} %get-tuple-element.31), channel_id=1, source_target_pairs={{0,12},{1,13},{2,14},{3,15},{4,0},{5,1},{6,2},{7,3},{8,4},{9,5},{1... | collective-permute-start | bytes 1572872 | tf_op jit(solution)/shard_map/ppermute | solution.py:27
  24.6 21.3 %collective-permute-start.2 = (bf16[2,8,32,512]{3,2,1,0:T(8,128)(2,1)S(1)}, bf16[2,8,32,512]{3,2,1,0:T(8,128)(2,1)S(1)}, u32[]{:S(2)}, u32[]{:S(2)}) collective-permute-start(bf16[2,8,32,512]{3,2,1,0:T(8,128)(2,1)S(1)} %get-tuple-element.30), channel_id=1, source_target_pairs={{0,8},{1,9},{2,10},{3,11},{4,12},{5,13},{6,14},{7,15},{8,0},{9,1},... | collective-permute-start | bytes 1572872 | tf_op jit(solution)/shard_map/ppermute | solution.py:27
  45.9 28.6 %collective-permute-start.4 = (bf16[4,8,32,512]{3,2,1,0:T(8,128)(2,1)S(1)}, bf16[4,8,32,512]{3,2,1,0:T(8,128)(2,1)S(1)}, u32[]{:S(2)}, u32[]{:S(2)}) collective-permute-start(bf16[4,8,32,512]{3,2,1,0:T(8,128)(2,1)S(1)} %regroup.2), channel_id=1, source_target_pairs={{0,2},{1,3},{2,0},{3,1},{4,6},{5,7},{6,4},{7,5},{8,10},{9,11},{10,... | collective-permute-start | bytes 3145736 | tf_op jit(solution)/shard_map/ppermute | solution.py:27
  48.2 25.8 %collective-permute-start.6 = (bf16[2,8,32,512]{3,2,1,0:T(8,128)(2,1)S(1)}, bf16[2,8,32,512]{3,2,1,0:T(8,128)(2,1)S(1)}, u32[]{:S(2)}, u32[]{:S(2)}) collective-permute-start(bf16[2,8,32,512]{3,2,1,0:T(8,128)(2,1)S(1)} %get-tuple-element.34), channel_id=1, source_target_pairs={{0,4},{1,5},{2,6},{3,7},{4,8},{5,9},{6,10},{7,11},{8,12},{9,13},{1... | collective-permute-start | bytes 1572872 | tf_op jit(solution)/shard_map/ppermute | solution.py:27
  50.1 23.9 %collective-permute-start.7 = (bf16[2,8,32,512]{3,2,1,0:T(8,128)(2,1)S(1)}, bf16[2,8,32,512]{3,2,1,0:T(8,128)(2,1)S(1)}, u32[]{:S(2)}, u32[]{:S(2)}) collective-permute-start(bf16[2,8,32,512]{3,2,1,0:T(8,128)(2,1)S(1)} %get-tuple-element.35), channel_id=1, source_target_pairs={{0,8},{1,9},{2,10},{3,11},{4,12},{5,13},{6,14},{7,15},{8,0},{9,1},... | collective-permute-start | bytes 1572872 | tf_op jit(solution)/shard_map/ppermute | solution.py:27
  52.5 22.1 %collective-permute-start.8 = (bf16[2,8,32,512]{3,2,1,0:T(8,128)(2,1)S(1)}, bf16[2,8,32,512]{3,2,1,0:T(8,128)(2,1)S(1)}, u32[]{:S(2)}, u32[]{:S(2)}) collective-permute-start(bf16[2,8,32,512]{3,2,1,0:T(8,128)(2,1)S(1)} %get-tuple-element.36), channel_id=1, source_target_pairs={{0,12},{1,13},{2,14},{3,15},{4,0},{5,1},{6,2},{7,3},{8,4},{9,5},{1... | collective-permute-start | bytes 1572872 | tf_op jit(solution)/shard_map/ppermute | solution.py:27
  81.4 29.7 %collective-permute-start.10 = (bf16[2,32,4352]{2,1,0:T(8,128)(2,1)S(1)}, bf16[2,32,4352]{2,1,0:T(8,128)(2,1)S(1)}, u32[]{:S(2)}, u32[]{:S(2)}) collective-permute-start(bf16[2,32,4352]{2,1,0:T(8,128)(2,1)S(1)} %get-tuple-element.38), channel_id=1, source_target_pairs={{0,12},{1,13},{2,14},{3,15},{4,0},{5,1},{6,2},{7,3},{8,4},{9,5},{1... | collective-permute-start | bytes 1671176 | tf_op jit(solution)/shard_map/ppermute | solution.py:27
  84.1 29.0 %collective-permute-start.11 = (bf16[2,32,4352]{2,1,0:T(8,128)(2,1)S(1)}, bf16[2,32,4352]{2,1,0:T(8,128)(2,1)S(1)}, u32[]{:S(2)}, u32[]{:S(2)}) collective-permute-start(bf16[2,32,4352]{2,1,0:T(8,128)(2,1)S(1)} %get-tuple-element.39), channel_id=1, source_target_pairs={{0,4},{1,5},{2,6},{3,7},{4,8},{5,9},{6,10},{7,11},{8,12},{9,13},{1... | collective-permute-start | bytes 1671176 | tf_op jit(solution)/shard_map/ppermute | solution.py:27
  84.1 29.0 %collective-permute-start.12 = (bf16[2,32,4352]{2,1,0:T(8,128)(2,1)S(1)}, bf16[2,32,4352]{2,1,0:T(8,128)(2,1)S(1)}, u32[]{:S(2)}, u32[]{:S(2)}) collective-permute-start(bf16[2,32,4352]{2,1,0:T(8,128)(2,1)S(1)} %get-tuple-element.40), channel_id=1, source_target_pairs={{0,8},{1,9},{2,10},{3,11},{4,12},{5,13},{6,14},{7,15},{8,0},{9,1},... | collective-permute-start | bytes 1671176 | tf_op jit(solution)/shard_map/ppermute | solution.py:27
  89.5 12.9 %collective-permute-start.15 = (bf16[64,2816]{1,0:T(8,128)(2,1)S(1)}, bf16[64,2816]{1,0:T(8,128)(2,1)S(1)}, u32[]{:S(2)}, u32[]{:S(2)}) collective-permute-start(bf16[64,2816]{1,0:T(8,128)(2,1)S(1)} %get-tuple-element.46), channel_id=1, source_target_pairs={{0,2},{1,3},{2,0},{3,1},{4,6},{5,7},{6,4},{7,5},{8,10},{9,11},{10,... | collective-permute-start | bytes 1081352 | tf_op jit(solution)/shard_map/ppermute | solution.py:27
  91.5 17.0 %collective-permute-start.16 = (bf16[64,2816]{1,0:T(8,128)(2,1)S(1)}, bf16[64,2816]{1,0:T(8,128)(2,1)S(1)}, u32[]{:S(2)}, u32[]{:S(2)}) collective-permute-start(bf16[64,2816]{1,0:T(8,128)(2,1)S(1)} %get-tuple-element.47), channel_id=1, source_target_pairs={{0,2},{1,3},{2,0},{3,1},{4,6},{5,7},{6,4},{7,5},{8,10},{9,11},{10,... | collective-permute-start | bytes 1081352 | tf_op jit(solution)/shard_map/ppermute | solution.py:27
  108.7 8.3 %collective-permute-start.17 = (bf16[32,2816]{1,0:T(8,128)(2,1)S(1)}, bf16[32,2816]{1,0:T(8,128)(2,1)S(1)}, u32[]{:S(2)}, u32[]{:S(2)}) collective-permute-start(bf16[32,2816]{1,0:T(8,128)(2,1)S(1)} %get-tuple-element.49), channel_id=1, source_target_pairs={{0,12},{1,13},{2,14},{3,15},{4,0},{5,1},{6,2},{7,3},{8,4},{9,5},{1... | collective-permute-start | bytes 540680 | tf_op jit(solution)/shard_map/ppermute | solution.py:27
  110.5 9.8 %collective-permute-start.18 = (bf16[32,2816]{1,0:T(8,128)(2,1)S(1)}, bf16[32,2816]{1,0:T(8,128)(2,1)S(1)}, u32[]{:S(2)}, u32[]{:S(2)}) collective-permute-start(bf16[32,2816]{1,0:T(8,128)(2,1)S(1)} %get-tuple-element.50), channel_id=1, source_target_pairs={{0,4},{1,5},{2,6},{3,7},{4,8},{5,9},{6,10},{7,11},{8,12},{9,13},{1... | collective-permute-start | bytes 540680 | tf_op jit(solution)/shard_map/ppermute | solution.py:27
  111.1 9.1 %collective-permute-start.19 = (bf16[32,2816]{1,0:T(8,128)(2,1)S(1)}, bf16[32,2816]{1,0:T(8,128)(2,1)S(1)}, u32[]{:S(2)}, u32[]{:S(2)}) collective-permute-start(bf16[32,2816]{1,0:T(8,128)(2,1)S(1)} %get-tuple-element.51), channel_id=1, source_target_pairs={{0,8},{1,9},{2,10},{3,11},{4,12},{5,13},{6,14},{7,15},{8,0},{9,1},... | collective-permute-start | bytes 540680 | tf_op jit(solution)/shard_map/ppermute | solution.py:27
  113.4 6.9 %collective-permute-start.13 = (bf16[32,2176]{1,0:T(8,128)(2,1)S(1)}, bf16[32,2176]{1,0:T(8,128)(2,1)S(1)}, u32[]{:S(2)}, u32[]{:S(2)}) collective-permute-start(bf16[32,2176]{1,0:T(8,128)(2,1)S(1)} %get-tuple-element.42), channel_id=1, source_target_pairs={{0,2},{1,3},{2,0},{3,1},{4,6},{5,7},{6,4},{7,5},{8,10},{9,11},{10,... | collective-permute-start | bytes 417800 | tf_op jit(solution)/shard_map/ppermute | solution.py:27
  115.1 6.6 %collective-permute-start.14 = (bf16[32,2176]{1,0:T(8,128)(2,1)S(1)}, bf16[32,2176]{1,0:T(8,128)(2,1)S(1)}, u32[]{:S(2)}, u32[]{:S(2)}) collective-permute-start(bf16[32,2176]{1,0:T(8,128)(2,1)S(1)} %get-tuple-element.43), channel_id=1, source_target_pairs={{0,2},{1,3},{2,0},{3,1},{4,6},{5,7},{6,4},{7,5},{8,10},{9,11},{10,... | collective-permute-start | bytes 417800 | tf_op jit(solution)/shard_map/ppermute | solution.py:27
  (3 other events, 140.7 us)
